TPU v7x, 32 devices: a whole 2x2x4 slice. The times are simulated.
32 devices in a mesh: groups: 2 (over x), heads: 16 (over z, y, core).
Axes of the slice: x: 2, y: 2, z: 4, core: 2. Of those that a mesh axis runs over, the one named last changes fastest.
Arguments:
- tokens: bfloat16 [64, 4, 2304], P('groups'), parts along dimension 0, may hold values from -6 to 6
- qkv_weight: bfloat16 [4608, 12288], P(('groups', 'heads')), parts along dimension 0, may hold values from -0.125 to 0.125
- gate_weight: bfloat16 [4608, 64], P(('groups', 'heads')), parts along dimension 0, may hold values from -0.125 to 0.125
- conv_weight: bfloat16 [8, 12288], P('groups', 'heads'), parts along dimension 0, may hold values from -3 to 3
- delta_state: float32 [64, 32, 128, 128], P(('groups', 'heads')), parts along dimension 0, may hold values from -0.8 to 0.8
- conv_state: float32 [64, 3, 12288], P(('groups', 'heads')), parts along dimension 0, may hold values from -6 to 6
- old_heads: int32 [32], replicated, may hold values from 0 to 31, each once
- new_units: int32 [64], replicated, may hold values from 0 to 63, each once
- slot_of: int32 [64], P('groups'), parts along dimension 0, may hold values from 0 to 31, each once
- lengths: int32 [64], P('groups'), parts along dimension 0, may hold values from 1 to 4, as said below
Outputs:
- readout: bfloat16 [64, 4, 4096], P('groups', None, 'heads'), parts along dimension 0
There are 2 independent parts, one for each index of `groups`. A program takes and returns all parts, laid end to end along the dimension named above; an argument that names none is the same for every part. Nothing has to cross between parts.
Inputs may be any that keep to these rules, and one draw needn't show every extreme that they name: `old_heads`: a permutation of the heads; old column slot p holds head old_heads[p]. `new_units`: a permutation of the head units; unit u is the half u % 2 of the values of head u // 2. `slot_of`: a permutation of the rows. `lengths`: some row decodes all 4 steps and some row only one.
All inputs are finite; a program needn't handle non-finite values.
Results may differ from a plain program's by a relative error of at most 0.001.
Values may be sent and summed in bfloat16 or wider, within the bound.
No kernel may reach another device: no remote copies, remote signals or barrier semaphores. Data moves between devices by JAX's collectives and lax.ppermute only.
A program may use at most 128 MiB of HBM per device.

v0:
```python
import jax
import jax.numpy as jnp
from jax import lax
from jax.sharding import PartitionSpec as P

D = 2304
H = 32
DK = 128
TAPS = 4
STEPS = 4
HALF = 64
UNITS = 64


norm_eps = 1e-06


def unit_tables(old_heads, new_units):
    positions = jnp.arange(H, dtype=jnp.int32)
    inverse = jnp.sum(
        jnp.where(old_heads[None, :] == positions[:, None], positions[None, :], 0), axis=1
    )
    heads_of = new_units // 2
    halves = new_units % 2
    old_slots = jnp.sum(
        jnp.where(heads_of[:, None] == positions[None, :], inverse[None, :], 0), axis=1
    )
    return (old_slots, halves)


def select_units(source, selector, halves, precise):
    lead = source.shape[:-1]
    shaped = source.reshape(lead + (3, H, DK))
    if precise:
        picked = jnp.einsum("...mhk,uh->...muk", shaped, selector, precision=lax.Precision.HIGHEST)
    else:
        picked = jnp.einsum(
            "...mhk,uh->...muk", shaped, selector, preferred_element_type=jnp.float32
        ).astype(source.dtype)
    query_part = picked[..., 0, :, :]
    key_part = picked[..., 1, :, :]
    value_full = picked[..., 2, :, :]
    value_part = jnp.where((halves == 0)[:, None], value_full[..., :HALF], value_full[..., HALF:])
    return jnp.concatenate([query_part, key_part, value_part], axis=-1)


def pick_state(delta_state, selector, halves):
    picked = jnp.einsum("rhkv,uh->rukv", delta_state, selector, precision=lax.Precision.HIGHEST)
    return jnp.where((halves == 0)[None, :, None, None], picked[..., :HALF], picked[..., HALF:])


def normalize(values):
    return values * lax.rsqrt(jnp.sum(values * values, axis=-1, keepdims=True) + norm_eps)


def run_steps(projected, gate_pre, history, tap_weights, carried, live_lengths):
    sequence = jnp.concatenate([history, projected], axis=1)
    weights_f = tap_weights.astype(jnp.float32)
    convolved = weights_f[0][None, None] * sequence[:, 0:STEPS]
    for tap_index in range(1, TAPS):
        convolved = (
            convolved
            + weights_f[tap_index][None, None] * sequence[:, tap_index : tap_index + STEPS]
        )
    activated = jax.nn.silu(convolved)
    queries = normalize(activated[..., :DK])
    keys_all = normalize(activated[..., DK : 2 * DK])
    values_all = activated[..., 2 * DK :]
    beta = jax.nn.sigmoid(gate_pre[..., 0])
    decay = jnp.exp(-jax.nn.softplus(gate_pre[..., 1]))
    readouts = []
    for step_index in range(STEPS):
        is_live = (step_index < live_lengths)[:, None, None, None]
        faded = decay[:, step_index, :, None, None] * carried
        predicted = jnp.sum(keys_all[:, step_index, :, :, None] * faded, axis=2)
        updated = (
            faded
            + beta[:, step_index, :, None, None]
            * keys_all[:, step_index, :, :, None]
            * (values_all[:, step_index] - predicted)[:, :, None, :]
        )
        heads_now = jnp.sum(queries[:, step_index, :, :, None] * updated, axis=2)
        carried = jnp.where(is_live, updated, carried)
        readouts.append(jnp.where(is_live[..., 0], heads_now, jnp.zeros_like(heads_now)))
    return jnp.stack(readouts, axis=1).astype(jnp.bfloat16)


def on_device(
    tokens,
    qkv_weight,
    gate_weight,
    conv_weight,
    delta_state,
    conv_state,
    old_heads,
    new_units,
    slot_of,
    lengths,
):
    devices = lax.axis_size("heads")
    my_index = lax.axis_index("heads")
    per_device = UNITS // devices
    unit_width = 2 * DK + HALF
    old_slots, halves = unit_tables(old_heads, new_units)
    head_range = jnp.arange(H, dtype=jnp.int32)
    selector_bits = old_slots[:, None] == head_range[None, :]
    selector_low = selector_bits.astype(jnp.bfloat16)
    selector_full = selector_bits.astype(jnp.float32)
    local_rows = qkv_weight.shape[0]
    packed = select_units(qkv_weight, selector_low, halves, False).reshape(
        local_rows, devices, per_device, unit_width
    )
    gate_shaped = gate_weight.reshape(local_rows, 2, H)
    packed_gate = jnp.einsum(
        "rmh,uh->rum", gate_shaped, selector_low, preferred_element_type=jnp.float32
    ).astype(jnp.bfloat16)
    packed_gate = packed_gate.reshape(local_rows, devices, per_device, 2)
    mine_weight, mine_gate = (
        lax.all_to_all(packed, "heads", split_axis=1, concat_axis=0, tiled=True),
        lax.all_to_all(packed_gate, "heads", split_axis=1, concat_axis=0, tiled=True),
    )
    row_count = tokens.shape[0]
    row_range = jnp.arange(row_count, dtype=jnp.int32)
    match_rows = slot_of[None, :] == row_range[:, None]
    to_old = match_rows.astype(jnp.bfloat16)
    tokens_old = jnp.einsum(
        "ob,bsd->osd", to_old, tokens, preferred_element_type=jnp.float32
    ).astype(jnp.bfloat16)
    lengths_old = jnp.sum(jnp.where(match_rows, lengths[None, :], 0), axis=1)
    flattened = tokens_old.reshape(row_count * STEPS, D)
    projected = jnp.dot(
        flattened,
        mine_weight.reshape(D, per_device * unit_width),
        preferred_element_type=jnp.float32,
    ).reshape(row_count, STEPS, per_device, unit_width)
    gate_pre = jnp.dot(
        flattened, mine_gate.reshape(D, per_device * 2), preferred_element_type=jnp.float32
    ).reshape(row_count, STEPS, per_device, 2)
    taps_all = lax.all_gather(conv_weight, "heads", axis=1, tiled=True)
    tap_table = select_units(taps_all, selector_low, halves, False)
    rows_dev = delta_state.shape[0]
    got_projected, got_gate = (
        lax.all_to_all(projected, "heads", split_axis=0, concat_axis=2, tiled=True),
        lax.all_to_all(gate_pre, "heads", split_axis=0, concat_axis=2, tiled=True),
    )
    live_lengths = lax.dynamic_slice_in_dim(lengths_old, my_index * rows_dev, rows_dev, 0)
    history = select_units(conv_state, selector_full, halves, True)
    carried = pick_state(delta_state, selector_full, halves)
    local_out = run_steps(got_projected, got_gate, history, tap_table, carried, live_lengths)
    outputs_old = lax.all_to_all(local_out, "heads", split_axis=2, concat_axis=0, tiled=True)
    flat_old = outputs_old.reshape(row_count, STEPS, per_device * HALF)
    outputs = jnp.einsum(
        "ob,osc->bsc", to_old, flat_old, preferred_element_type=jnp.float32
    ).astype(jnp.bfloat16)
    return outputs


def solution(mesh):
    in_specs = (
        P("groups", None, None),
        P(("groups", "heads"), None),
        P(("groups", "heads"), None),
        P("groups", "heads"),
        P(("groups", "heads"), None, None, None),
        P(("groups", "heads"), None, None),
        P(),
        P(),
        P("groups"),
        P("groups"),
    )
    out_specs = P("groups", None, "heads")
    return jax.shard_map(
        on_device, mesh=mesh, in_specs=in_specs, out_specs=out_specs, check_vma=False
    )
```

profile of v0, /device:TPU:0, one launch (start us, length us, event | category | flops | bytes accessed | tf_op | source)
XLA Modules:
  0.0 337.1 jit_solution(10728899009877708103)
XLA Ops:
  0.0 0.7 and_select_fusion.1
  0.7 0.7 select_reduce_fusion.1
  1.6 1.0 fusion.9
  2.5 0.7 copy.168
  3.2 7.4 %all-to-all-start.2 = ((bf16[144,16,4,2]{0,3,2,1:T(2,128)(2,1)}), bf16[144,16,4,2]{0,3,2,1:T(2,128)(2,1)S(1)}, u32[]{:S(2)}, u32[]{:S(2)}) async-start(bf16[144,16,4,2]{0,3,2,1:T(2,128)(2,1)} %bitcast.40), calls=%async_computation.2 | async-start | bytes 131072 | tf_op jit(solution)/shard_map/all_to_all | solution.py:120
  10.6 0.7 fusion.50
  11.3 2.7 copy.172
  14.0 2.0 convert_bitcast_fusion
  16.1 2.5 fusion.52
  18.6 0.8 slice_select_fusion.1
  19.3 6.9 %pad_maximum_fusion = bf16[144,16,4,320]{3,2,1,0:T(4,128)(2,1)} fusion(bf16[144,16,4,64]{3,2,1,0:T(4,128)(2,1)S(1)} %bitcast.162, bf16[144,16,4,128]{3,2,1,0:T(4,128)(2,1)S(1)} %bitcast.161, bf16[144,16,4,128]{3,2,1,0:T(4,128)(2,1)S(1)} %bitcast.160), kind=kLoop, calls=%fused_computation.15 | loop fusion | flops 17694720 | bytes 11796480 | tf_op jit(solution)/shard_map/concatenate | solution.py:44
  26.2 9.1 %copy.167 = bf16[144,16,4,320]{3,2,0,1:T(4,128)(2,1)} copy(bf16[144,16,4,320]{3,2,1,0:T(4,128)(2,1)} %pad_maximum_fusion) | data formatting | bytes 11796480 | tf_op jit(solution)/shard_map/concatenate | solution.py:44
  35.4 6.2 %all-to-all-start = ((bf16[144,16,4,320]{3,2,0,1:T(4,128)(2,1)}), bf16[144,16,4,320]{3,2,0,1:T(4,128)(2,1)}, u32[]{:S(2)}, u32[]{:S(2)}) async-start(bf16[144,16,4,320]{3,2,0,1:T(4,128)(2,1)} %copy.167), calls=%async_computation | async-start | bytes 14155776 | tf_op jit(solution)/shard_map/all_to_all | solution.py:119
  41.6 141.5 %all_gather.3 = bf16[4,12288]{1,0:T(4,128)(2,1)S(1)} all-gather(bf16[4,768]{1,0:T(4,128)(2,1)S(1)} %copy-done.3), channel_id=1, replica_groups=mesh['groups'=2,'heads'=16] {'heads'}, dimensions={1}, use_global_device_ids=true | all-gather | bytes 104448 | tf_op jit(solution)/shard_map/all_gather | solution.py:139
  185.5 11.6 %fusion.5 = f32[2,64,128,128]{3,1,2,0:T(8,128)} fusion(f32[2,32,128,128]{3,2,1,0:T(8,128)} %param.14, s32[64]{0:T(128)S(1)} %select_reduce_fusion), kind=kOutput, calls=%fused_computation.21 | convolution fusion | flops 805308416 | bytes 12583168 | tf_op jit(solution)/shard_map/rhkv,uh->rukv/dot_general | solution.py:48
  197.3 0.5 fusion.24
  197.8 0.8 copy.143
  198.6 27.4 %all-to-all-start.3 = ((f32[32,4,4,2]{2,3,1,0:T(2,128)}), f32[32,4,4,2]{2,3,1,0:T(2,128)S(1)}, u32[]{:S(2)}, u32[]{:S(2)}) async-start(f32[32,4,4,2]{2,3,1,0:T(2,128)} %copy.143), calls=%async_computation.3 | async-start | bytes 262144 | tf_op jit(solution)/shard_map/all_to_all | solution.py:144
  226.0 11.9 %reshape.189 = bf16[2304,1280]{1,0:T(8,128)(2,1)} reshape(bf16[16,144,1,4,320]{4,3,1,0,2:T(4,128)(2,1)} %bitcast.24) | data formatting | bytes 11796480 | tf_op jit(solution)/shard_map/reshape | solution.py:133
  237.8 8.9 %copy.135 = bf16[1280,2304]{1,0:T(8,128)(2,1)} copy(bf16[1280,2304]{0,1:T(8,128)(2,1)} %bitcast.158) | data formatting | bytes 11796480 | tf_op jit(solution)/shard_map/dot_general | solution.py:131
  246.7 4.7 %fusion.58 = f32[32,4,4,320]{3,0,2,1:T(8,128)S(1)} fusion(bf16[32,4,2304,1]{2,0,3,1:T(8,128)(2,1)S(1)} %fusion.4, bf16[4,320,2304,1]{2,1,0,3:T(8,128)(2,1)} %bitcast.163), kind=kOutput, calls=%fused_computation.124 | convolution fusion | flops 754974720 | bytes 7143424 | tf_op jit(solution)/shard_map/dot_general | solution.py:131
  251.5 1.4 copy.136
  252.9 6.0 %all-to-all-start.1 = ((f32[32,4,4,320]{3,2,1,0:T(4,128)}), f32[32,4,4,320]{3,2,1,0:T(4,128)S(1)}, u32[]{:S(2)}, u32[]{:S(2)}) async-start(f32[32,4,4,320]{3,2,1,0:T(4,128)} %copy.136), calls=%async_computation.1 | async-start | bytes 1572864 | tf_op jit(solution)/shard_map/all_to_all | solution.py:143
  259.3 18.4 %all-to-all-done.1 = f32[32,4,4,320]{3,2,1,0:T(4,128)S(1)} async-done(((f32[32,4,4,320]{3,2,1,0:T(4,128)}), f32[32,4,4,320]{3,2,1,0:T(4,128)S(1)}, u32[]{:S(2)}, u32[]{:S(2)}) %all-to-all-start.1) | async-done | bytes 655392 | tf_op jit(solution)/shard_map/all_to_all | solution.py:143
  277.8 1.5 divide_multiply_fusion
  282.2 8.5 %multiply_reduce_fusion.7 = (f32[2,64,64]{2,1,0:T(8,128)S(1)}, f32[2,64,128,64]{3,1,2,0:T(8,128)S(1)}) fusion(f32[2,64,128]{1,2,0:T(8,128)S(1)} %copy.148, f32[2,64]{1,0:T(2,128)S(1)} %bitcast.195, f32[2,64,128,128]{3,1,2,0:T(8,128)} %fusion.5, pred[64]{0:T(512)(128)(4,1)S(1)} %fusion.50), kind=kLoop, calls=%fused_computation.12 | loop fusion | flops 4186112 | bytes 12681792 | tf_op jit(solution)/shard_map/reduce_sum | solution.py:75
  290.7 5.1 %multiply_reduce_fusion.5 = f32[2,64,64]{2,1,0:T(8,128)S(1)} fusion(f32[2,64,128,64]{3,1,2,0:T(8,128)S(1)} %get-tuple-element.16, f32[2,64,128]{1,2,0:T(8,128)S(1)} %copy.151, f32[2,64]{1,0:T(2,128)S(1)} %bitcast.202, f32[2,64,64]{2,1,0:T(8,128)S(1)} %sub.35, f32[2,64,128]{1,2,0:T(8,128)S(1)} %copy.147, f32[2,64]{1,0:T(2,128)S(1)} %bitcast.196, ...), kind=kLoop, calls=%fused_computation.9 | loop fusion | flops 7331840 | bytes 4391938 | tf_op jit(solution)/shard_map/reduce_sum | solution.py:75
  295.9 11.4 %multiply_reduce_fusion.6 = (bf16[2,64,64]{2,1,0:T(8,128)(2,1)S(1)}, bf16[2,64,64]{2,1,0:T(8,128)(2,1)S(1)}, f32[2,64,64]{2,1,0:T(8,128)S(1)}, f32[2,64,128,64]{3,1,2,0:T(8,128)S(1)}) fusion(f32[2,64,128,64]{3,1,2,0:T(8,128)S(1)} %get-tuple-element.16, f32[2,64,64]{2,1,0:T(8,128)S(1)} %sub.35, f32[2,64,128]{1,2,0:T(8,128)S(1)} %copy.147, ...), kind=kLoop, calls=%fused_computation.10 | loop fusion | flops 15704064 | bytes 8848900 | tf_op jit(solution)/shard_map/reduce_sum | solution.py:82
  307.3 5.1 %multiply_reduce_fusion.1 = f32[2,64,64]{2,1,0:T(8,128)S(1)} fusion(f32[2,64,128,64]{3,1,2,0:T(8,128)S(1)} %get-tuple-element.18, f32[2,64,128]{1,2,0:T(8,128)S(1)} %copy.157, f32[2,64]{1,0:T(2,128)S(1)} %bitcast.200, f32[2,64,64]{2,1,0:T(8,128)S(1)} %sub.37, f32[2,64,128]{1,2,0:T(8,128)S(1)} %copy.153, f32[2,64]{1,0:T(2,128)S(1)} %bitcast.193, ...), kind=kLoop, calls=%fused_computation.2 | loop fusion | flops 7331840 | bytes 4391938 | tf_op jit(solution)/shard_map/reduce_sum | solution.py:75
  312.5 10.5 %multiply_reduce_fusion.2 = (bf16[2,64,64]{2,1,0:T(8,128)(2,1)S(1)}, bf16[2,64,64]{2,1,0:T(8,128)(2,1)S(1)}) fusion(f32[2,64,128,64]{3,1,2,0:T(8,128)S(1)} %get-tuple-element.18, f32[2,64,64]{2,1,0:T(8,128)S(1)} %sub.37, f32[2,64,128]{1,2,0:T(8,128)S(1)} %copy.153, f32[2,64]{1,0:T(2,128)S(1)} %bitcast.194, f32[2,64,128]{1,2,0:T(8,128)S(1)} %copy.152, ...), kind=kLoop, calls=%fused_computation.4 | loop fusion | flops 11517952 | bytes 4555778 | tf_op jit(solution)/shard_map/reduce_sum | solution.py:82
  323.6 12.2 %all_to_all.81 = bf16[16,2,1024]{2,1,0:T(2,128)(2,1)S(1)} all-to-all(bf16[16,2,1024]{2,1,0:T(2,128)(2,1)S(1)} %reshape.202), channel_id=1, replica_groups=mesh['groups'=2,'heads'=16] {'heads'}, dimensions={0} | all-to-all | bytes 131072 | tf_op jit(solution)/shard_map/all_to_all | solution.py:150
  336.4 0.7 copy.161
  (81 shorter events, 7.0 us)
Async XLA Ops:
  0.0 184.7 %copy-start = (bf16[32,4,2304]{2,1,0:T(4,128)(2,1)S(1)}, bf16[32,4,2304]{2,1,0:T(4,128)(2,1)}, u32[]{:S(2)}) copy-start(bf16[32,4,2304]{2,1,0:T(4,128)(2,1)} %param.10) | copy-start | bytes 1769476
  3.2 32.2 %all-to-all-start.2 = ((bf16[144,16,4,2]{0,3,2,1:T(2,128)(2,1)}), bf16[144,16,4,2]{0,3,2,1:T(2,128)(2,1)S(1)}, u32[]{:S(2)}, u32[]{:S(2)}) async-start(bf16[144,16,4,2]{0,3,2,1:T(2,128)(2,1)} %bitcast.40), calls=%async_computation.2 | async-start | bytes 131072 | tf_op jit(solution)/shard_map/all_to_all | solution.py:120
  35.4 6.2 %copy-start.3 = (bf16[4,768]{1,0:T(4,128)(2,1)S(1)}, bf16[4,768]{1,0:T(4,128)(2,1)}, u32[]{:S(2)}) copy-start(bf16[4,768]{1,0:T(4,128)(2,1)} %param.13) | copy-start | bytes 18436
  35.4 147.7 %copy-start.2 = (f32[2,3,12288]{2,0,1:T(2,128)S(1)}, f32[2,3,12288]{2,0,1:T(2,128)}, u32[]{:S(2)}) copy-start(f32[2,3,12288]{2,0,1:T(2,128)} %param.15) | copy-start | bytes 884740
  35.4 149.1 %copy-start.4 = (s32[32]{0:T(128)S(1)}, s32[32]{0:T(128)}, u32[]{:S(2)}) copy-start(s32[32]{0:T(128)} %param.18) | copy-start | bytes 388
  35.4 149.1 %copy-start.5 = (s32[32]{0:T(128)S(1)}, s32[32]{0:T(128)}, u32[]{:S(2)}) copy-start(s32[32]{0:T(128)} %param.19) | copy-start | bytes 388
  35.4 163.2 %all-to-all-start = ((bf16[144,16,4,320]{3,2,0,1:T(4,128)(2,1)}), bf16[144,16,4,320]{3,2,0,1:T(4,128)(2,1)}, u32[]{:S(2)}, u32[]{:S(2)}) async-start(bf16[144,16,4,320]{3,2,0,1:T(4,128)(2,1)} %copy.167), calls=%async_computation | async-start | bytes 14155776 | tf_op jit(solution)/shard_map/all_to_all | solution.py:119
  198.6 54.3 %all-to-all-start.3 = ((f32[32,4,4,2]{2,3,1,0:T(2,128)}), f32[32,4,4,2]{2,3,1,0:T(2,128)S(1)}, u32[]{:S(2)}, u32[]{:S(2)}) async-start(f32[32,4,4,2]{2,3,1,0:T(2,128)} %copy.143), calls=%async_computation.3 | async-start | bytes 262144 | tf_op jit(solution)/shard_map/all_to_all | solution.py:144
  252.9 24.7 %all-to-all-start.1 = ((f32[32,4,4,320]{3,2,1,0:T(4,128)}), f32[32,4,4,320]{3,2,1,0:T(4,128)S(1)}, u32[]{:S(2)}, u32[]{:S(2)}) async-start(f32[32,4,4,320]{3,2,1,0:T(4,128)} %copy.136), calls=%async_computation.1 | async-start | bytes 1572864 | tf_op jit(solution)/shard_map/all_to_all | solution.py:143
  307.3 29.7 %copy-start.1 = (bf16[32,4,2304]{2,1,0:T(4,128)(2,1)S(1)}, bf16[32,4,2304]{2,1,0:T(4,128)(2,1)}, u32[]{:S(2)}) copy-start(bf16[32,4,2304]{2,1,0:T(4,128)(2,1)} %param.10) | copy-start | bytes 1769476
where the time goes:
time: 338 us; the launch traced here: 337 us
  blocking collectives  154 us (46%)
  other arithmetic  54 us (16%)
  starting transfers between devices  46.9 us (14%)
  local copies, waits for them, and re-layouts  42.4 us (13%)
  matrix products  21.1 us (6%)
  waiting for transfers between devices  18.4 us (5%)
    all_gather x1, blocking collectives, on_device(): taps_all = lax.all_gather(conv_weight, 'heads', axis=1, tiled=True)  141 us
    all_to_all x1, starting transfers between devices, on_device(): lax.all_to_all(gate_pre, 'heads', split_axis=0, concat_axis=2, tiled=True)  27.4 us
    reduce_sum x2, other arithmetic, run_steps(): heads_now = jnp.sum(queries[:, step_index, :, :, None] * updated, axis=2)  22 us
    reduce_sum x3, other arithmetic, run_steps(): predicted = jnp.sum(keys_all[:, step_index, :, :, None] * faded, axis=2)  18.7 us
    all_to_all x1, waiting for transfers between devices, on_device(): lax.all_to_all(projected, 'heads', split_axis=0, concat_axis=2, tiled=True)  18.4 us
    all_to_all x1, blocking collectives, on_device(): lax.all_to_all(local_out, 'heads', split_axis=2, concat_axis=0, tiled=True)  12.2 us
    reshape x1, local copies, waits for them, and re-layouts, on_device(): mine_weight.reshape(D, per_device * unit_width)  11.9 us
    dot_general x1, matrix products, pick_state(): jnp.einsum('rhkv,uh->rukv', delta_state, selector, precision=lax.Precisio...  11.6 us
  transfers between devices with their start and end apart: 4, of which 1 were waited for; matrix products, arithmetic and copies ran while one was open for 20% of the time, Pallas kernels for 0%

commit v1 on v0

v1 whole, which is shorter than its diff:
```python
import functools

import jax
import jax.numpy as jnp
from jax import lax
from jax.experimental import pallas as pl
from jax.experimental.pallas import tpu as pltpu
from jax.sharding import PartitionSpec as P

D = 2304
H = 32
DK = 128
TAPS = 4
STEPS = 4
HALF = 64
UNITS = 64
LOCAL = 2
ROWS = LOCAL * STEPS
HEADS_WIDTH = H * DK

norm_eps = 1e-06


def unit_tables(old_heads, new_units):
    positions = jnp.arange(H, dtype=jnp.int32)
    inverse = jnp.sum(
        jnp.where(old_heads[None, :] == positions[:, None], positions[None, :], 0), axis=1
    )
    heads_of = new_units // 2
    halves = new_units % 2
    old_slots = jnp.sum(
        jnp.where(heads_of[:, None] == positions[None, :], inverse[None, :], 0), axis=1
    )
    return (old_slots, halves)


def shift_rows(value, lag, row_step):
    if lag == 0:
        return value
    moved = pltpu.roll(value, lag, 0)
    return jnp.where(row_step >= lag, moved, 0.0)


def delta_kernel(
    slots_ref, halves_ref, lengths_ref, queries_ref, keys_ref, values_ref, gates_ref,
    early_ref, taps_ref, state_ref, out_ref, heads_ref,
):
    row = lax.broadcasted_iota(jnp.int32, (ROWS, DK), 0)
    row_step = row % STEPS
    lane = lax.broadcasted_iota(jnp.int32, (ROWS, DK), 1)
    row_length = jnp.where(row < STEPS, lengths_ref[0], lengths_ref[1])
    live = row_step < row_length

    def activate(source_ref, part, head):
        columns = pl.ds(part * HEADS_WIDTH + head * DK, DK)
        fresh = source_ref[:, pl.ds(head * DK, DK)]
        total = early_ref[:, columns]
        for lag in range(TAPS):
            tap = taps_ref[TAPS - 1 - lag : TAPS - lag, columns].astype(jnp.float32)
            total = total + tap * shift_rows(fresh, lag, row_step)
        return total / (1.0 + jnp.exp(-total))

    def lane_sum(value):
        return jnp.sum(value, axis=-1, keepdims=True)

    def unit_length(value):
        return value * lax.rsqrt(lane_sum(value * value) + norm_eps)

    for head in range(H):
        query = unit_length(activate(queries_ref, 0, head))
        key = unit_length(activate(keys_ref, 1, head))
        value = activate(values_ref, 2, head)
        beta_logit = jnp.broadcast_to(gates_ref[:, head : head + 1], (ROWS, DK))
        decay_logit = jnp.broadcast_to(gates_ref[:, H + head : H + head + 1], (ROWS, DK))
        beta = 1.0 / (1.0 + jnp.exp(-beta_logit))
        decay = 1.0 / (1.0 + jnp.exp(decay_logit))
        fades = [jnp.ones_like(decay)]
        for lag in range(1, STEPS + 1):
            fades.append(
                jnp.where(
                    row_step >= lag - 1,
                    fades[-1] * (pltpu.roll(decay, lag - 1, 0) if lag > 1 else decay),
                    fades[-1],
                )
            )
        both = jnp.concatenate([key, query], axis=0)
        seen = [
            jnp.dot(both, state_ref[r, head], precision=lax.Precision.HIGHEST,
                    preferred_element_type=jnp.float32)
            for r in range(LOCAL)
        ]
        key_seen = jnp.where(row < STEPS, seen[0][:ROWS], seen[1][:ROWS])
        query_seen = jnp.where(row < STEPS, seen[0][ROWS:], seen[1][ROWS:])
        base = beta * (value - fades[STEPS] * key_seen)
        pulls = [None] + [
            beta * fades[lag] * lane_sum(key * shift_rows(key, lag, row_step))
            for lag in range(1, STEPS)
        ]
        solved = base
        for _ in range(STEPS - 1):
            following = base
            for lag in range(1, STEPS):
                following = following - pulls[lag] * shift_rows(solved, lag, row_step)
            solved = following
        out = fades[STEPS] * query_seen
        for lag in range(STEPS):
            moved_key = shift_rows(key, lag, row_step)
            weight = fades[lag] * lane_sum(query * moved_key)
            out = out + weight * shift_rows(solved, lag, row_step)
        heads_ref[head] = jnp.where(live, out, 0.0)

    for pair in range(UNITS // 2):
        first = heads_ref[slots_ref[2 * pair]]
        second = heads_ref[slots_ref[2 * pair + 1]]
        first = jnp.where(halves_ref[2 * pair] == 0, first, pltpu.roll(first, HALF, 1))
        second = jnp.where(halves_ref[2 * pair + 1] == 0, pltpu.roll(second, HALF, 1), second)
        joined = jnp.where(lane < HALF, first, second)
        heads_ref[H + pair] = joined
    for quad in range(UNITS // 4):
        out_ref[quad] = jnp.concatenate(
            [heads_ref[H + 2 * quad], heads_ref[H + 2 * quad + 1]], axis=0
        ).astype(jnp.bfloat16)


def run_delta(slots, halves, lengths, queries, keys, values, gates, early, taps, state):
    smem = pl.BlockSpec(memory_space=pltpu.SMEM)
    vmem = pl.BlockSpec(memory_space=pltpu.VMEM)
    return pl.pallas_call(
        delta_kernel,
        out_shape=jax.ShapeDtypeStruct((UNITS // 4, 2 * ROWS, DK), jnp.bfloat16),
        in_specs=[smem] * 3 + [vmem] * 7,
        out_specs=vmem,
        scratch_shapes=[pltpu.VMEM((2 * H, ROWS, DK), jnp.float32)],
        compiler_params=pltpu.CompilerParams(vmem_limit_bytes=32 * 1024 * 1024),
        cost_estimate=pl.CostEstimate(flops=40_000_000, bytes_accessed=5_000_000, transcendentals=0),
        name="delta_rule",
    )(slots, halves, lengths, queries, keys, values, gates, early, taps, state)


def swap(value, bit, devices):
    return lax.ppermute(value, "heads", [(i, i ^ bit) for i in range(devices)])


def on_device(
    tokens,
    qkv_weight,
    gate_weight,
    conv_weight,
    delta_state,
    conv_state,
    old_heads,
    new_units,
    slot_of,
    lengths,
):
    devices = lax.axis_size("heads")
    me = lax.axis_index("heads")
    per_device = UNITS // devices
    depth = qkv_weight.shape[0]
    row_count = tokens.shape[0]
    chips = devices // 2

    old_slots, halves = unit_tables(old_heads, new_units)
    bits = [1 << b for b in range(1, devices.bit_length() - 1)]
    order = []
    for place in range(chips):
        offset = 0
        for at, bit in enumerate(bits):
            if place & (chips >> (at + 1)):
                offset |= bit
        order.append(offset)
    holders = jnp.bitwise_xor(jnp.asarray(order, jnp.int32), me)
    old_rows = (holders[:, None] * LOCAL + jnp.arange(LOCAL, dtype=jnp.int32)[None, :]).reshape(-1)
    flat_tokens = tokens.reshape(row_count * STEPS, D)
    steps = jnp.arange(STEPS, dtype=jnp.int32)
    wanted = (old_rows[:, None] * STEPS + steps[None, :]).reshape(-1)
    offered = (slot_of[:, None] * STEPS + steps[None, :]).reshape(-1)
    picker = (wanted[:, None] == offered[None, :]).astype(jnp.bfloat16)

    def token_part(owner):
        columns = lax.dynamic_slice_in_dim(flat_tokens, owner * depth, depth, 1)
        return jnp.dot(picker, columns, preferred_element_type=jnp.float32).astype(jnp.bfloat16)

    mine, theirs = token_part(me), token_part(jnp.bitwise_xor(me, 1))
    half_rows = chips * ROWS // 2

    chunks = []
    for part in (1, 0, 2):
        block = qkv_weight[:, part * HEADS_WIDTH : (part + 1) * HEADS_WIDTH]
        if part == 1:
            block = jnp.concatenate([block, gate_weight], axis=1)
        chunks.append(block)
    others = [swap(block, 1, devices) for block in chunks]

    def product(rows, block, other):
        return jnp.dot(mine[rows], block, preferred_element_type=jnp.float32) + jnp.dot(
            theirs[rows], other, preferred_element_type=jnp.float32
        )

    sums = []
    for block, other in zip(chunks, others):
        sent = swap(product(slice(half_rows, None), block, other), bits[0], devices)
        kept = product(slice(0, half_rows), block, other)
        total = kept + sent
        for bit in bits[1:]:
            half = total.shape[0] // 2
            total = total[:half] + swap(total[half:], bit, devices)
        sums.append(total)

    taps = lax.all_gather(conv_weight, "heads", axis=1, tiled=True)
    taps_f = taps.astype(jnp.float32)
    early = []
    for step in range(STEPS):
        term = jnp.zeros_like(conv_state[:, 0])
        for tap in range(TAPS - 1 - step):
            term = term + taps_f[tap][None] * conv_state[:, step + tap]
        early.append(term)
    early = jnp.stack(early, axis=1).reshape(ROWS, 3 * HEADS_WIDTH)

    my_rows = me * LOCAL + jnp.arange(LOCAL, dtype=jnp.int32)
    my_lengths = jnp.sum(
        jnp.where(slot_of[None, :] == my_rows[:, None], lengths[None, :], 0), axis=1
    )
    keys, gates = sums[0][:, :HEADS_WIDTH], sums[0][:, HEADS_WIDTH:]
    local_out = run_delta(
        old_slots, halves, my_lengths, sums[1], keys, sums[2], gates, early, taps, delta_state
    )

    placer = (offered[:, None] == jnp.arange(row_count * STEPS, dtype=jnp.int32)[None, :]).astype(
        jnp.bfloat16
    )
    if per_device % 2 == 0:
        pairs = per_device // 2
        sending = local_out.reshape(devices, pairs * ROWS, DK)
        got = lax.all_to_all(sending, "heads", split_axis=0, concat_axis=0, tiled=True)
        got = got.reshape(devices, pairs, ROWS, DK)
        got = jnp.concatenate([got[:, pair] for pair in range(pairs)], axis=-1)
        got = got.reshape(devices * ROWS, pairs * DK)
    else:
        units = local_out.reshape(UNITS // 2, ROWS, 2, HALF).transpose(0, 2, 1, 3)
        sending = units.reshape(devices, per_device * ROWS, HALF)
        got = lax.all_to_all(sending, "heads", split_axis=0, concat_axis=0, tiled=True)
        got = got.reshape(devices, per_device, ROWS, HALF).transpose(0, 2, 1, 3)
        got = got.reshape(devices * ROWS, per_device * HALF)
    outputs = jnp.dot(placer, got, preferred_element_type=jnp.float32).astype(jnp.bfloat16)
    return outputs.reshape(row_count, STEPS, per_device * HALF)


def solution(mesh):
    in_specs = (
        P("groups", None, None),
        P(("groups", "heads"), None),
        P(("groups", "heads"), None),
        P("groups", "heads"),
        P(("groups", "heads"), None, None, None),
        P(("groups", "heads"), None, None),
        P(),
        P(),
        P("groups"),
        P("groups"),
    )
    out_specs = P("groups", None, "heads")
    return jax.shard_map(
        on_device, mesh=mesh, in_specs=in_specs, out_specs=out_specs, check_vma=False
    )
```

time: 338 us -> 124 us (0.37)
  blocking collectives: 154 us -> 32.4 us
  other arithmetic: 54 us -> 3.71 us
  starting transfers between devices: 46.9 us -> 6.93 us
  local copies, waits for them, and re-layouts: 42.4 us -> 10.8 us
  waiting for transfers between devices: 18.4 us -> 44.7 us
  Pallas kernels: 0 us -> 6.71 us
    all_gather x1, blocking collectives: 141 us -> 22.9 us  [on_device(): taps = lax.all_gather(conv_weight, 'heads', axis=1, tiled=True)]
    all_to_all x4 -> x0, starting transfers between devices: 46.9 us -> none  [the longest x1 27.4 us: on_device(): lax.all_to_all(gate_pre, 'heads', split_axis=0, concat_axis=2, tiled=True)]
    ppermute x0 -> x12, waiting for transfers between devices: none -> 44.7 us  [swap(): return lax.ppermute(value, 'heads', [(i, i ^ bit) for i in range(devices)])]
    reduce_sum x7 -> x1, other arithmetic: 41.1 us -> 0.18 us  [on_device(): jnp.sum(jnp.where(slot_of[None, :] == my_rows[:, None], lengths[None, :],...]
    all_to_all x4 -> x0, waiting for transfers between devices: 18.4 us -> none  [the longest x1 18.4 us: on_device(): lax.all_to_all(projected, 'heads', split_axis=0, concat_axis=2, tiled=True)]
    dot_general x4 -> x0, local copies, waits for them, and re-layouts: 11.2 us -> none  [the longest x2 10.3 us: on_device(): jnp.dot(flattened, mine_weight.reshape(D, per_device * unit_width), prefe...]
    reshape x5 -> x3, local copies, waits for them, and re-layouts: 13.1 us -> 3.09 us  [the longest x1 2.3 us: on_device(): flat_tokens = tokens.reshape(row_count * STEPS, D)]
    concatenate x2 -> x1, local copies, waits for them, and re-layouts: 9.54 us -> 0.01 us  [on_device(): got = jnp.concatenate([got[:, pair] for pair in range(pairs)], axis=-1)]
  transfers between devices with their start and end apart: 4 -> 12, of which waited for: 1 -> 7; matrix products, arithmetic and copies ran while one was open for 20% -> 21% of each run, Pallas kernels for 0% -> 0%
where the time goes in v1:
time: 124 us
  waiting for transfers between devices  44.7 us (36%)
  blocking collectives  32.4 us (26%)
  matrix products  17.9 us (14%)
  local copies, waits for them, and re-layouts  10.8 us (9%)
  starting transfers between devices  6.93 us (6%)
  Pallas kernels  6.71 us (5%)
  other arithmetic  3.71 us (3%)
    ppermute x12, waiting for transfers between devices, swap(): return lax.ppermute(value, 'heads', [(i, i ^ bit) for i in range(devices)])  44.7 us
    all_gather x1, blocking collectives, on_device(): taps = lax.all_gather(conv_weight, 'heads', axis=1, tiled=True)  22.9 us
    all_to_all x1, blocking collectives, on_device(): lax.all_to_all(sending, 'heads', split_axis=0, concat_axis=0, tiled=True)  9.59 us
    dot_general x6, matrix products, product(): jnp.dot(theirs[rows], other, preferred_element_type=jnp.float32)  9.5 us
    ppermute x12, starting transfers between devices, swap(): return lax.ppermute(value, 'heads', [(i, i ^ bit) for i in range(devices)])  6.93 us
    pallas_call x1, Pallas kernels, run_delta(): pl.pallas_call(delta_kernel, out_shape=jax.ShapeDtypeStruct((UNITS // 4,...  6.71 us
    dot_general x6, matrix products, product(): jnp.dot(mine[rows], block, preferred_element_type=jnp.float32)  6.01 us
    slice x1, local copies, waits for them, and re-layouts, on_device(): block = qkv_weight[:, part * HEADS_WIDTH:(part + 1) * HEADS_WIDTH]  3.94 us
  transfers between devices with their start and end apart: 12, of which 7 were waited for; matrix products, arithmetic and copies ran while one was open for 21% of the time, Pallas kernels for 0%

profile of v1, /device:TPU:0, one launch (start us, length us, event | category | flops | bytes accessed | tf_op | source)
XLA Modules:
  0.0 123.7 jit_solution(7416237529264360110)
XLA Ops:
  0.0 3.9 %fusion.41 = (bf16[144,4096]{1,0:T(8,128)(2,1)}, bf16[144,4096]{1,0:T(8,128)(2,1)}, bf16[144,4096]{1,0:T(8,128)(2,1)}) fusion(bf16[144,12288]{1,0:T(8,128)(2,1)} %param.12), kind=kLoop, calls=%fused_computation.80 | loop fusion | bytes 7077888 | tf_op jit(solution)/shard_map/slice | solution.py:189
  4.4 0.7 copy.16
  5.1 2.6 %pad_maximum_fusion = bf16[144,4160]{1,0:T(8,128)(2,1)} fusion(bf16[144,64]{1,0:T(8,128)(2,1)} %copy.16, bf16[144,4096]{1,0:T(8,128)(2,1)} %get-tuple-element.7), kind=kLoop, calls=%fused_computation.9 | loop fusion | flops 2396160 | bytes 2396160 | tf_op jit(solution)/shard_map/concatenate | solution.py:191
  8.4 0.7 add.156
  9.2 0.7 add.146
  9.9 2.3 %reshape.124 = bf16[128,2304]{1,0:T(8,128)(2,1)} reshape(bf16[32,4,2304]{2,1,0:T(4,128)(2,1)} %param.11) | data formatting | bytes 1179648 | tf_op jit(solution)/shard_map/reshape | solution.py:174
  12.1 1.1 convolution_convert_fusion.2
  13.3 1.1 fusion.18
  14.4 1.1 fusion.27
  16.4 1.1 convolution_convert_fusion.1
  17.5 22.9 %all_gather.3.taps_ref = bf16[4,12288]{1,0:T(4,128)(2,1)S(1)} all-gather(bf16[4,768]{1,0:T(4,128)(2,1)S(1)} %copy-done.12), channel_id=1, replica_groups=mesh['groups'=2,'heads'=16] {'heads'}, dimensions={1}, use_global_device_ids=true | all-gather | bytes 104448 | tf_op jit(solution)/shard_map/all_gather | solution.py:210
  41.7 0.5 copy-done.3
  42.6 1.6 %fusion.22 = f32[32,4096]{1,0:T(8,128)S(1)} fusion(bf16[64,144]{1,0:T(8,128)(2,1)S(1)} %copy-done.7, bf16[144,12288]{1,0:T(8,128)(2,1)} %param.12), kind=kOutput, calls=%fused_computation.50 | convolution fusion | flops 37748736 | bytes 1720320 | tf_op jit(solution)/shard_map/dot_general | solution.py:196
  44.2 1.6 %fusion.31 = f32[32,4096]{1,0:T(8,128)S(1)} fusion(bf16[64,144]{1,0:T(8,128)(2,1)S(1)} %copy-done.7, bf16[144,12288]{1,0:T(8,128)(2,1)} %param.12), kind=kOutput, calls=%fused_computation.59 | convolution fusion | flops 37748736 | bytes 1720320 | tf_op jit(solution)/shard_map/dot_general | solution.py:196
  45.8 1.6 %convolution_add_fusion.2 = f32[32,4096]{1,0:T(8,128)S(1)} fusion(f32[32,4096]{1,0:T(8,128)S(1)} %copy-done.4, bf16[144,4096]{1,0:T(8,128)(2,1)} %collective-permute-done.8, bf16[64,144]{1,0:T(8,128)(2,1)S(1)} %convolution_convert_fusion.1), kind=kOutput, calls=%fused_computation.3 | convolution fusion | flops 37879808 | bytes 2244608 | tf_op jit(solution)/shard_map/dot_general | solution.py:196
  47.5 1.6 %convolution_add_fusion.4 = f32[32,4096]{1,0:T(8,128)S(1)} fusion(f32[32,4096]{1,0:T(8,128)S(1)} %fusion.22, bf16[144,4096]{1,0:T(8,128)(2,1)} %collective-permute-done, bf16[64,144]{1,0:T(8,128)(2,1)S(1)} %convolution_convert_fusion.1), kind=kOutput, calls=%fused_computation.5 | convolution fusion | flops 37879808 | bytes 2244608 | tf_op jit(solution)/shard_map/dot_general | solution.py:196
  49.1 2.1 %collective-permute-start.1 = (f32[32,4096]{1,0:T(8,128)S(1)}, f32[32,4096]{1,0:T(8,128)S(1)}, u32[]{:S(2)}, u32[]{:S(2)}) collective-permute-start(f32[32,4096]{1,0:T(8,128)S(1)} %convolution_add_fusion.4), channel_id=1, source_target_pairs={{0,2},{1,3},{2,0},{3,1},{4,6},{5,7},{6,4},{7,5},{8,10},{9,11},{10,... | collective-permute-start | bytes 1572872 | tf_op jit(solution)/shard_map/ppermute | solution.py:141
  51.1 1.6 %convolution_add_fusion = f32[32,4160]{1,0:T(8,128)S(1)} fusion(f32[32,4160]{1,0:T(8,128)S(1)} %fusion.20, bf16[144,4160]{1,0:T(8,128)(2,1)} %collective-permute-done.4, bf16[64,144]{1,0:T(8,128)(2,1)S(1)} %convolution_convert_fusion.1), kind=kOutput, calls=%fused_computation | convolution fusion | flops 38471680 | bytes 2287616 | tf_op jit(solution)/shard_map/dot_general | solution.py:196
  52.9 9.3 %collective-permute-done.9 = f32[32,4096]{1,0:T(8,128)S(1)} collective-permute-done((f32[32,4096]{1,0:T(8,128)S(1)}, f32[32,4096]{1,0:T(8,128)S(1)}, u32[]{:S(2)}, u32[]{:S(2)}) %collective-permute-start.9) | collective-permute-done | bytes 524320 | tf_op jit(solution)/shard_map/ppermute | solution.py:141
  62.2 1.6 %fusion.2 = f32[32,4096]{1,0:T(8,128)S(1)} fusion(f32[32,4096]{1,0:T(8,128)S(1)} %collective-permute-done.9, f32[32,4096]{1,0:T(8,128)S(1)} %copy-done.5, bf16[144,4096]{1,0:T(8,128)(2,1)} %collective-permute-done.8, bf16[64,144]{1,0:T(8,128)(2,1)S(1)} %convolution_convert_fusion.1), kind=kOutput, calls=%fused_computation.8 | convolution fusion | flops 38010880 | bytes 2768896 | tf_op jit(solution)/shard_map/dot_general | solution.py:196
  63.9 9.5 %collective-permute-done.1 = f32[32,4096]{1,0:T(8,128)S(1)} collective-permute-done((f32[32,4096]{1,0:T(8,128)S(1)}, f32[32,4096]{1,0:T(8,128)S(1)}, u32[]{:S(2)}, u32[]{:S(2)}) %collective-permute-start.1) | collective-permute-done | bytes 524320 | tf_op jit(solution)/shard_map/ppermute | solution.py:141
  73.4 1.6 %fusion.1 = f32[32,4096]{1,0:T(8,128)S(1)} fusion(f32[32,4096]{1,0:T(8,128)S(1)} %collective-permute-done.1, f32[32,4096]{1,0:T(8,128)S(1)} %fusion.31, bf16[144,4096]{1,0:T(8,128)(2,1)} %collective-permute-done, bf16[64,144]{1,0:T(8,128)(2,1)S(1)} %convolution_convert_fusion.1), kind=kOutput, calls=%fused_computation.7 | convolution fusion | flops 38010880 | bytes 2768896 | tf_op jit(solution)/shard_map/dot_general | solution.py:196
  75.1 9.3 %collective-permute-done.5 = f32[32,4160]{1,0:T(8,128)S(1)} collective-permute-done((f32[32,4160]{1,0:T(8,128)S(1)}, f32[32,4160]{1,0:T(8,128)S(1)}, u32[]{:S(2)}, u32[]{:S(2)}) %collective-permute-start.5) | collective-permute-done | bytes 532512 | tf_op jit(solution)/shard_map/ppermute | solution.py:141
  84.5 1.6 %fusion = f32[32,4160]{1,0:T(8,128)S(1)} fusion(f32[32,4160]{1,0:T(8,128)S(1)} %collective-permute-done.5, f32[32,4160]{1,0:T(8,128)S(1)} %fusion.29, bf16[144,4160]{1,0:T(8,128)(2,1)} %collective-permute-done.4, bf16[64,144]{1,0:T(8,128)(2,1)S(1)} %convolution_convert_fusion.1), kind=kOutput, calls=%fused_computation.2 | convolution fusion | flops 38604800 | bytes 2828288 | tf_op jit(solution)/shard_map/dot_general | solution.py:196
  86.4 3.0 %collective-permute-start.3 = (f32[8,4096]{1,0:T(8,128)S(1)}, f32[8,4096]{1,0:T(8,128)S(1)}, u32[]{:S(2)}, u32[]{:S(2)}) collective-permute-start(f32[8,4096]{1,0:T(8,128)S(1)} %slice.146), channel_id=1, source_target_pairs={{0,8},{1,9},{2,10},{3,11},{4,12},{5,13},{6,14},{7,15},{8,0},{9,1},... | collective-permute-start | bytes 393224 | tf_op jit(solution)/shard_map/ppermute | solution.py:141
  89.3 6.5 %collective-permute-done.6 = f32[16,4160]{1,0:T(8,128)S(1)} collective-permute-done((f32[16,4160]{1,0:T(8,128)S(1)}, f32[16,4160]{1,0:T(8,128)S(1)}, u32[]{:S(2)}, u32[]{:S(2)}) %collective-permute-start.6) | collective-permute-done | bytes 266272 | tf_op jit(solution)/shard_map/ppermute | solution.py:141
  96.4 5.7 %collective-permute-done.11 = f32[8,4096]{1,0:T(8,128)S(1)} collective-permute-done((f32[8,4096]{1,0:T(8,128)S(1)}, f32[8,4096]{1,0:T(8,128)S(1)}, u32[]{:S(2)}, u32[]{:S(2)}) %collective-permute-start.11) | collective-permute-done | bytes 131104 | tf_op jit(solution)/shard_map/ppermute | solution.py:141
  102.0 2.8 %collective-permute-done.3 = f32[8,4096]{1,0:T(8,128)S(1)} collective-permute-done((f32[8,4096]{1,0:T(8,128)S(1)}, f32[8,4096]{1,0:T(8,128)S(1)}, u32[]{:S(2)}, u32[]{:S(2)}) %collective-permute-start.3) | collective-permute-done | bytes 131104 | tf_op jit(solution)/shard_map/ppermute | solution.py:141
  104.9 1.5 %collective-permute-done.7 = f32[8,4160]{1,0:T(8,128)S(1)} collective-permute-done((f32[8,4160]{1,0:T(8,128)S(1)}, f32[8,4160]{1,0:T(8,128)S(1)}, u32[]{:S(2)}, u32[]{:S(2)}) %collective-permute-start.7) | collective-permute-done | bytes 133152 | tf_op jit(solution)/shard_map/ppermute | solution.py:141
  106.5 6.7 %delta_rule.1 = bf16[16,16,128]{2,1,0:T(8,128)(2,1)S(1)} custom-call(s32[64]{0:T(128)S(1)} %select_reduce_fusion.slots_ref, s32[64]{0:T(128)S(1)} %get-tuple-element.16.halves_ref, s32[2]{0:T(128)S(1)} %fusion.33.lengths_ref, f32[8,4096]{1,0:T(8,128)S(1)} %slice_add_fusion.5.queries_ref, f32[8,4096]{1,0:T(8,128)S(1)} %slice.151.keys_ref, ...), custom_call_target="tpu_custom_call" | custom-call | flops 40000000 | bytes 5000000 | tf_op jit(solution)/shard_map/delta_rule/pallas_call | solution.py:128
  113.2 9.6 %all_to_all.5 = bf16[16,16,128]{2,1,0:T(8,128)(2,1)S(1)} all-to-all(bf16[16,16,128]{2,1,0:T(8,128)(2,1)S(1)} %delta_rule.1), channel_id=1, replica_groups=mesh['groups'=2,'heads'=16] {'heads'}, dimensions={0} | all-to-all | bytes 131072 | tf_op jit(solution)/shard_map/all_to_all | solution.py:235
  123.0 0.7 reshape.127
  (91 shorter events, 5.3 us)
Async XLA Ops:
  0.0 4.4 %copy-start.11 = (bf16[144,64]{0,1:T(8,128)(2,1)S(1)}, bf16[144,64]{0,1:T(8,128)(2,1)}, u32[]{:S(2)}) copy-start(bf16[144,64]{0,1:T(8,128)(2,1)} %param.13) | copy-start | bytes 55300
  0.0 8.2 %copy-start.20 = (s32[8]{0:T(128)S(1)}, s32[8]{0:T(128)}, u32[]{:S(2)}) copy-start(s32[8]{0:T(128)} %constant.44.clone) | copy-start | bytes 100
  0.0 9.1 %copy-start.16 = (s32[32]{0:T(128)S(1)}, s32[32]{0:T(128)}, u32[]{:S(2)}) copy-start(s32[32]{0:T(128)} %param.19) | copy-start | bytes 388
  4.0 41.9 %collective-permute-start.8 = (bf16[144,4096]{1,0:T(8,128)(2,1)}, bf16[144,4096]{1,0:T(8,128)(2,1)}, u32[]{:S(2)}, u32[]{:S(2)}) collective-permute-start(bf16[144,4096]{1,0:T(8,128)(2,1)} %get-tuple-element.5), channel_id=1, source_target_pairs={{0,1},{1,0},{2,3},{3,2},{4,5},{5,4},{6,7},{7,6},{8,9},{9,8},{10,11... | collective-permute-start | bytes 3538952 | tf_op jit(solution)/shard_map/ppermute | solution.py:141
  5.1 8.1 %copy-start.1 = (bf16[144,12288]{1,0:T(8,128)(2,1)S(1)}, bf16[144,12288]{1,0:T(8,128)(2,1)}, u32[]{:S(2)}) copy-start(bf16[144,12288]{1,0:T(8,128)(2,1)} %param.12) | copy-start | bytes 10616836
  7.7 43.4 %collective-permute-start.4 = (bf16[144,4160]{1,0:T(8,128)(2,1)}, bf16[144,4160]{1,0:T(8,128)(2,1)}, u32[]{:S(2)}, u32[]{:S(2)}) collective-permute-start(bf16[144,4160]{1,0:T(8,128)(2,1)} %pad_maximum_fusion), channel_id=1, source_target_pairs={{0,1},{1,0},{2,3},{3,2},{4,5},{5,4},{6,7},{7,6},{8,9},{9,8},{10,11... | collective-permute-start | bytes 3594248 | tf_op jit(solution)/shard_map/ppermute | solution.py:141
  7.8 39.7 %collective-permute-start = (bf16[144,4096]{1,0:T(8,128)(2,1)}, bf16[144,4096]{1,0:T(8,128)(2,1)}, u32[]{:S(2)}, u32[]{:S(2)}) collective-permute-start(bf16[144,4096]{1,0:T(8,128)(2,1)} %get-tuple-element.6), channel_id=1, source_target_pairs={{0,1},{1,0},{2,3},{3,2},{4,5},{5,4},{6,7},{7,6},{8,9},{9,8},{10,11... | collective-permute-start | bytes 3538952 | tf_op jit(solution)/shard_map/ppermute | solution.py:141
  13.3 2.2 %copy-start.6 = (bf16[64,144]{1,0:T(8,128)(2,1)}, bf16[64,144]{1,0:T(8,128)(2,1)S(1)}, u32[]{:S(2)}) copy-start(bf16[64,144]{1,0:T(8,128)(2,1)S(1)} %convolution_convert_fusion.2) | copy-start | bytes 55300
  14.4 1.4 %copy-start.2 = (bf16[144,4096]{1,0:T(8,128)(2,1)S(1)}, bf16[144,4096]{1,0:T(8,128)(2,1)}, u32[]{:S(2)}) copy-start(bf16[144,4096]{1,0:T(8,128)(2,1)} %get-tuple-element.7) | copy-start | bytes 3538948
  14.4 1.4 %copy-start.9 = (bf16[144,64]{1,0:T(8,128)(2,1)S(1)}, bf16[144,64]{1,0:T(8,128)(2,1)}, u32[]{:S(2)}) copy-start(bf16[144,64]{1,0:T(8,128)(2,1)} %copy.16) | copy-start | bytes 55300
  15.7 0.7 copy-start.14
  15.7 1.8 %copy-start.12 = (bf16[4,768]{1,0:T(4,128)(2,1)S(1)}, bf16[4,768]{1,0:T(4,128)(2,1)}, u32[]{:S(2)}) copy-start(bf16[4,768]{1,0:T(4,128)(2,1)} %param.14) | copy-start | bytes 18436
  15.7 24.8 %copy-start.15 = (s32[32]{0:T(128)S(1)}, s32[32]{0:T(128)}, u32[]{:S(2)}) copy-start(s32[32]{0:T(128)} %param.20) | copy-start | bytes 388
  15.8 24.8 %copy-start.17 = (s32[32]{0:T(128)S(1)}, s32[32]{0:T(128)}, u32[]{:S(2)}) copy-start(s32[32]{0:T(128)} %param.19) | copy-start | bytes 388
  15.8 25.0 %copy-start.8 = (f32[2,3,12288]{2,0,1:T(2,128)S(1)}, f32[2,3,12288]{2,0,1:T(2,128)}, u32[]{:S(2)}) copy-start(f32[2,3,12288]{2,0,1:T(2,128)} %param.16) | copy-start | bytes 884740
  16.1 25.1 %copy-start.18 = (s32[64]{0:T(128)S(1)}, s32[64]{0:T(128)}, u32[]{:S(2)}) copy-start(s32[64]{0:T(128)} %param.18) | copy-start | bytes 772
  16.1 25.1 %copy-start.19 = (s32[32]{0:T(128)S(1)}, s32[32]{0:T(128)}, u32[]{:S(2)}) copy-start(s32[32]{0:T(128)} %param.17) | copy-start | bytes 388
  40.9 1.3 %copy-start.3 = (bf16[144,4096]{1,0:T(8,128)(2,1)S(1)}, bf16[144,4096]{1,0:T(8,128)(2,1)}, u32[]{:S(2)}) copy-start(bf16[144,4096]{1,0:T(8,128)(2,1)} %get-tuple-element.7) | copy-start | bytes 3538948
  40.9 1.3 %copy-start.7 = (bf16[64,144]{1,0:T(8,128)(2,1)S(1)}, bf16[64,144]{1,0:T(8,128)(2,1)}, u32[]{:S(2)}) copy-start(bf16[64,144]{1,0:T(8,128)(2,1)} %copy-done.6) | copy-start | bytes 55300
  40.9 1.3 %copy-start.10 = (bf16[144,64]{1,0:T(8,128)(2,1)S(1)}, bf16[144,64]{1,0:T(8,128)(2,1)}, u32[]{:S(2)}) copy-start(bf16[144,64]{1,0:T(8,128)(2,1)} %copy.16) | copy-start | bytes 55300
  44.2 1.6 %copy-start.4 = (f32[32,4096]{1,0:T(8,128)S(1)}, f32[32,4096]{1,0:T(8,128)}, u32[]{:S(2)}) copy-start(f32[32,4096]{1,0:T(8,128)} %fusion.18) | copy-start | bytes 1572868
  47.4 14.8 %collective-permute-start.9 = (f32[32,4096]{1,0:T(8,128)S(1)}, f32[32,4096]{1,0:T(8,128)S(1)}, u32[]{:S(2)}, u32[]{:S(2)}) collective-permute-start(f32[32,4096]{1,0:T(8,128)S(1)} %convolution_add_fusion.2), channel_id=1, source_target_pairs={{0,2},{1,3},{2,0},{3,1},{4,6},{5,7},{6,4},{7,5},{8,10},{9,11},{10,... | collective-permute-start | bytes 1572872 | tf_op jit(solution)/shard_map/ppermute | solution.py:141
  49.1 13.1 %copy-start.5 = (f32[32,4096]{1,0:T(8,128)S(1)}, f32[32,4096]{1,0:T(8,128)}, u32[]{:S(2)}) copy-start(f32[32,4096]{1,0:T(8,128)} %fusion.27) | copy-start | bytes 1572868
  49.1 24.4 %collective-permute-start.1 = (f32[32,4096]{1,0:T(8,128)S(1)}, f32[32,4096]{1,0:T(8,128)S(1)}, u32[]{:S(2)}, u32[]{:S(2)}) collective-permute-start(f32[32,4096]{1,0:T(8,128)S(1)} %convolution_add_fusion.4), channel_id=1, source_target_pairs={{0,2},{1,3},{2,0},{3,1},{4,6},{5,7},{6,4},{7,5},{8,10},{9,11},{10,... | collective-permute-start | bytes 1572872 | tf_op jit(solution)/shard_map/ppermute | solution.py:141
  52.7 31.7 %collective-permute-start.5 = (f32[32,4160]{1,0:T(8,128)S(1)}, f32[32,4160]{1,0:T(8,128)S(1)}, u32[]{:S(2)}, u32[]{:S(2)}) collective-permute-start(f32[32,4160]{1,0:T(8,128)S(1)} %convolution_add_fusion), channel_id=1, source_target_pairs={{0,2},{1,3},{2,0},{3,1},{4,6},{5,7},{6,4},{7,5},{8,10},{9,11},{10,... | collective-permute-start | bytes 1597448 | tf_op jit(solution)/shard_map/ppermute | solution.py:141
  63.8 22.3 %collective-permute-start.10 = (f32[16,4096]{1,0:T(8,128)S(1)}, f32[16,4096]{1,0:T(8,128)S(1)}, u32[]{:S(2)}, u32[]{:S(2)}) collective-permute-start(f32[16,4096]{1,0:T(8,128)S(1)} %slice.153), channel_id=1, source_target_pairs={{0,4},{1,5},{2,6},{3,7},{4,0},{5,1},{6,2},{7,3},{8,12},{9,13},{10,... | collective-permute-start | bytes 786440 | tf_op jit(solution)/shard_map/ppermute | solution.py:141
  75.0 11.3 %collective-permute-start.2 = (f32[16,4096]{1,0:T(8,128)S(1)}, f32[16,4096]{1,0:T(8,128)S(1)}, u32[]{:S(2)}, u32[]{:S(2)}) collective-permute-start(f32[16,4096]{1,0:T(8,128)S(1)} %slice.144), channel_id=1, source_target_pairs={{0,4},{1,5},{2,6},{3,7},{4,0},{5,1},{6,2},{7,3},{8,12},{9,13},{10,... | collective-permute-start | bytes 786440 | tf_op jit(solution)/shard_map/ppermute | solution.py:141
  86.1 9.8 %collective-permute-start.6 = (f32[16,4160]{1,0:T(8,128)S(1)}, f32[16,4160]{1,0:T(8,128)S(1)}, u32[]{:S(2)}, u32[]{:S(2)}) collective-permute-start(f32[16,4160]{1,0:T(8,128)S(1)} %slice.148), channel_id=1, source_target_pairs={{0,4},{1,5},{2,6},{3,7},{4,0},{5,1},{6,2},{7,3},{8,12},{9,13},{10,... | collective-permute-start | bytes 798728 | tf_op jit(solution)/shard_map/ppermute | solution.py:141
  86.2 20.3 %copy-start = (f32[2,32,128,128]{3,2,1,0:T(8,128)S(1)}, f32[2,32,128,128]{3,2,1,0:T(8,128)}, u32[]{:S(2)}) copy-start(f32[2,32,128,128]{3,2,1,0:T(8,128)} %state_ref.1) | copy-start | bytes 12582916
  86.2 15.8 %collective-permute-start.11 = (f32[8,4096]{1,0:T(8,128)S(1)}, f32[8,4096]{1,0:T(8,128)S(1)}, u32[]{:S(2)}, u32[]{:S(2)}) collective-permute-start(f32[8,4096]{1,0:T(8,128)S(1)} %slice.155), channel_id=1, source_target_pairs={{0,8},{1,9},{2,10},{3,11},{4,12},{5,13},{6,14},{7,15},{8,0},{9,1},... | collective-permute-start | bytes 393224 | tf_op jit(solution)/shard_map/ppermute | solution.py:141
  86.4 18.5 %collective-permute-start.3 = (f32[8,4096]{1,0:T(8,128)S(1)}, f32[8,4096]{1,0:T(8,128)S(1)}, u32[]{:S(2)}, u32[]{:S(2)}) collective-permute-start(f32[8,4096]{1,0:T(8,128)S(1)} %slice.146), channel_id=1, source_target_pairs={{0,8},{1,9},{2,10},{3,11},{4,12},{5,13},{6,14},{7,15},{8,0},{9,1},... | collective-permute-start | bytes 393224 | tf_op jit(solution)/shard_map/ppermute | solution.py:141
  95.9 10.5 %collective-permute-start.7 = (f32[8,4160]{1,0:T(8,128)S(1)}, f32[8,4160]{1,0:T(8,128)S(1)}, u32[]{:S(2)}, u32[]{:S(2)}) collective-permute-start(f32[8,4160]{1,0:T(8,128)S(1)} %slice.150), channel_id=1, source_target_pairs={{0,8},{1,9},{2,10},{3,11},{4,12},{5,13},{6,14},{7,15},{8,0},{9,1},... | collective-permute-start | bytes 399368 | tf_op jit(solution)/shard_map/ppermute | solution.py:141
  (1 other events, 0.6 us)

commit v2 on v1

v2 whole, which is shorter than its diff:
```python
import functools

import jax
import jax.numpy as jnp
from jax import lax
from jax.experimental import pallas as pl
from jax.experimental.pallas import tpu as pltpu
from jax.sharding import PartitionSpec as P

D = 2304
H = 32
DK = 128
TAPS = 4
STEPS = 4
HALF = 64
UNITS = 64
LOCAL = 2
ROWS = LOCAL * STEPS
HEADS_WIDTH = H * DK
PIECES = 2

norm_eps = 1e-06


def unit_tables(old_heads, new_units):
    positions = jnp.arange(H, dtype=jnp.int32)
    inverse = jnp.sum(
        jnp.where(old_heads[None, :] == positions[:, None], positions[None, :], 0), axis=1
    )
    heads_of = new_units // 2
    halves = new_units % 2
    old_slots = jnp.sum(
        jnp.where(heads_of[:, None] == positions[None, :], inverse[None, :], 0), axis=1
    )
    return (old_slots, halves)


def shift_rows(value, lag, row_step):
    if lag == 0:
        return value
    moved = pltpu.roll(value, lag, 0)
    return jnp.where(row_step >= lag, moved, 0.0)


def lane_sum(value):
    return jnp.sum(value, axis=-1, keepdims=True)


def unit_length(value):
    return value * lax.rsqrt(lane_sum(value * value) + norm_eps)


def activate(pieces, part, head, early_ref, taps_ref, row_step):
    per_piece = H // len(pieces)
    kept_ref, sent_ref = pieces[head // per_piece]
    inner = pl.ds(head % per_piece * DK, DK)
    fresh = kept_ref[:ROWS, inner] + sent_ref[:, inner]
    columns = pl.ds(part * HEADS_WIDTH + head * DK, DK)
    total = early_ref[:, columns]
    for lag in range(TAPS):
        tap = taps_ref[TAPS - 1 - lag : TAPS - lag, columns].astype(jnp.float32)
        total = total + tap * shift_rows(fresh, lag, row_step)
    return total / (1.0 + jnp.exp(-total))


def keys_kernel(*refs):
    ins, outs = refs[: 4 * PIECES + 3], refs[4 * PIECES + 3 :]
    key_refs = [(ins[2 * i], ins[2 * i + 1]) for i in range(PIECES)]
    query_refs = [(ins[2 * i], ins[2 * i + 1]) for i in range(PIECES, 2 * PIECES)]
    early_ref, taps_ref, state_ref = ins[4 * PIECES :]
    beta_ref, key_seen_ref, query_seen_ref, pulls_ref, weights_ref = outs
    row = lax.broadcasted_iota(jnp.int32, (ROWS, DK), 0)
    row_step = row % STEPS
    kept_ref, sent_ref = key_refs[0]
    width = HEADS_WIDTH // PIECES
    gates = kept_ref[:ROWS, width : width + 2 * H] + sent_ref[:, width : width + 2 * H]
    for head in range(H):
        key = unit_length(activate(key_refs, 1, head, early_ref, taps_ref, row_step))
        query = unit_length(activate(query_refs, 0, head, early_ref, taps_ref, row_step))
        beta_logit = jnp.broadcast_to(gates[:, head : head + 1], (ROWS, DK))
        decay_logit = jnp.broadcast_to(gates[:, H + head : H + head + 1], (ROWS, DK))
        beta = 1.0 / (1.0 + jnp.exp(-beta_logit))
        decay = 1.0 / (1.0 + jnp.exp(decay_logit))
        fades = [jnp.ones_like(decay), decay]
        for lag in range(2, STEPS + 1):
            earlier = pltpu.roll(decay, lag - 1, 0)
            fades.append(jnp.where(row_step >= lag - 1, fades[-1] * earlier, fades[-1]))
        both = jnp.concatenate([key, query], axis=0)
        seen = [
            jnp.dot(both, state_ref[r, head], precision=lax.Precision.HIGHEST,
                    preferred_element_type=jnp.float32)
            for r in range(LOCAL)
        ]
        beta_ref[head] = beta
        key_seen_ref[head] = beta * fades[STEPS] * jnp.where(
            row < STEPS, seen[0][:ROWS], seen[1][:ROWS]
        )
        query_seen_ref[head] = fades[STEPS] * jnp.where(
            row < STEPS, seen[0][ROWS:], seen[1][ROWS:]
        )
        for lag in range(STEPS):
            moved_key = shift_rows(key, lag, row_step)
            if lag:
                pulls_ref[lag - 1, head] = beta * fades[lag] * lane_sum(key * moved_key)
            weights_ref[lag, head] = fades[lag] * lane_sum(query * moved_key)


def values_kernel(slots_ref, halves_ref, lengths_ref, *refs):
    value_refs = [(refs[2 * i], refs[2 * i + 1]) for i in range(PIECES)]
    early_ref, taps_ref, beta_ref, key_seen_ref, query_seen_ref, pulls_ref, weights_ref = refs[
        2 * PIECES : 2 * PIECES + 7
    ]
    out_ref, heads_ref = refs[2 * PIECES + 7 :]
    row = lax.broadcasted_iota(jnp.int32, (ROWS, DK), 0)
    row_step = row % STEPS
    lane = lax.broadcasted_iota(jnp.int32, (ROWS, DK), 1)
    row_length = jnp.where(row < STEPS, lengths_ref[0], lengths_ref[1])
    live = row_step < row_length
    for head in range(H):
        value = activate(value_refs, 2, head, early_ref, taps_ref, row_step)
        base = beta_ref[head] * value - key_seen_ref[head]
        solved = base
        for _ in range(STEPS - 1):
            following = base
            for lag in range(1, STEPS):
                following = following - pulls_ref[lag - 1, head] * shift_rows(
                    solved, lag, row_step
                )
            solved = following
        out = query_seen_ref[head]
        for lag in range(STEPS):
            out = out + weights_ref[lag, head] * shift_rows(solved, lag, row_step)
        heads_ref[head] = jnp.where(live, out, 0.0)
    for quad in range(UNITS // 4):
        joined = []
        for pair in (2 * quad, 2 * quad + 1):
            first = heads_ref[slots_ref[2 * pair]]
            second = heads_ref[slots_ref[2 * pair + 1]]
            first = jnp.where(halves_ref[2 * pair] == 0, first, pltpu.roll(first, HALF, 1))
            second = jnp.where(halves_ref[2 * pair + 1] == 0, pltpu.roll(second, HALF, 1), second)
            joined.append(jnp.where(lane < HALF, first, second))
        out_ref[quad] = jnp.concatenate(joined, axis=0).astype(jnp.bfloat16)


def run_delta(slots, halves, lengths, keys, queries, values, early, taps, state):
    smem = pl.BlockSpec(memory_space=pltpu.SMEM)
    vmem = pl.BlockSpec(memory_space=pltpu.VMEM)
    params = pltpu.CompilerParams(vmem_limit_bytes=32 * 1024 * 1024)
    per_head = jax.ShapeDtypeStruct((H, ROWS, DK), jnp.float32)
    lags = [
        jax.ShapeDtypeStruct((count, H, ROWS, DK), jnp.float32) for count in (STEPS - 1, STEPS)
    ]
    flat = lambda pieces: [ref for piece in pieces for ref in piece]
    prepared = pl.pallas_call(
        keys_kernel,
        out_shape=[per_head] * 3 + lags,
        in_specs=[vmem] * (4 * PIECES + 3),
        out_specs=[vmem] * 5,
        compiler_params=params,
        cost_estimate=pl.CostEstimate(flops=40_000_000, bytes_accessed=9_000_000, transcendentals=0),
        name="keys_part",
    )(*flat(keys), *flat(queries), early, taps, state)
    return pl.pallas_call(
        values_kernel,
        out_shape=jax.ShapeDtypeStruct((UNITS // 4, 2 * ROWS, DK), jnp.bfloat16),
        in_specs=[smem] * 3 + [vmem] * (2 * PIECES + 7),
        out_specs=vmem,
        scratch_shapes=[pltpu.VMEM((H, ROWS, DK), jnp.float32)],
        compiler_params=params,
        cost_estimate=pl.CostEstimate(flops=4_000_000, bytes_accessed=2_000_000, transcendentals=0),
        name="values_part",
    )(slots, halves, lengths, *flat(values), early, taps, *prepared)


def swap(value, bit, devices):
    return lax.ppermute(value, "heads", [(i, i ^ bit) for i in range(devices)])


def on_device(
    tokens,
    qkv_weight,
    gate_weight,
    conv_weight,
    delta_state,
    conv_state,
    old_heads,
    new_units,
    slot_of,
    lengths,
):
    devices = lax.axis_size("heads")
    me = lax.axis_index("heads")
    per_device = UNITS // devices
    depth = qkv_weight.shape[0]
    row_count = tokens.shape[0]
    chips = devices // 2

    old_slots, halves = unit_tables(old_heads, new_units)
    bits = [1 << b for b in range(1, devices.bit_length() - 1)]
    order = []
    for place in range(chips):
        offset = 0
        for at, bit in enumerate(bits):
            if place & (chips >> (at + 1)):
                offset |= bit
        order.append(offset)
    holders = jnp.bitwise_xor(jnp.asarray(order, jnp.int32), me)
    old_rows = (holders[:, None] * LOCAL + jnp.arange(LOCAL, dtype=jnp.int32)[None, :]).reshape(-1)
    flat_tokens = tokens.reshape(row_count * STEPS, D)
    steps = jnp.arange(STEPS, dtype=jnp.int32)
    wanted = (old_rows[:, None] * STEPS + steps[None, :]).reshape(-1)
    offered = (slot_of[:, None] * STEPS + steps[None, :]).reshape(-1)
    picker = (wanted[:, None] == offered[None, :]).astype(jnp.bfloat16)

    def token_part(owner):
        columns = lax.dynamic_slice_in_dim(flat_tokens, owner * depth, depth, 1)
        return jnp.dot(picker, columns, preferred_element_type=jnp.float32).astype(jnp.bfloat16)

    mine, theirs = token_part(me), token_part(jnp.bitwise_xor(me, 1))
    half_rows = chips * ROWS // 2

    width = HEADS_WIDTH // PIECES
    chunks, others = [], []
    weight = qkv_weight
    for part in (1, 0, 2):
        for piece in range(PIECES):
            begin = part * HEADS_WIDTH + piece * width
            block = weight[:, begin : begin + width]
            if not chunks:
                block = jnp.concatenate([block, gate_weight], axis=1)
            block, weight = lax.optimization_barrier((block, weight))
            chunks.append(block)
            others.append(swap(block, 1, devices))

    pieces = []
    for block, other in zip(chunks, others):
        total = jnp.dot(mine, block, preferred_element_type=jnp.float32)
        total = total + jnp.dot(theirs, other, preferred_element_type=jnp.float32)
        for bit in bits[:-1]:
            half = total.shape[0] // 2
            total = total[:half] + swap(total[half:], bit, devices)
        pieces.append((total, swap(total[ROWS:], bits[-1], devices)))
    keys, queries, values = (pieces[i * PIECES : (i + 1) * PIECES] for i in range(3))

    gathered = conv_weight[None]
    for b in range(devices.bit_length() - 1):
        gathered = jnp.concatenate([gathered, swap(gathered, 1 << b, devices)], axis=0)
    places = jnp.arange(devices, dtype=jnp.int32)
    sorter = (jnp.bitwise_xor(places, me)[:, None] == places[None, :]).astype(jnp.bfloat16)
    taps = jnp.einsum("aj,jtc->tac", sorter, gathered, preferred_element_type=jnp.float32)
    taps = taps.astype(jnp.bfloat16).reshape(TAPS, 3 * HEADS_WIDTH)
    taps_f = taps.astype(jnp.float32)
    early = []
    for step in range(STEPS):
        term = jnp.zeros_like(conv_state[:, 0])
        for tap in range(TAPS - 1 - step):
            term = term + taps_f[tap][None] * conv_state[:, step + tap]
        early.append(term)
    early = jnp.stack(early, axis=1).reshape(ROWS, 3 * HEADS_WIDTH)

    my_rows = me * LOCAL + jnp.arange(LOCAL, dtype=jnp.int32)
    my_lengths = jnp.sum(
        jnp.where(slot_of[None, :] == my_rows[:, None], lengths[None, :], 0), axis=1
    )
    local_out = run_delta(
        old_slots, halves, my_lengths, keys, queries, values, early, taps, delta_state
    )

    placer = (offered[:, None] == jnp.arange(row_count * STEPS, dtype=jnp.int32)[None, :]).astype(
        jnp.bfloat16
    )
    if per_device % 2 == 0:
        pairs = per_device // 2
        sending = local_out.reshape(devices, pairs * ROWS, DK)
        got = lax.all_to_all(sending, "heads", split_axis=0, concat_axis=0, tiled=True)
        got = got.reshape(devices, pairs, ROWS, DK)
        got = jnp.concatenate([got[:, pair] for pair in range(pairs)], axis=-1)
        got = got.reshape(devices * ROWS, pairs * DK)
    else:
        units = local_out.reshape(UNITS // 2, ROWS, 2, HALF).transpose(0, 2, 1, 3)
        sending = units.reshape(devices, per_device * ROWS, HALF)
        got = lax.all_to_all(sending, "heads", split_axis=0, concat_axis=0, tiled=True)
        got = got.reshape(devices, per_device, ROWS, HALF).transpose(0, 2, 1, 3)
        got = got.reshape(devices * ROWS, per_device * HALF)
    outputs = jnp.dot(placer, got, preferred_element_type=jnp.float32).astype(jnp.bfloat16)
    return outputs.reshape(row_count, STEPS, per_device * HALF)


def solution(mesh):
    in_specs = (
        P("groups", None, None),
        P(("groups", "heads"), None),
        P(("groups", "heads"), None),
        P("groups", "heads"),
        P(("groups", "heads"), None, None, None),
        P(("groups", "heads"), None, None),
        P(),
        P(),
        P("groups"),
        P("groups"),
    )
    out_specs = P("groups", None, "heads")
    return jax.shard_map(
        on_device, mesh=mesh, in_specs=in_specs, out_specs=out_specs, check_vma=False
    )
```

time: 124 us -> 122 us (0.984)
  starting transfers between devices: 6.93 us -> 36.5 us
  blocking collectives: 32.4 us -> 11.3 us
  waiting for transfers between devices: 44.7 us -> 33.4 us
  Pallas kernels: 6.71 us -> 4.7 us
  local copies, waits for them, and re-layouts: 10.8 us -> 12.7 us
  other arithmetic: 3.71 us -> 5.4 us
    ppermute x12 -> x28, starting transfers between devices: 6.93 us -> 36.5 us  [swap(): return lax.ppermute(value, 'heads', [(i, i ^ bit) for i in range(devices)])]
    all_gather x1 -> x0, blocking collectives: 22.9 us -> none  [on_device(): taps = lax.all_gather(conv_weight, 'heads', axis=1, tiled=True)]
    ppermute x12 -> x28, waiting for transfers between devices: 44.7 us -> 33.4 us  [swap(): return lax.ppermute(value, 'heads', [(i, i ^ bit) for i in range(devices)])]
    unnamed x43 -> x48, local copies, waits for them, and re-layouts: 1.84 us -> 4.55 us
    concatenate x0 -> x3, other arithmetic: none -> 2.26 us  [on_device(): jnp.concatenate([gathered, swap(gathered, 1 << b, devices)], axis=0)]
    reshape x1, local copies, waits for them, and re-layouts: 2.3 us -> 0.14 us  [on_device(): flat_tokens = tokens.reshape(row_count * STEPS, D)]
    pallas_call x1 -> x2, Pallas kernels: 6.71 us -> 4.7 us  [the longest x1 3.65 us: run_delta(): pl.pallas_call(keys_kernel, out_shape=[per_head] * 3 + lags, in_specs=[vm...]
    all_to_all x1, blocking collectives: 9.59 us -> 11.3 us  [on_device(): lax.all_to_all(sending, 'heads', split_axis=0, concat_axis=0, tiled=True)]
  transfers between devices with their start and end apart: 12 -> 28, of which waited for: 7 -> 13; matrix products, arithmetic and copies ran while one was open for 21% -> 19% of each run, Pallas kernels for 0% -> 3%
where the time goes in v2:
time: 122 us
  starting transfers between devices  36.5 us (30%)
  waiting for transfers between devices  33.4 us (27%)
  matrix products  17.1 us (14%)
  local copies, waits for them, and re-layouts  12.7 us (10%)
  blocking collectives  11.3 us (9%)
  other arithmetic  5.4 us (4%)
  Pallas kernels  4.7 us (4%)
    ppermute x28, starting transfers between devices, swap(): return lax.ppermute(value, 'heads', [(i, i ^ bit) for i in range(devices)])  36.5 us
    ppermute x28, waiting for transfers between devices, swap(): return lax.ppermute(value, 'heads', [(i, i ^ bit) for i in range(devices)])  33.4 us
    all_to_all x1, blocking collectives, on_device(): lax.all_to_all(sending, 'heads', split_axis=0, concat_axis=0, tiled=True)  11.3 us
    dot_general x6, matrix products, on_device(): total = jnp.dot(mine, block, preferred_element_type=jnp.float32)  9.07 us
    dot_general x6, matrix products, on_device(): total = total + jnp.dot(theirs, other, preferred_element_type=jnp.float32)  5.63 us
    slice x7, local copies, waits for them, and re-layouts, on_device(): block = weight[:, begin:begin + width]  5.46 us
    unnamed x48, local copies, waits for them, and re-layouts  4.55 us
    pallas_call x1, Pallas kernels, run_delta(): pl.pallas_call(keys_kernel, out_shape=[per_head] * 3 + lags, in_specs=[vm...  3.65 us
  transfers between devices with their start and end apart: 28, of which 13 were waited for; matrix products, arithmetic and copies ran while one was open for 19% of the time, Pallas kernels for 3%

profile of v2, /device:TPU:0, one launch (start us, length us, event | category | flops | bytes accessed | tf_op | source)
XLA Modules:
  0.0 121.7 jit_solution(11517192183801512615)
XLA Ops:
  2.0 2.3 %slice.145 = bf16[144,2048]{1,0:T(8,128)(2,1)} slice(bf16[144,12288]{1,0:T(8,128)(2,1)} %param.12), slice={[0:144], [6144:8192]} | slice | bytes 1179648 | tf_op jit(solution)/shard_map/slice | solution.py:228
  4.3 2.0 %slice.146 = bf16[144,2048]{1,0:T(8,128)(2,1)} slice(bf16[144,12288]{1,0:T(8,128)(2,1)} %param.12), slice={[0:144], [0:2048]} | slice | bytes 1179648 | tf_op jit(solution)/shard_map/slice | solution.py:228
  10.3 2.2 %fusion.26 = f32[64,2048]{1,0:T(8,128)} fusion(bf16[64,144]{1,0:T(8,128)(2,1)S(1)} %convolution_convert_fusion.3, bf16[144,2048]{1,0:T(8,128)(2,1)} %slice.147), kind=kOutput, calls=%fused_computation.76 | convolution fusion | flops 37748736 | bytes 1132544 | tf_op jit(solution)/shard_map/dot_general | solution.py:237
  12.4 2.3 %fusion.25 = f32[64,2048]{1,0:T(8,128)} fusion(bf16[64,144]{1,0:T(8,128)(2,1)S(1)} %convolution_convert_fusion.3, bf16[144,2048]{1,0:T(8,128)(2,1)} %slice.146), kind=kOutput, calls=%fused_computation.75 | convolution fusion | flops 37748736 | bytes 1132544 | tf_op jit(solution)/shard_map/dot_general | solution.py:237
  14.7 2.1 %fusion.24 = f32[64,2048]{1,0:T(8,128)} fusion(bf16[64,144]{1,0:T(8,128)(2,1)S(1)} %convolution_convert_fusion.3, bf16[144,2048]{1,0:T(8,128)(2,1)} %slice.145), kind=kOutput, calls=%fused_computation.74 | convolution fusion | flops 37748736 | bytes 1132544 | tf_op jit(solution)/shard_map/dot_general | solution.py:237
  16.8 2.1 %fusion.23 = f32[64,2112]{1,0:T(8,128)} fusion(bf16[64,144]{1,0:T(8,128)(2,1)S(1)} %convolution_convert_fusion.3, bf16[144,2112]{1,0:T(8,128)(2,1)} %pad_maximum_fusion), kind=kOutput, calls=%fused_computation.73 | convolution fusion | flops 38928384 | bytes 1167360 | tf_op jit(solution)/shard_map/dot_general | solution.py:237
  23.0 2.6 %collective-permute-start.9 = (bf16[2,4,768]{2,0,1:T(2,128)(2,1)S(1)}, bf16[2,4,768]{2,0,1:T(2,128)(2,1)S(1)}, u32[]{:S(2)}, u32[]{:S(2)}) collective-permute-start(bf16[2,4,768]{2,0,1:T(2,128)(2,1)S(1)} %pad_maximum_fusion.3), channel_id=1, source_target_pairs={{0,2},{1,3},{2,0},{3,1},{4,6},{5,7},{6,4},{7,5},{8,10},{9,11},{10,... | collective-permute-start | bytes 36872 | tf_op jit(solution)/shard_map/ppermute | solution.py:176
  28.0 2.1 %collective-permute-start.10 = (bf16[4,4,768]{2,0,1:T(4,128)(2,1)S(1)}, bf16[4,4,768]{2,0,1:T(4,128)(2,1)S(1)}, u32[]{:S(2)}, u32[]{:S(2)}) collective-permute-start(bf16[4,4,768]{2,0,1:T(4,128)(2,1)S(1)} %pad_maximum_fusion.2), channel_id=1, source_target_pairs={{0,4},{1,5},{2,6},{3,7},{4,0},{5,1},{6,2},{7,3},{8,12},{9,13},{10,... | collective-permute-start | bytes 73736 | tf_op jit(solution)/shard_map/ppermute | solution.py:176
  30.2 1.7 %collective-permute-done.10 = bf16[4,4,768]{2,0,1:T(4,128)(2,1)S(1)} collective-permute-done((bf16[4,4,768]{2,0,1:T(4,128)(2,1)S(1)}, bf16[4,4,768]{2,0,1:T(4,128)(2,1)S(1)}, u32[]{:S(2)}, u32[]{:S(2)}) %collective-permute-start.10) | collective-permute-done | bytes 24608 | tf_op jit(solution)/shard_map/ppermute | solution.py:176
  32.7 3.1 %collective-permute-start.11 = (bf16[8,4,768]{2,0,1:T(8,128)(2,1)S(1)}, bf16[8,4,768]{2,0,1:T(8,128)(2,1)S(1)}, u32[]{:S(2)}, u32[]{:S(2)}) collective-permute-start(bf16[8,4,768]{2,0,1:T(8,128)(2,1)S(1)} %pad_maximum_fusion.1), channel_id=1, source_target_pairs={{0,8},{1,9},{2,10},{3,11},{4,12},{5,13},{6,14},{7,15},{8,0},{9,1},... | collective-permute-start | bytes 147464 | tf_op jit(solution)/shard_map/ppermute | solution.py:176
  35.9 2.0 %collective-permute-done.11 = bf16[8,4,768]{2,0,1:T(8,128)(2,1)S(1)} collective-permute-done((bf16[8,4,768]{2,0,1:T(8,128)(2,1)S(1)}, bf16[8,4,768]{2,0,1:T(8,128)(2,1)S(1)}, u32[]{:S(2)}, u32[]{:S(2)}) %collective-permute-start.11) | collective-permute-done | bytes 49184 | tf_op jit(solution)/shard_map/ppermute | solution.py:176
  42.2 1.9 %collective-permute-start.25 = (f32[32,2048]{1,0:T(8,128)S(1)}, f32[32,2048]{1,0:T(8,128)S(1)}, u32[]{:S(2)}, u32[]{:S(2)}) collective-permute-start(f32[32,2048]{1,0:T(8,128)S(1)} %slice.220), channel_id=1, source_target_pairs={{0,2},{1,3},{2,0},{3,1},{4,6},{5,7},{6,4},{7,5},{8,10},{9,11},{10,... | collective-permute-start | bytes 786440 | tf_op jit(solution)/shard_map/ppermute | solution.py:176
  47.0 1.9 %collective-permute-start.17 = (f32[32,2048]{1,0:T(8,128)S(1)}, f32[32,2048]{1,0:T(8,128)S(1)}, u32[]{:S(2)}, u32[]{:S(2)}) collective-permute-start(f32[32,2048]{1,0:T(8,128)S(1)} %slice.210), channel_id=1, source_target_pairs={{0,2},{1,3},{2,0},{3,1},{4,6},{5,7},{6,4},{7,5},{8,10},{9,11},{10,... | collective-permute-start | bytes 786440 | tf_op jit(solution)/shard_map/ppermute | solution.py:176
  49.7 1.9 %collective-permute-start.1 = (f32[32,2048]{1,0:T(8,128)S(1)}, f32[32,2048]{1,0:T(8,128)S(1)}, u32[]{:S(2)}, u32[]{:S(2)}) collective-permute-start(f32[32,2048]{1,0:T(8,128)S(1)} %slice.192), channel_id=1, source_target_pairs={{0,2},{1,3},{2,0},{3,1},{4,6},{5,7},{6,4},{7,5},{8,10},{9,11},{10,... | collective-permute-start | bytes 786440 | tf_op jit(solution)/shard_map/ppermute | solution.py:176
  53.3 3.7 %collective-permute-done.21 = f32[32,2048]{1,0:T(8,128)S(1)} collective-permute-done((f32[32,2048]{1,0:T(8,128)S(1)}, f32[32,2048]{1,0:T(8,128)S(1)}, u32[]{:S(2)}, u32[]{:S(2)}) %collective-permute-start.21) | collective-permute-done | bytes 262176 | tf_op jit(solution)/shard_map/ppermute | solution.py:176
  57.0 1.9 %collective-permute-start.26 = (f32[16,2048]{1,0:T(8,128)S(1)}, f32[16,2048]{1,0:T(8,128)S(1)}, u32[]{:S(2)}, u32[]{:S(2)}) collective-permute-start(f32[16,2048]{1,0:T(8,128)S(1)} %slice.222), channel_id=1, source_target_pairs={{0,4},{1,5},{2,6},{3,7},{4,0},{5,1},{6,2},{7,3},{8,12},{9,13},{10,... | collective-permute-start | bytes 393224 | tf_op jit(solution)/shard_map/ppermute | solution.py:176
  59.0 3.6 %collective-permute-done.17 = f32[32,2048]{1,0:T(8,128)S(1)} collective-permute-done((f32[32,2048]{1,0:T(8,128)S(1)}, f32[32,2048]{1,0:T(8,128)S(1)}, u32[]{:S(2)}, u32[]{:S(2)}) %collective-permute-start.17) | collective-permute-done | bytes 262176 | tf_op jit(solution)/shard_map/ppermute | solution.py:176
  62.6 1.9 %collective-permute-start.22 = (f32[16,2048]{1,0:T(8,128)S(1)}, f32[16,2048]{1,0:T(8,128)S(1)}, u32[]{:S(2)}, u32[]{:S(2)}) collective-permute-start(f32[16,2048]{1,0:T(8,128)S(1)} %slice.217), channel_id=1, source_target_pairs={{0,4},{1,5},{2,6},{3,7},{4,0},{5,1},{6,2},{7,3},{8,12},{9,13},{10,... | collective-permute-start | bytes 393224 | tf_op jit(solution)/shard_map/ppermute | solution.py:176
  64.6 3.6 %collective-permute-done.5 = f32[32,2048]{1,0:T(8,128)S(1)} collective-permute-done((f32[32,2048]{1,0:T(8,128)S(1)}, f32[32,2048]{1,0:T(8,128)S(1)}, u32[]{:S(2)}, u32[]{:S(2)}) %collective-permute-start.5) | collective-permute-done | bytes 262176 | tf_op jit(solution)/shard_map/ppermute | solution.py:176
  68.2 1.9 %collective-permute-start.18 = (f32[16,2048]{1,0:T(8,128)S(1)}, f32[16,2048]{1,0:T(8,128)S(1)}, u32[]{:S(2)}, u32[]{:S(2)}) collective-permute-start(f32[16,2048]{1,0:T(8,128)S(1)} %slice.212), channel_id=1, source_target_pairs={{0,4},{1,5},{2,6},{3,7},{4,0},{5,1},{6,2},{7,3},{8,12},{9,13},{10,... | collective-permute-start | bytes 393224 | tf_op jit(solution)/shard_map/ppermute | solution.py:176
  70.2 3.6 %collective-permute-done.1 = f32[32,2048]{1,0:T(8,128)S(1)} collective-permute-done((f32[32,2048]{1,0:T(8,128)S(1)}, f32[32,2048]{1,0:T(8,128)S(1)}, u32[]{:S(2)}, u32[]{:S(2)}) %collective-permute-start.1) | collective-permute-done | bytes 262176 | tf_op jit(solution)/shard_map/ppermute | solution.py:176
  73.9 1.9 %collective-permute-start.6 = (f32[16,2048]{1,0:T(8,128)S(1)}, f32[16,2048]{1,0:T(8,128)S(1)}, u32[]{:S(2)}, u32[]{:S(2)}) collective-permute-start(f32[16,2048]{1,0:T(8,128)S(1)} %slice.199), channel_id=1, source_target_pairs={{0,4},{1,5},{2,6},{3,7},{4,0},{5,1},{6,2},{7,3},{8,12},{9,13},{10,... | collective-permute-start | bytes 393224 | tf_op jit(solution)/shard_map/ppermute | solution.py:176
  75.8 3.2 %collective-permute-done.13 = f32[32,2112]{1,0:T(8,128)S(1)} collective-permute-done((f32[32,2112]{1,0:T(8,128)S(1)}, f32[32,2112]{1,0:T(8,128)S(1)}, u32[]{:S(2)}, u32[]{:S(2)}) %collective-permute-start.13) | collective-permute-done | bytes 270368 | tf_op jit(solution)/shard_map/ppermute | solution.py:176
  79.1 1.8 %collective-permute-start.2 = (f32[16,2048]{1,0:T(8,128)S(1)}, f32[16,2048]{1,0:T(8,128)S(1)}, u32[]{:S(2)}, u32[]{:S(2)}) collective-permute-start(f32[16,2048]{1,0:T(8,128)S(1)} %slice.194), channel_id=1, source_target_pairs={{0,4},{1,5},{2,6},{3,7},{4,0},{5,1},{6,2},{7,3},{8,12},{9,13},{10,... | collective-permute-start | bytes 393224 | tf_op jit(solution)/shard_map/ppermute | solution.py:176
  81.3 2.9 %collective-permute-start.27 = (f32[8,2048]{1,0:T(8,128)S(1)}, f32[8,2048]{1,0:T(8,128)S(1)}, u32[]{:S(2)}, u32[]{:S(2)}) collective-permute-start(f32[8,2048]{1,0:T(8,128)S(1)} %slice.223), channel_id=1, source_target_pairs={{0,8},{1,9},{2,10},{3,11},{4,12},{5,13},{6,14},{7,15},{8,0},{9,1},... | collective-permute-start | bytes 196616 | tf_op jit(solution)/shard_map/ppermute | solution.py:176
  84.4 2.9 %collective-permute-start.19 = (f32[8,2048]{1,0:T(8,128)S(1)}, f32[8,2048]{1,0:T(8,128)S(1)}, u32[]{:S(2)}, u32[]{:S(2)}) collective-permute-start(f32[8,2048]{1,0:T(8,128)S(1)} %slice.213), channel_id=1, source_target_pairs={{0,8},{1,9},{2,10},{3,11},{4,12},{5,13},{6,14},{7,15},{8,0},{9,1},... | collective-permute-start | bytes 196616 | tf_op jit(solution)/shard_map/ppermute | solution.py:176
  91.6 2.2 %collective-permute-start.15 = (f32[8,2112]{1,0:T(8,128)S(1)}, f32[8,2112]{1,0:T(8,128)S(1)}, u32[]{:S(2)}, u32[]{:S(2)}) collective-permute-start(f32[8,2112]{1,0:T(8,128)S(1)} %slice.208), channel_id=1, source_target_pairs={{0,8},{1,9},{2,10},{3,11},{4,12},{5,13},{6,14},{7,15},{8,0},{9,1},... | collective-permute-start | bytes 202760 | tf_op jit(solution)/shard_map/ppermute | solution.py:176
  94.3 3.1 %collective-permute-done.23.refs_5_ = f32[8,2048]{1,0:T(8,128)S(1)} collective-permute-done((f32[8,2048]{1,0:T(8,128)S(1)}, f32[8,2048]{1,0:T(8,128)S(1)}, u32[]{:S(2)}, u32[]{:S(2)}) %collective-permute-start.23) | collective-permute-done | bytes 65568 | tf_op jit(solution)/shard_map/ppermute | solution.py:176
  98.8 3.8 %collective-permute-done.15.refs_1_ = f32[8,2112]{1,0:T(8,128)S(1)} collective-permute-done((f32[8,2112]{1,0:T(8,128)S(1)}, f32[8,2112]{1,0:T(8,128)S(1)}, u32[]{:S(2)}, u32[]{:S(2)}) %collective-permute-start.15) | collective-permute-done | bytes 67616 | tf_op jit(solution)/shard_map/ppermute | solution.py:176
  102.6 2.2 %copy-done = f32[2,32,128,128]{3,2,1,0:T(8,128)S(1)} copy-done((f32[2,32,128,128]{3,2,1,0:T(8,128)S(1)}, f32[2,32,128,128]{3,2,1,0:T(8,128)}, u32[]{:S(2)}) %copy-start) | copy-done | bytes 4194328
  104.8 3.6 %keys_part.1 = (f32[32,8,128]{2,1,0:T(8,128)S(1)}, f32[32,8,128]{2,1,0:T(8,128)S(1)}, f32[32,8,128]{2,1,0:T(8,128)S(1)}, f32[3,32,8,128]{3,2,1,0:T(8,128)S(1)}, f32[4,32,8,128]{3,2,1,0:T(8,128)S(1)}) custom-call(f32[16,2112]{1,0:T(8,128)S(1)} %slice_add_fusion.6.refs_0_, f32[8,2112]{1,0:T(8,128)S(1)} %collective-permute-done.15.refs_1_, ...), custom_call_target="tpu_custom_call" | custom-call | flops 40000000 | bytes 9000000 | tf_op jit(solution)/shard_map/keys_part/pallas_call | solution.py:154
  109.5 11.3 %all_to_all.5 = bf16[16,16,128]{2,1,0:T(8,128)(2,1)S(1)} all-to-all(bf16[16,16,128]{2,1,0:T(8,128)(2,1)S(1)} %values_part.1), channel_id=1, replica_groups=mesh['groups'=2,'heads'=16] {'heads'}, dimensions={0} | all-to-all | bytes 131072 | tf_op jit(solution)/shard_map/all_to_all | solution.py:275
  (157 shorter events, 31.4 us)
Async XLA Ops:
  7.2 33.0 %collective-permute-start.24 = (bf16[144,2048]{1,0:T(8,128)(2,1)}, bf16[144,2048]{1,0:T(8,128)(2,1)}, u32[]{:S(2)}, u32[]{:S(2)}) collective-permute-start(bf16[144,2048]{1,0:T(8,128)(2,1)} %slice.147), channel_id=1, source_target_pairs={{0,1},{1,0},{2,3},{3,2},{4,5},{5,4},{6,7},{7,6},{8,9},{9,8},{10,11... | collective-permute-start | bytes 1769480 | tf_op jit(solution)/shard_map/ppermute | solution.py:176
  7.7 34.5 %collective-permute-start.20 = (bf16[144,2048]{1,0:T(8,128)(2,1)}, bf16[144,2048]{1,0:T(8,128)(2,1)}, u32[]{:S(2)}, u32[]{:S(2)}) collective-permute-start(bf16[144,2048]{1,0:T(8,128)(2,1)} %slice.146), channel_id=1, source_target_pairs={{0,1},{1,0},{2,3},{3,2},{4,5},{5,4},{6,7},{7,6},{8,9},{9,8},{10,11... | collective-permute-start | bytes 1769480 | tf_op jit(solution)/shard_map/ppermute | solution.py:176
  7.7 37.7 %collective-permute-start.16 = (bf16[144,2048]{1,0:T(8,128)(2,1)}, bf16[144,2048]{1,0:T(8,128)(2,1)}, u32[]{:S(2)}, u32[]{:S(2)}) collective-permute-start(bf16[144,2048]{1,0:T(8,128)(2,1)} %slice.145), channel_id=1, source_target_pairs={{0,1},{1,0},{2,3},{3,2},{4,5},{5,4},{6,7},{7,6},{8,9},{9,8},{10,11... | collective-permute-start | bytes 1769480 | tf_op jit(solution)/shard_map/ppermute | solution.py:176
  8.2 41.5 %collective-permute-start.12 = (bf16[144,2112]{1,0:T(8,128)(2,1)}, bf16[144,2112]{1,0:T(8,128)(2,1)}, u32[]{:S(2)}, u32[]{:S(2)}) collective-permute-start(bf16[144,2112]{1,0:T(8,128)(2,1)} %pad_maximum_fusion), channel_id=1, source_target_pairs={{0,1},{1,0},{2,3},{3,2},{4,5},{5,4},{6,7},{7,6},{8,9},{9,8},{10,11... | collective-permute-start | bytes 1824776 | tf_op jit(solution)/shard_map/ppermute | solution.py:176
  8.2 14.0 %collective-permute-start.8 = (bf16[1,4,768]{2,0,1:T(2,128)(2,1)S(1)}, bf16[1,4,768]{2,0,1:T(2,128)(2,1)}, u32[]{:S(2)}, u32[]{:S(2)}) collective-permute-start(bf16[1,4,768]{2,0,1:T(2,128)(2,1)S(1)} %copy.26), channel_id=1, source_target_pairs={{0,1},{1,0},{2,3},{3,2},{4,5},{5,4},{6,7},{7,6},{8,9},{9,8},{10,11... | collective-permute-start | bytes 18440 | tf_op jit(solution)/shard_map/ppermute | solution.py:176
  12.4 8.2 %copy-start.2 = (bf16[144,12288]{1,0:T(8,128)(2,1)S(1)}, bf16[144,12288]{1,0:T(8,128)(2,1)}, u32[]{:S(2)}) copy-start(bf16[144,12288]{1,0:T(8,128)(2,1)} %param.12) | copy-start | bytes 10616836
  21.7 19.1 %copy-start.9 = (f32[64,2048]{1,0:T(8,128)S(1)}, f32[64,2048]{1,0:T(8,128)}, u32[]{:S(2)}) copy-start(f32[64,2048]{1,0:T(8,128)} %fusion.26) | copy-start | bytes 1572868
  21.7 19.1 %copy-start.10 = (bf16[64,144]{1,0:T(8,128)(2,1)S(1)}, bf16[64,144]{1,0:T(8,128)(2,1)}, u32[]{:S(2)}) copy-start(bf16[64,144]{1,0:T(8,128)(2,1)} %convolution_convert_fusion.2) | copy-start | bytes 55300
  22.0 18.3 %copy-start.4 = (bf16[144,2048]{1,0:T(8,128)(2,1)S(1)}, bf16[144,2048]{1,0:T(8,128)(2,1)}, u32[]{:S(2)}) copy-start(bf16[144,2048]{1,0:T(8,128)(2,1)} %copy-done.3) | copy-start | bytes 1769476
  23.0 4.3 %collective-permute-start.9 = (bf16[2,4,768]{2,0,1:T(2,128)(2,1)S(1)}, bf16[2,4,768]{2,0,1:T(2,128)(2,1)S(1)}, u32[]{:S(2)}, u32[]{:S(2)}) collective-permute-start(bf16[2,4,768]{2,0,1:T(2,128)(2,1)S(1)} %pad_maximum_fusion.3), channel_id=1, source_target_pairs={{0,2},{1,3},{2,0},{3,1},{4,6},{5,7},{6,4},{7,5},{8,10},{9,11},{10,... | collective-permute-start | bytes 36872 | tf_op jit(solution)/shard_map/ppermute | solution.py:176
  28.0 3.9 %collective-permute-start.10 = (bf16[4,4,768]{2,0,1:T(4,128)(2,1)S(1)}, bf16[4,4,768]{2,0,1:T(4,128)(2,1)S(1)}, u32[]{:S(2)}, u32[]{:S(2)}) collective-permute-start(bf16[4,4,768]{2,0,1:T(4,128)(2,1)S(1)} %pad_maximum_fusion.2), channel_id=1, source_target_pairs={{0,4},{1,5},{2,6},{3,7},{4,0},{5,1},{6,2},{7,3},{8,12},{9,13},{10,... | collective-permute-start | bytes 73736 | tf_op jit(solution)/shard_map/ppermute | solution.py:176
  32.7 5.2 %collective-permute-start.11 = (bf16[8,4,768]{2,0,1:T(8,128)(2,1)S(1)}, bf16[8,4,768]{2,0,1:T(8,128)(2,1)S(1)}, u32[]{:S(2)}, u32[]{:S(2)}) collective-permute-start(bf16[8,4,768]{2,0,1:T(8,128)(2,1)S(1)} %pad_maximum_fusion.1), channel_id=1, source_target_pairs={{0,8},{1,9},{2,10},{3,11},{4,12},{5,13},{6,14},{7,15},{8,0},{9,1},... | collective-permute-start | bytes 147464 | tf_op jit(solution)/shard_map/ppermute | solution.py:176
  37.9 9.1 %collective-permute-start.4 = (bf16[144,2048]{1,0:T(8,128)(2,1)}, bf16[144,2048]{1,0:T(8,128)(2,1)S(1)}, u32[]{:S(2)}, u32[]{:S(2)}) collective-permute-start(bf16[144,2048]{1,0:T(8,128)(2,1)} %copy-done.5), channel_id=1, source_target_pairs={{0,1},{1,0},{2,3},{3,2},{4,5},{5,4},{6,7},{7,6},{8,9},{9,8},{10,11... | collective-permute-start | bytes 1769480 | tf_op jit(solution)/shard_map/ppermute | solution.py:176
  40.3 8.9 %collective-permute-start = (bf16[144,2048]{1,0:T(8,128)(2,1)S(1)}, bf16[144,2048]{1,0:T(8,128)(2,1)S(1)}, u32[]{:S(2)}, u32[]{:S(2)}) collective-permute-start(bf16[144,2048]{1,0:T(8,128)(2,1)S(1)} %copy-done.4), channel_id=1, source_target_pairs={{0,1},{1,0},{2,3},{3,2},{4,5},{5,4},{6,7},{7,6},{8,9},{9,8},{10,11... | collective-permute-start | bytes 1769480 | tf_op jit(solution)/shard_map/ppermute | solution.py:176
  42.2 10.8 %collective-permute-start.25 = (f32[32,2048]{1,0:T(8,128)S(1)}, f32[32,2048]{1,0:T(8,128)S(1)}, u32[]{:S(2)}, u32[]{:S(2)}) collective-permute-start(f32[32,2048]{1,0:T(8,128)S(1)} %slice.220), channel_id=1, source_target_pairs={{0,2},{1,3},{2,0},{3,1},{4,6},{5,7},{6,4},{7,5},{8,10},{9,11},{10,... | collective-permute-start | bytes 786440 | tf_op jit(solution)/shard_map/ppermute | solution.py:176
  45.4 11.6 %collective-permute-start.21 = (f32[32,2048]{1,0:T(8,128)S(1)}, f32[32,2048]{1,0:T(8,128)S(1)}, u32[]{:S(2)}, u32[]{:S(2)}) collective-permute-start(f32[32,2048]{1,0:T(8,128)S(1)} %slice.215), channel_id=1, source_target_pairs={{0,2},{1,3},{2,0},{3,1},{4,6},{5,7},{6,4},{7,5},{8,10},{9,11},{10,... | collective-permute-start | bytes 786440 | tf_op jit(solution)/shard_map/ppermute | solution.py:176
  47.0 15.6 %collective-permute-start.17 = (f32[32,2048]{1,0:T(8,128)S(1)}, f32[32,2048]{1,0:T(8,128)S(1)}, u32[]{:S(2)}, u32[]{:S(2)}) collective-permute-start(f32[32,2048]{1,0:T(8,128)S(1)} %slice.210), channel_id=1, source_target_pairs={{0,2},{1,3},{2,0},{3,1},{4,6},{5,7},{6,4},{7,5},{8,10},{9,11},{10,... | collective-permute-start | bytes 786440 | tf_op jit(solution)/shard_map/ppermute | solution.py:176
  49.2 19.0 %collective-permute-start.5 = (f32[32,2048]{1,0:T(8,128)S(1)}, f32[32,2048]{1,0:T(8,128)S(1)}, u32[]{:S(2)}, u32[]{:S(2)}) collective-permute-start(f32[32,2048]{1,0:T(8,128)S(1)} %slice.197), channel_id=1, source_target_pairs={{0,2},{1,3},{2,0},{3,1},{4,6},{5,7},{6,4},{7,5},{8,10},{9,11},{10,... | collective-permute-start | bytes 786440 | tf_op jit(solution)/shard_map/ppermute | solution.py:176
  49.7 24.1 %collective-permute-start.1 = (f32[32,2048]{1,0:T(8,128)S(1)}, f32[32,2048]{1,0:T(8,128)S(1)}, u32[]{:S(2)}, u32[]{:S(2)}) collective-permute-start(f32[32,2048]{1,0:T(8,128)S(1)} %slice.192), channel_id=1, source_target_pairs={{0,2},{1,3},{2,0},{3,1},{4,6},{5,7},{6,4},{7,5},{8,10},{9,11},{10,... | collective-permute-start | bytes 786440 | tf_op jit(solution)/shard_map/ppermute | solution.py:176
  53.0 26.1 %collective-permute-start.13 = (f32[32,2112]{1,0:T(8,128)S(1)}, f32[32,2112]{1,0:T(8,128)S(1)}, u32[]{:S(2)}, u32[]{:S(2)}) collective-permute-start(f32[32,2112]{1,0:T(8,128)S(1)} %slice.205), channel_id=1, source_target_pairs={{0,2},{1,3},{2,0},{3,1},{4,6},{5,7},{6,4},{7,5},{8,10},{9,11},{10,... | collective-permute-start | bytes 811016 | tf_op jit(solution)/shard_map/ppermute | solution.py:176
  57.0 23.9 %collective-permute-start.26 = (f32[16,2048]{1,0:T(8,128)S(1)}, f32[16,2048]{1,0:T(8,128)S(1)}, u32[]{:S(2)}, u32[]{:S(2)}) collective-permute-start(f32[16,2048]{1,0:T(8,128)S(1)} %slice.222), channel_id=1, source_target_pairs={{0,4},{1,5},{2,6},{3,7},{4,0},{5,1},{6,2},{7,3},{8,12},{9,13},{10,... | collective-permute-start | bytes 393224 | tf_op jit(solution)/shard_map/ppermute | solution.py:176
  62.6 18.6 %collective-permute-start.22 = (f32[16,2048]{1,0:T(8,128)S(1)}, f32[16,2048]{1,0:T(8,128)S(1)}, u32[]{:S(2)}, u32[]{:S(2)}) collective-permute-start(f32[16,2048]{1,0:T(8,128)S(1)} %slice.217), channel_id=1, source_target_pairs={{0,4},{1,5},{2,6},{3,7},{4,0},{5,1},{6,2},{7,3},{8,12},{9,13},{10,... | collective-permute-start | bytes 393224 | tf_op jit(solution)/shard_map/ppermute | solution.py:176
  68.2 16.0 %collective-permute-start.18 = (f32[16,2048]{1,0:T(8,128)S(1)}, f32[16,2048]{1,0:T(8,128)S(1)}, u32[]{:S(2)}, u32[]{:S(2)}) collective-permute-start(f32[16,2048]{1,0:T(8,128)S(1)} %slice.212), channel_id=1, source_target_pairs={{0,4},{1,5},{2,6},{3,7},{4,0},{5,1},{6,2},{7,3},{8,12},{9,13},{10,... | collective-permute-start | bytes 393224 | tf_op jit(solution)/shard_map/ppermute | solution.py:176
  73.9 10.6 %collective-permute-start.6 = (f32[16,2048]{1,0:T(8,128)S(1)}, f32[16,2048]{1,0:T(8,128)S(1)}, u32[]{:S(2)}, u32[]{:S(2)}) collective-permute-start(f32[16,2048]{1,0:T(8,128)S(1)} %slice.199), channel_id=1, source_target_pairs={{0,4},{1,5},{2,6},{3,7},{4,0},{5,1},{6,2},{7,3},{8,12},{9,13},{10,... | collective-permute-start | bytes 393224 | tf_op jit(solution)/shard_map/ppermute | solution.py:176
  79.1 9.2 %collective-permute-start.2 = (f32[16,2048]{1,0:T(8,128)S(1)}, f32[16,2048]{1,0:T(8,128)S(1)}, u32[]{:S(2)}, u32[]{:S(2)}) collective-permute-start(f32[16,2048]{1,0:T(8,128)S(1)} %slice.194), channel_id=1, source_target_pairs={{0,4},{1,5},{2,6},{3,7},{4,0},{5,1},{6,2},{7,3},{8,12},{9,13},{10,... | collective-permute-start | bytes 393224 | tf_op jit(solution)/shard_map/ppermute | solution.py:176
  80.9 9.8 %collective-permute-start.14 = (f32[16,2112]{1,0:T(8,128)S(1)}, f32[16,2112]{1,0:T(8,128)S(1)}, u32[]{:S(2)}, u32[]{:S(2)}) collective-permute-start(f32[16,2112]{1,0:T(8,128)S(1)} %slice.207), channel_id=1, source_target_pairs={{0,4},{1,5},{2,6},{3,7},{4,0},{5,1},{6,2},{7,3},{8,12},{9,13},{10,... | collective-permute-start | bytes 405512 | tf_op jit(solution)/shard_map/ppermute | solution.py:176
  81.3 10.3 %collective-permute-start.27 = (f32[8,2048]{1,0:T(8,128)S(1)}, f32[8,2048]{1,0:T(8,128)S(1)}, u32[]{:S(2)}, u32[]{:S(2)}) collective-permute-start(f32[8,2048]{1,0:T(8,128)S(1)} %slice.223), channel_id=1, source_target_pairs={{0,8},{1,9},{2,10},{3,11},{4,12},{5,13},{6,14},{7,15},{8,0},{9,1},... | collective-permute-start | bytes 196616 | tf_op jit(solution)/shard_map/ppermute | solution.py:176
  84.2 13.2 %collective-permute-start.23 = (f32[8,2048]{1,0:T(8,128)S(1)}, f32[8,2048]{1,0:T(8,128)S(1)}, u32[]{:S(2)}, u32[]{:S(2)}) collective-permute-start(f32[8,2048]{1,0:T(8,128)S(1)} %slice.218), channel_id=1, source_target_pairs={{0,8},{1,9},{2,10},{3,11},{4,12},{5,13},{6,14},{7,15},{8,0},{9,1},... | collective-permute-start | bytes 196616 | tf_op jit(solution)/shard_map/ppermute | solution.py:176
  84.4 14.4 %collective-permute-start.19 = (f32[8,2048]{1,0:T(8,128)S(1)}, f32[8,2048]{1,0:T(8,128)S(1)}, u32[]{:S(2)}, u32[]{:S(2)}) collective-permute-start(f32[8,2048]{1,0:T(8,128)S(1)} %slice.213), channel_id=1, source_target_pairs={{0,8},{1,9},{2,10},{3,11},{4,12},{5,13},{6,14},{7,15},{8,0},{9,1},... | collective-permute-start | bytes 196616 | tf_op jit(solution)/shard_map/ppermute | solution.py:176
  88.2 20.2 %collective-permute-start.7 = (f32[8,2048]{1,0:T(8,128)S(1)}, f32[8,2048]{1,0:T(8,128)S(1)}, u32[]{:S(2)}, u32[]{:S(2)}) collective-permute-start(f32[8,2048]{1,0:T(8,128)S(1)} %slice.200), channel_id=1, source_target_pairs={{0,8},{1,9},{2,10},{3,11},{4,12},{5,13},{6,14},{7,15},{8,0},{9,1},... | collective-permute-start | bytes 196616 | tf_op jit(solution)/shard_map/ppermute | solution.py:176
  90.7 17.7 %collective-permute-start.3 = (f32[8,2048]{1,0:T(8,128)S(1)}, f32[8,2048]{1,0:T(8,128)S(1)}, u32[]{:S(2)}, u32[]{:S(2)}) collective-permute-start(f32[8,2048]{1,0:T(8,128)S(1)} %slice.195), channel_id=1, source_target_pairs={{0,8},{1,9},{2,10},{3,11},{4,12},{5,13},{6,14},{7,15},{8,0},{9,1},... | collective-permute-start | bytes 196616 | tf_op jit(solution)/shard_map/ppermute | solution.py:176
  91.6 11.0 %collective-permute-start.15 = (f32[8,2112]{1,0:T(8,128)S(1)}, f32[8,2112]{1,0:T(8,128)S(1)}, u32[]{:S(2)}, u32[]{:S(2)}) collective-permute-start(f32[8,2112]{1,0:T(8,128)S(1)} %slice.208), channel_id=1, source_target_pairs={{0,8},{1,9},{2,10},{3,11},{4,12},{5,13},{6,14},{7,15},{8,0},{9,1},... | collective-permute-start | bytes 202760 | tf_op jit(solution)/shard_map/ppermute | solution.py:176
  (20 other events, 56.7 us)

commit v3 on v2

--- a/solution.py
+++ b/solution.py
@@ -17,7 +17,9 @@
 LOCAL = 2
 ROWS = LOCAL * STEPS
 HEADS_WIDTH = H * DK
-PIECES = 2
+KEY_WIDTHS = (1024, 3072)
+QUERY_WIDTHS = (4096,)
+VALUE_WIDTHS = (3072, 1024)
 
 norm_eps = 1e-06
 
@@ -51,9 +53,12 @@
 
 
 def activate(pieces, part, head, early_ref, taps_ref, row_step):
-    per_piece = H // len(pieces)
-    kept_ref, sent_ref = pieces[head // per_piece]
-    inner = pl.ds(head % per_piece * DK, DK)
+    begin = head * DK
+    for kept_ref, sent_ref, width in pieces:
+        if begin < width:
+            break
+        begin -= width
+    inner = pl.ds(begin, DK)
     fresh = kept_ref[:ROWS, inner] + sent_ref[:, inner]
     columns = pl.ds(part * HEADS_WIDTH + head * DK, DK)
     total = early_ref[:, columns]
@@ -63,16 +68,19 @@
     return total / (1.0 + jnp.exp(-total))
 
 
+def paired(refs, widths):
+    return [(refs[2 * i], refs[2 * i + 1], width) for i, width in enumerate(widths)]
+
+
 def keys_kernel(*refs):
-    ins, outs = refs[: 4 * PIECES + 3], refs[4 * PIECES + 3 :]
-    key_refs = [(ins[2 * i], ins[2 * i + 1]) for i in range(PIECES)]
-    query_refs = [(ins[2 * i], ins[2 * i + 1]) for i in range(PIECES, 2 * PIECES)]
-    early_ref, taps_ref, state_ref = ins[4 * PIECES :]
+    key_refs = paired(refs, KEY_WIDTHS)
+    query_refs = paired(refs[2 * len(KEY_WIDTHS) :], QUERY_WIDTHS)
+    rest = refs[2 * len(KEY_WIDTHS + QUERY_WIDTHS) :]
+    (early_ref, taps_ref, state_ref), outs = rest[:3], rest[3:]
     beta_ref, key_seen_ref, query_seen_ref, pulls_ref, weights_ref = outs
     row = lax.broadcasted_iota(jnp.int32, (ROWS, DK), 0)
     row_step = row % STEPS
-    kept_ref, sent_ref = key_refs[0]
-    width = HEADS_WIDTH // PIECES
+    kept_ref, sent_ref, width = key_refs[0]
     gates = kept_ref[:ROWS, width : width + 2 * H] + sent_ref[:, width : width + 2 * H]
     for head in range(H):
         key = unit_length(activate(key_refs, 1, head, early_ref, taps_ref, row_step))
@@ -106,11 +114,10 @@
 
 
 def values_kernel(slots_ref, halves_ref, lengths_ref, *refs):
-    value_refs = [(refs[2 * i], refs[2 * i + 1]) for i in range(PIECES)]
-    early_ref, taps_ref, beta_ref, key_seen_ref, query_seen_ref, pulls_ref, weights_ref = refs[
-        2 * PIECES : 2 * PIECES + 7
-    ]
-    out_ref, heads_ref = refs[2 * PIECES + 7 :]
+    value_refs = paired(refs, VALUE_WIDTHS)
+    rest = refs[2 * len(VALUE_WIDTHS) :]
+    early_ref, taps_ref, beta_ref, key_seen_ref, query_seen_ref, pulls_ref, weights_ref = rest[:7]
+    out_ref, heads_ref = rest[7:]
     row = lax.broadcasted_iota(jnp.int32, (ROWS, DK), 0)
     row_step = row % STEPS
     lane = lax.broadcasted_iota(jnp.int32, (ROWS, DK), 1)
@@ -154,7 +161,7 @@
     prepared = pl.pallas_call(
         keys_kernel,
         out_shape=[per_head] * 3 + lags,
-        in_specs=[vmem] * (4 * PIECES + 3),
+        in_specs=[vmem] * (2 * len(KEY_WIDTHS + QUERY_WIDTHS) + 3),
         out_specs=[vmem] * 5,
         compiler_params=params,
         cost_estimate=pl.CostEstimate(flops=40_000_000, bytes_accessed=9_000_000, transcendentals=0),
@@ -163,7 +170,7 @@
     return pl.pallas_call(
         values_kernel,
         out_shape=jax.ShapeDtypeStruct((UNITS // 4, 2 * ROWS, DK), jnp.bfloat16),
-        in_specs=[smem] * 3 + [vmem] * (2 * PIECES + 7),
+        in_specs=[smem] * 3 + [vmem] * (2 * len(VALUE_WIDTHS) + 7),
         out_specs=vmem,
         scratch_shapes=[pltpu.VMEM((H, ROWS, DK), jnp.float32)],
         compiler_params=params,
@@ -206,43 +213,48 @@
         order.append(offset)
     holders = jnp.bitwise_xor(jnp.asarray(order, jnp.int32), me)
     old_rows = (holders[:, None] * LOCAL + jnp.arange(LOCAL, dtype=jnp.int32)[None, :]).reshape(-1)
-    flat_tokens = tokens.reshape(row_count * STEPS, D)
     steps = jnp.arange(STEPS, dtype=jnp.int32)
     wanted = (old_rows[:, None] * STEPS + steps[None, :]).reshape(-1)
     offered = (slot_of[:, None] * STEPS + steps[None, :]).reshape(-1)
     picker = (wanted[:, None] == offered[None, :]).astype(jnp.bfloat16)
 
     def token_part(owner):
-        columns = lax.dynamic_slice_in_dim(flat_tokens, owner * depth, depth, 1)
+        columns = lax.dynamic_slice_in_dim(tokens, owner * depth, depth, 2)
+        columns = columns.reshape(row_count * STEPS, depth)
         return jnp.dot(picker, columns, preferred_element_type=jnp.float32).astype(jnp.bfloat16)
 
     mine, theirs = token_part(me), token_part(jnp.bitwise_xor(me, 1))
-    half_rows = chips * ROWS // 2
-
-    width = HEADS_WIDTH // PIECES
-    chunks, others = [], []
+
+    blocks, others = [], []
     weight = qkv_weight
-    for part in (1, 0, 2):
-        for piece in range(PIECES):
-            begin = part * HEADS_WIDTH + piece * width
+    for part, widths in ((1, KEY_WIDTHS), (0, QUERY_WIDTHS), (2, VALUE_WIDTHS)):
+        begin = part * HEADS_WIDTH
+        for width in widths:
             block = weight[:, begin : begin + width]
-            if not chunks:
+            if not blocks:
                 block = jnp.concatenate([block, gate_weight], axis=1)
             block, weight = lax.optimization_barrier((block, weight))
-            chunks.append(block)
+            blocks.append(block)
             others.append(swap(block, 1, devices))
-
-    pieces = []
-    for block, other in zip(chunks, others):
+            begin += width
+
+    products = []
+    for block, other in zip(blocks, others):
         total = jnp.dot(mine, block, preferred_element_type=jnp.float32)
         total = total + jnp.dot(theirs, other, preferred_element_type=jnp.float32)
+        total, mine, theirs = lax.optimization_barrier((total, mine, theirs))
+        products.append(total)
+    first_tap, _ = lax.optimization_barrier((conv_weight, products[-1]))
+    pieces = []
+    for total in products:
         for bit in bits[:-1]:
             half = total.shape[0] // 2
             total = total[:half] + swap(total[half:], bit, devices)
         pieces.append((total, swap(total[ROWS:], bits[-1], devices)))
-    keys, queries, values = (pieces[i * PIECES : (i + 1) * PIECES] for i in range(3))
-
-    gathered = conv_weight[None]
+    keys, pieces = pieces[: len(KEY_WIDTHS)], pieces[len(KEY_WIDTHS) :]
+    queries, values = pieces[: len(QUERY_WIDTHS)], pieces[len(QUERY_WIDTHS) :]
+
+    gathered = first_tap[None]
     for b in range(devices.bit_length() - 1):
         gathered = jnp.concatenate([gathered, swap(gathered, 1 << b, devices)], axis=0)
     places = jnp.arange(devices, dtype=jnp.int32)

time: 122 us -> 115 us (0.943)
  starting transfers between devices: 36.5 us -> 23.7 us
  waiting for transfers between devices: 33.4 us -> 42.1 us
  matrix products: 17.1 us -> 9 us
  local copies, waits for them, and re-layouts: 12.7 us -> 17.1 us
    ppermute x28 -> x24, starting transfers between devices: 36.5 us -> 23.7 us  [swap(): return lax.ppermute(value, 'heads', [(i, i ^ bit) for i in range(devices)])]
    ppermute x28 -> x24, waiting for transfers between devices: 33.4 us -> 42.1 us  [swap(): return lax.ppermute(value, 'heads', [(i, i ^ bit) for i in range(devices)])]
    dot_general x6 -> x5, matrix products: 9.07 us -> 2.4 us  [on_device(): total = jnp.dot(mine, block, preferred_element_type=jnp.float32)]
    add x12 -> x10, other arithmetic: 0.29 us -> 4.3 us  [on_device(): total = total[:half] + swap(total[half:], bit, devices)]
    slice x12 -> x10, local copies, waits for them, and re-layouts: 0.18 us -> 2.36 us  [on_device(): total = total[:half] + swap(total[half:], bit, devices)]
    concatenate x3, other arithmetic: 2.26 us -> 0.14 us  [on_device(): jnp.concatenate([gathered, swap(gathered, 1 << b, devices)], axis=0)]
    dot_general x2, matrix products: 1.94 us -> 0.38 us  [token_part(): jnp.dot(picker, columns, preferred_element_type=jnp.float32)]
    unnamed x48 -> x18, local copies, waits for them, and re-layouts: 4.55 us -> 3.15 us
  transfers between devices with their start and end apart: 28 -> 24, of which waited for: 13 -> 8; matrix products, arithmetic and copies ran while one was open for 19% -> 23% of each run, Pallas kernels for 3% -> 3%
where the time goes in v3:
time: 115 us; the launch traced here: 114 us
  waiting for transfers between devices  42.1 us (37%)
  starting transfers between devices  23.7 us (21%)
  local copies, waits for them, and re-layouts  17.1 us (15%)
  blocking collectives  10.9 us (9%)
  matrix products  9 us (8%)
  other arithmetic  6.44 us (6%)
  Pallas kernels  4.69 us (4%)
    ppermute x24, waiting for transfers between devices, swap(): return lax.ppermute(value, 'heads', [(i, i ^ bit) for i in range(devices)])  42.1 us
    ppermute x24, starting transfers between devices, swap(): return lax.ppermute(value, 'heads', [(i, i ^ bit) for i in range(devices)])  23.7 us
    all_to_all x1, blocking collectives, on_device(): lax.all_to_all(sending, 'heads', split_axis=0, concat_axis=0, tiled=True)  10.9 us
    slice x5, local copies, waits for them, and re-layouts, on_device(): block = weight[:, begin:begin + width]  6.65 us
    dot_general x5, matrix products, on_device(): total = total + jnp.dot(theirs, other, preferred_element_type=jnp.float32)  5.8 us
    add x10, other arithmetic, on_device(): total = total[:half] + swap(total[half:], bit, devices)  4.3 us
    pallas_call x1, Pallas kernels, run_delta(): pl.pallas_call(keys_kernel, out_shape=[per_head] * 3 + lags, in_specs=[vm...  3.64 us
    unnamed x18, local copies, waits for them, and re-layouts  3.15 us
  transfers between devices with their start and end apart: 24, of which 8 were waited for; matrix products, arithmetic and copies ran while one was open for 23% of the time, Pallas kernels for 3%

profile of v3, /device:TPU:0, one launch (start us, length us, event | category | flops | bytes accessed | tf_op | source)
XLA Modules:
  0.0 114.4 jit_solution(8741513360413128997)
XLA Ops:
  2.4 1.2 %slice.127 = bf16[144,3072]{1,0:T(8,128)(2,1)S(1)} slice(bf16[144,12288]{1,0:T(8,128)(2,1)} %param.12), slice={[0:144], [5120:8192]} | slice | bytes 1769472 | tf_op jit(solution)/shard_map/slice | solution.py:233
  3.8 1.3 %slice.128 = bf16[144,4096]{1,0:T(8,128)(2,1)S(1)} slice(bf16[144,12288]{1,0:T(8,128)(2,1)} %param.12), slice={[0:144], [0:4096]} | slice | bytes 2359296 | tf_op jit(solution)/shard_map/slice | solution.py:233
  5.7 2.1 %slice.129 = bf16[144,3072]{1,0:T(8,128)(2,1)} slice(bf16[144,12288]{1,0:T(8,128)(2,1)} %param.12), slice={[0:144], [8192:11264]} | slice | bytes 1769472 | tf_op jit(solution)/shard_map/slice | solution.py:233
  9.3 1.1 constant_dynamic-slice_fusion.1
  12.5 1.4 %convolution_add_fusion.2 = f32[64,3072]{1,0:T(8,128)S(1)} fusion(f32[64,3072]{1,0:T(8,128)S(1)} %fusion.18, bf16[64,144]{1,0:T(8,128)(2,1)S(1)} %convolution_convert_fusion.2, bf16[144,3072]{1,0:T(8,128)(2,1)} %collective-permute-done.1), kind=kOutput, calls=%fused_computation.2 | convolution fusion | flops 56819712 | bytes 2476032 | tf_op jit(solution)/shard_map/dot_general | solution.py:244
  14.3 1.6 %convolution_add_fusion = f32[64,4096]{1,0:T(8,128)S(1)} fusion(f32[64,4096]{1,0:T(8,128)S(1)} %fusion.19, bf16[64,144]{1,0:T(8,128)(2,1)S(1)} %convolution_convert_fusion.2, bf16[144,4096]{1,0:T(8,128)(2,1)} %collective-permute-done.2), kind=kOutput, calls=%fused_computation | convolution fusion | flops 75759616 | bytes 3295232 | tf_op jit(solution)/shard_map/dot_general | solution.py:244
  15.9 1.4 %fusion.20 = f32[64,3072]{1,0:T(8,128)S(1)} fusion(bf16[64,144]{1,0:T(8,128)(2,1)S(1)} %convolution_convert_fusion.3, bf16[144,3072]{1,0:T(8,128)(2,1)} %slice.129), kind=kOutput, calls=%fused_computation.69 | convolution fusion | flops 56623104 | bytes 1689600 | tf_op jit(solution)/shard_map/dot_general | solution.py:243
  17.4 1.4 %convolution_add_fusion.1 = f32[64,3072]{1,0:T(8,128)S(1)} fusion(f32[64,3072]{1,0:T(8,128)S(1)} %fusion.20, bf16[64,144]{1,0:T(8,128)(2,1)S(1)} %convolution_convert_fusion.2, bf16[144,3072]{1,0:T(8,128)(2,1)} %collective-permute-done.3), kind=kOutput, calls=%fused_computation.1 | convolution fusion | flops 56819712 | bytes 2476032 | tf_op jit(solution)/shard_map/dot_general | solution.py:244
  19.0 1.1 convolution_add_fusion.4
  20.4 3.0 %collective-permute-start.15 = (f32[32,1088]{1,0:T(8,128)S(1)}, f32[32,1088]{1,0:T(8,128)S(1)}, u32[]{:S(2)}, u32[]{:S(2)}) collective-permute-start(f32[32,1088]{1,0:T(8,128)S(1)} %slice.151), channel_id=1, source_target_pairs={{0,2},{1,3},{2,0},{3,1},{4,6},{5,7},{6,4},{7,5},{8,10},{9,11},{10,... | collective-permute-start | bytes 417800 | tf_op jit(solution)/shard_map/ppermute | solution.py:183
  24.3 3.5 %collective-permute-done.12 = bf16[2,4,768]{2,0,1:T(2,128)(2,1)S(1)} collective-permute-done((bf16[2,4,768]{2,0,1:T(2,128)(2,1)S(1)}, bf16[2,4,768]{2,0,1:T(2,128)(2,1)S(1)}, u32[]{:S(2)}, u32[]{:S(2)}) %collective-permute-start.12) | collective-permute-done | bytes 12320 | tf_op jit(solution)/shard_map/ppermute | solution.py:183
  27.8 1.9 %collective-permute-start.13 = (bf16[4,4,768]{2,0,1:T(4,128)(2,1)S(1)}, bf16[4,4,768]{2,0,1:T(4,128)(2,1)S(1)}, u32[]{:S(2)}, u32[]{:S(2)}) collective-permute-start(bf16[4,4,768]{2,0,1:T(4,128)(2,1)S(1)} %pad_maximum_fusion.2), channel_id=1, source_target_pairs={{0,4},{1,5},{2,6},{3,7},{4,0},{5,1},{6,2},{7,3},{8,12},{9,13},{10,... | collective-permute-start | bytes 73736 | tf_op jit(solution)/shard_map/ppermute | solution.py:183
  30.0 2.0 %collective-permute-done.13 = bf16[4,4,768]{2,0,1:T(4,128)(2,1)S(1)} collective-permute-done((bf16[4,4,768]{2,0,1:T(4,128)(2,1)S(1)}, bf16[4,4,768]{2,0,1:T(4,128)(2,1)S(1)}, u32[]{:S(2)}, u32[]{:S(2)}) %collective-permute-start.13) | collective-permute-done | bytes 24608 | tf_op jit(solution)/shard_map/ppermute | solution.py:183
  32.0 2.8 %collective-permute-start.14 = (bf16[8,4,768]{2,0,1:T(8,128)(2,1)S(1)}, bf16[8,4,768]{2,0,1:T(8,128)(2,1)}, u32[]{:S(2)}, u32[]{:S(2)}) collective-permute-start(bf16[8,4,768]{2,0,1:T(8,128)(2,1)S(1)} %pad_maximum_fusion.1), channel_id=1, source_target_pairs={{0,8},{1,9},{2,10},{3,11},{4,12},{5,13},{6,14},{7,15},{8,0},{9,1},... | collective-permute-start | bytes 147464 | tf_op jit(solution)/shard_map/ppermute | solution.py:183
  35.5 1.9 %collective-permute-start.17 = (f32[8,1088]{1,0:T(8,128)}, f32[8,1088]{1,0:T(8,128)S(1)}, u32[]{:S(2)}, u32[]{:S(2)}) collective-permute-start(f32[8,1088]{1,0:T(8,128)} %slice.178), channel_id=1, source_target_pairs={{0,8},{1,9},{2,10},{3,11},{4,12},{5,13},{6,14},{7,15},{8,0},{9,1},... | collective-permute-start | bytes 104456 | tf_op jit(solution)/shard_map/ppermute | solution.py:183
  38.1 1.5 %collective-permute-start.18 = (f32[32,3072]{1,0:T(8,128)}, f32[32,3072]{1,0:T(8,128)}, u32[]{:S(2)}, u32[]{:S(2)}) collective-permute-start(f32[32,3072]{1,0:T(8,128)} %slice.156), channel_id=1, source_target_pairs={{0,2},{1,3},{2,0},{3,1},{4,6},{5,7},{6,4},{7,5},{8,10},{9,11},{10,... | collective-permute-start | bytes 1179656 | tf_op jit(solution)/shard_map/ppermute | solution.py:183
  41.6 1.5 %collective-permute-start.8 = (f32[32,1024]{1,0:T(8,128)}, f32[32,1024]{1,0:T(8,128)}, u32[]{:S(2)}, u32[]{:S(2)}) collective-permute-start(f32[32,1024]{1,0:T(8,128)} %slice.137), channel_id=1, source_target_pairs={{0,2},{1,3},{2,0},{3,1},{4,6},{5,7},{6,4},{7,5},{8,10},{9,11},{10,... | collective-permute-start | bytes 393224 | tf_op jit(solution)/shard_map/ppermute | solution.py:183
  43.8 1.6 %concatenate.30 = bf16[16,4,768]{2,0,1:T(8,128)(2,1)S(1)} concatenate(bf16[1,4,768]{2,0,1:T(2,128)(2,1)S(1)} %copy.26, bf16[1,4,768]{2,0,1:T(2,128)(2,1)S(1)} %collective-permute-done.11, bf16[2,4,768]{2,0,1:T(2,128)(2,1)S(1)} %collective-permute-done.12, bf16[4,4,768]{2,0,1:T(4,128)(2,1)} %copy-done.1, bf16[8,4,768]{2,0,1:T(8,128)(2,1)} %collective-permute-done.14), dimensions={0} | concatenate | bytes 196608 | tf_op jit(solution)/shard_map/concatenate | solution.py:259
  45.8 1.1 %multiply_add_fusion.1 = (f32[2,1,12288]{2,0,1:T(2,128)S(1)}, f32[2,1,12288]{2,0,1:T(2,128)S(1)}, f32[2,1,12288]{2,0,1:T(2,128)S(1)}) fusion(f32[2,3,12288]{2,0,1:T(2,128)} %param.16, f32[12288]{0:T(1024)S(1)} %bitcast.44, f32[12288]{0:T(1024)S(1)} %bitcast.45, f32[12288]{0:T(1024)S(1)} %bitcast.46), kind=kLoop, calls=%fused_computation.21 | loop fusion | flops 221184 | bytes 737280 | tf_op jit(solution)/shard_map/add | solution.py:269
  46.9 17.6 %collective-permute-done.8 = f32[32,1024]{1,0:T(8,128)} collective-permute-done((f32[32,1024]{1,0:T(8,128)}, f32[32,1024]{1,0:T(8,128)}, u32[]{:S(2)}, u32[]{:S(2)}) %collective-permute-start.8) | collective-permute-done | bytes 131104 | tf_op jit(solution)/shard_map/ppermute | solution.py:183
  67.1 1.6 %collective-permute-start.19 = (f32[16,3072]{1,0:T(8,128)S(1)}, f32[16,3072]{1,0:T(8,128)S(1)}, u32[]{:S(2)}, u32[]{:S(2)}) collective-permute-start(f32[16,3072]{1,0:T(8,128)S(1)} %slice.180), channel_id=1, source_target_pairs={{0,4},{1,5},{2,6},{3,7},{4,0},{5,1},{6,2},{7,3},{8,12},{9,13},{10,... | collective-permute-start | bytes 589832 | tf_op jit(solution)/shard_map/ppermute | solution.py:183
  68.7 2.2 %collective-permute-done.9 = f32[16,1024]{1,0:T(8,128)S(1)} collective-permute-done((f32[16,1024]{1,0:T(8,128)S(1)}, f32[16,1024]{1,0:T(8,128)S(1)}, u32[]{:S(2)}, u32[]{:S(2)}) %collective-permute-start.9) | collective-permute-done | bytes 65568 | tf_op jit(solution)/shard_map/ppermute | solution.py:183
  71.2 3.9 %collective-permute-done.19 = f32[16,3072]{1,0:T(8,128)S(1)} collective-permute-done((f32[16,3072]{1,0:T(8,128)S(1)}, f32[16,3072]{1,0:T(8,128)S(1)}, u32[]{:S(2)}, u32[]{:S(2)}) %collective-permute-start.19) | collective-permute-done | bytes 196640 | tf_op jit(solution)/shard_map/ppermute | solution.py:183
  75.1 1.9 %collective-permute-start.20 = (f32[8,3072]{1,0:T(8,128)S(1)}, f32[8,3072]{1,0:T(8,128)S(1)}, u32[]{:S(2)}, u32[]{:S(2)}) collective-permute-start(f32[8,3072]{1,0:T(8,128)S(1)} %slice.181), channel_id=1, source_target_pairs={{0,8},{1,9},{2,10},{3,11},{4,12},{5,13},{6,14},{7,15},{8,0},{9,1},... | collective-permute-start | bytes 294920 | tf_op jit(solution)/shard_map/ppermute | solution.py:183
  78.9 1.1 slice_add_fusion
  80.1 1.4 %collective-permute-start.22 = (f32[16,4096]{1,0:T(8,128)S(1)}, f32[16,4096]{1,0:T(8,128)S(1)}, u32[]{:S(2)}, u32[]{:S(2)}) collective-permute-start(f32[16,4096]{1,0:T(8,128)S(1)} %slice.183), channel_id=1, source_target_pairs={{0,4},{1,5},{2,6},{3,7},{4,0},{5,1},{6,2},{7,3},{8,12},{9,13},{10,... | collective-permute-start | bytes 786440 | tf_op jit(solution)/shard_map/ppermute | solution.py:183
  81.5 4.6 %collective-permute-done.5 = f32[16,3072]{1,0:T(8,128)S(1)} collective-permute-done((f32[16,3072]{1,0:T(8,128)S(1)}, f32[16,3072]{1,0:T(8,128)S(1)}, u32[]{:S(2)}, u32[]{:S(2)}) %collective-permute-start.5) | collective-permute-done | bytes 196640 | tf_op jit(solution)/shard_map/ppermute | solution.py:183
  86.5 2.4 %collective-permute-done.22 = f32[16,4096]{1,0:T(8,128)S(1)} collective-permute-done((f32[16,4096]{1,0:T(8,128)S(1)}, f32[16,4096]{1,0:T(8,128)S(1)}, u32[]{:S(2)}, u32[]{:S(2)}) %collective-permute-start.22) | collective-permute-done | bytes 262176 | tf_op jit(solution)/shard_map/ppermute | solution.py:183
  89.9 5.9 %collective-permute-done.23.refs_5_ = f32[8,4096]{1,0:T(8,128)S(1)} collective-permute-done((f32[8,4096]{1,0:T(8,128)S(1)}, f32[8,4096]{1,0:T(8,128)S(1)}, u32[]{:S(2)}, u32[]{:S(2)}) %collective-permute-start.23) | collective-permute-done | bytes 131104 | tf_op jit(solution)/shard_map/ppermute | solution.py:183
  95.8 2.2 %copy-done = f32[2,32,128,128]{3,2,1,0:T(8,128)S(1)} copy-done((f32[2,32,128,128]{3,2,1,0:T(8,128)S(1)}, f32[2,32,128,128]{3,2,1,0:T(8,128)}, u32[]{:S(2)}) %copy-start) | copy-done | bytes 4194328
  98.0 3.6 %keys_part.1 = (f32[32,8,128]{2,1,0:T(8,128)S(1)}, f32[32,8,128]{2,1,0:T(8,128)S(1)}, f32[32,8,128]{2,1,0:T(8,128)S(1)}, f32[3,32,8,128]{3,2,1,0:T(8,128)S(1)}, f32[4,32,8,128]{3,2,1,0:T(8,128)S(1)}) custom-call(f32[16,1088]{1,0:T(8,128)S(1)} %slice_add_fusion.8.refs_0_, f32[8,1088]{1,0:T(8,128)S(1)} %collective-permute-done.17.refs_1_, ...), custom_call_target="tpu_custom_call" | custom-call | flops 40000000 | bytes 9000000 | tf_op jit(solution)/shard_map/keys_part/pallas_call | solution.py:161
  102.7 10.9 %all_to_all.5 = bf16[16,16,128]{2,1,0:T(8,128)(2,1)S(1)} all-to-all(bf16[16,16,128]{2,1,0:T(8,128)(2,1)S(1)} %values_part.1), channel_id=1, replica_groups=mesh['groups'=2,'heads'=16] {'heads'}, dimensions={0} | all-to-all | bytes 131072 | tf_op jit(solution)/shard_map/all_to_all | solution.py:287
  (112 shorter events, 20.9 us)
Async XLA Ops:
  1.9 10.1 %collective-permute-start = (bf16[144,1088]{1,0:T(8,128)(2,1)S(1)}, bf16[144,1088]{1,0:T(8,128)(2,1)S(1)}, u32[]{:S(2)}, u32[]{:S(2)}) collective-permute-start(bf16[144,1088]{1,0:T(8,128)(2,1)S(1)} %pad_maximum_fusion), channel_id=1, source_target_pairs={{0,1},{1,0},{2,3},{3,2},{4,5},{5,4},{6,7},{7,6},{8,9},{9,8},{10,11... | collective-permute-start | bytes 940040 | tf_op jit(solution)/shard_map/ppermute | solution.py:183
  3.6 8.9 %collective-permute-start.1 = (bf16[144,3072]{1,0:T(8,128)(2,1)S(1)}, bf16[144,3072]{1,0:T(8,128)(2,1)}, u32[]{:S(2)}, u32[]{:S(2)}) collective-permute-start(bf16[144,3072]{1,0:T(8,128)(2,1)S(1)} %slice.127), channel_id=1, source_target_pairs={{0,1},{1,0},{2,3},{3,2},{4,5},{5,4},{6,7},{7,6},{8,9},{9,8},{10,11... | collective-permute-start | bytes 2654216 | tf_op jit(solution)/shard_map/ppermute | solution.py:183
  5.1 5.4 %copy-start.7 = (s32[8]{0:T(128)S(1)}, s32[8]{0:T(128)}, u32[]{:S(2)}) copy-start(s32[8]{0:T(128)} %constant.44.clone) | copy-start | bytes 100
  5.1 5.7 %copy-start.4 = (s32[32]{0:T(128)S(1)}, s32[32]{0:T(128)}, u32[]{:S(2)}) copy-start(s32[32]{0:T(128)} %param.19) | copy-start | bytes 388
  5.1 9.2 %collective-permute-start.2 = (bf16[144,4096]{1,0:T(8,128)(2,1)S(1)}, bf16[144,4096]{1,0:T(8,128)(2,1)}, u32[]{:S(2)}, u32[]{:S(2)}) collective-permute-start(bf16[144,4096]{1,0:T(8,128)(2,1)S(1)} %slice.128), channel_id=1, source_target_pairs={{0,1},{1,0},{2,3},{3,2},{4,5},{5,4},{6,7},{7,6},{8,9},{9,8},{10,11... | collective-permute-start | bytes 3538952 | tf_op jit(solution)/shard_map/ppermute | solution.py:183
  7.8 3.9 %copy-start.3 = (s32[32]{0:T(128)S(1)}, s32[32]{0:T(128)}, u32[]{:S(2)}) copy-start(s32[32]{0:T(128)} %param.20) | copy-start | bytes 388
  7.8 4.1 %copy-start.5 = (s32[64]{0:T(128)S(1)}, s32[64]{0:T(128)}, u32[]{:S(2)}) copy-start(s32[64]{0:T(128)} %param.18) | copy-start | bytes 772
  7.8 4.1 %copy-start.6 = (s32[32]{0:T(128)S(1)}, s32[32]{0:T(128)}, u32[]{:S(2)}) copy-start(s32[32]{0:T(128)} %param.17) | copy-start | bytes 388
  7.8 9.6 %collective-permute-start.3 = (bf16[144,3072]{1,0:T(8,128)(2,1)}, bf16[144,3072]{1,0:T(8,128)(2,1)}, u32[]{:S(2)}, u32[]{:S(2)}) collective-permute-start(bf16[144,3072]{1,0:T(8,128)(2,1)} %slice.129), channel_id=1, source_target_pairs={{0,1},{1,0},{2,3},{3,2},{4,5},{5,4},{6,7},{7,6},{8,9},{9,8},{10,11... | collective-permute-start | bytes 2654216 | tf_op jit(solution)/shard_map/ppermute | solution.py:183
  8.8 10.2 %collective-permute-start.7 = (bf16[144,1024]{1,0:T(8,128)(2,1)S(1)}, bf16[144,1024]{1,0:T(8,128)(2,1)}, u32[]{:S(2)}, u32[]{:S(2)}) collective-permute-start(bf16[144,1024]{1,0:T(8,128)(2,1)S(1)} %slice.135), channel_id=1, source_target_pairs={{0,1},{1,0},{2,3},{3,2},{4,5},{5,4},{6,7},{7,6},{8,9},{9,8},{10,11... | collective-permute-start | bytes 884744 | tf_op jit(solution)/shard_map/ppermute | solution.py:183
  18.8 1.4 %copy-start.2 = (bf16[4,768]{1,0:T(4,128)(2,1)S(1)}, bf16[4,768]{1,0:T(4,128)(2,1)}, u32[]{:S(2)}) copy-start(bf16[4,768]{1,0:T(4,128)(2,1)} %param.14) | copy-start | bytes 18436
  20.2 3.3 %collective-permute-start.11 = (bf16[1,4,768]{2,0,1:T(2,128)(2,1)S(1)}, bf16[1,4,768]{2,0,1:T(2,128)(2,1)S(1)}, u32[]{:S(2)}, u32[]{:S(2)}) collective-permute-start(bf16[1,4,768]{2,0,1:T(2,128)(2,1)S(1)} %copy.26), channel_id=1, source_target_pairs={{0,1},{1,0},{2,3},{3,2},{4,5},{5,4},{6,7},{7,6},{8,9},{9,8},{10,11... | collective-permute-start | bytes 18440 | tf_op jit(solution)/shard_map/ppermute | solution.py:183
  20.4 9.3 %collective-permute-start.15 = (f32[32,1088]{1,0:T(8,128)S(1)}, f32[32,1088]{1,0:T(8,128)S(1)}, u32[]{:S(2)}, u32[]{:S(2)}) collective-permute-start(f32[32,1088]{1,0:T(8,128)S(1)} %slice.151), channel_id=1, source_target_pairs={{0,2},{1,3},{2,0},{3,1},{4,6},{5,7},{6,4},{7,5},{8,10},{9,11},{10,... | collective-permute-start | bytes 417800 | tf_op jit(solution)/shard_map/ppermute | solution.py:183
  23.5 4.3 %collective-permute-start.12 = (bf16[2,4,768]{2,0,1:T(2,128)(2,1)S(1)}, bf16[2,4,768]{2,0,1:T(2,128)(2,1)S(1)}, u32[]{:S(2)}, u32[]{:S(2)}) collective-permute-start(bf16[2,4,768]{2,0,1:T(2,128)(2,1)S(1)} %pad_maximum_fusion.3), channel_id=1, source_target_pairs={{0,2},{1,3},{2,0},{3,1},{4,6},{5,7},{6,4},{7,5},{8,10},{9,11},{10,... | collective-permute-start | bytes 36872 | tf_op jit(solution)/shard_map/ppermute | solution.py:183
  27.8 4.2 %collective-permute-start.13 = (bf16[4,4,768]{2,0,1:T(4,128)(2,1)S(1)}, bf16[4,4,768]{2,0,1:T(4,128)(2,1)S(1)}, u32[]{:S(2)}, u32[]{:S(2)}) collective-permute-start(bf16[4,4,768]{2,0,1:T(4,128)(2,1)S(1)} %pad_maximum_fusion.2), channel_id=1, source_target_pairs={{0,4},{1,5},{2,6},{3,7},{4,0},{5,1},{6,2},{7,3},{8,12},{9,13},{10,... | collective-permute-start | bytes 73736 | tf_op jit(solution)/shard_map/ppermute | solution.py:183
  29.7 5.1 %collective-permute-start.16 = (f32[16,1088]{1,0:T(8,128)S(1)}, f32[16,1088]{1,0:T(8,128)S(1)}, u32[]{:S(2)}, u32[]{:S(2)}) collective-permute-start(f32[16,1088]{1,0:T(8,128)S(1)} %slice.177), channel_id=1, source_target_pairs={{0,4},{1,5},{2,6},{3,7},{4,0},{5,1},{6,2},{7,3},{8,12},{9,13},{10,... | collective-permute-start | bytes 208904 | tf_op jit(solution)/shard_map/ppermute | solution.py:183
  32.0 11.2 %copy-start.1 = (bf16[4,4,768]{2,0,1:T(4,128)(2,1)}, bf16[4,4,768]{2,0,1:T(4,128)(2,1)S(1)}, u32[]{:S(2)}) copy-start(bf16[4,4,768]{2,0,1:T(4,128)(2,1)S(1)} %collective-permute-done.13) | copy-start | bytes 73732
  32.0 11.2 %collective-permute-start.14 = (bf16[8,4,768]{2,0,1:T(8,128)(2,1)S(1)}, bf16[8,4,768]{2,0,1:T(8,128)(2,1)}, u32[]{:S(2)}, u32[]{:S(2)}) collective-permute-start(bf16[8,4,768]{2,0,1:T(8,128)(2,1)S(1)} %pad_maximum_fusion.1), channel_id=1, source_target_pairs={{0,8},{1,9},{2,10},{3,11},{4,12},{5,13},{6,14},{7,15},{8,0},{9,1},... | collective-permute-start | bytes 147464 | tf_op jit(solution)/shard_map/ppermute | solution.py:183
  35.5 54.4 %collective-permute-start.17 = (f32[8,1088]{1,0:T(8,128)}, f32[8,1088]{1,0:T(8,128)S(1)}, u32[]{:S(2)}, u32[]{:S(2)}) collective-permute-start(f32[8,1088]{1,0:T(8,128)} %slice.178), channel_id=1, source_target_pairs={{0,8},{1,9},{2,10},{3,11},{4,12},{5,13},{6,14},{7,15},{8,0},{9,1},... | collective-permute-start | bytes 104456 | tf_op jit(solution)/shard_map/ppermute | solution.py:183
  38.1 27.9 %collective-permute-start.18 = (f32[32,3072]{1,0:T(8,128)}, f32[32,3072]{1,0:T(8,128)}, u32[]{:S(2)}, u32[]{:S(2)}) collective-permute-start(f32[32,3072]{1,0:T(8,128)} %slice.156), channel_id=1, source_target_pairs={{0,2},{1,3},{2,0},{3,1},{4,6},{5,7},{6,4},{7,5},{8,10},{9,11},{10,... | collective-permute-start | bytes 1179656 | tf_op jit(solution)/shard_map/ppermute | solution.py:183
  41.1 37.8 %collective-permute-start.21 = (f32[32,4096]{1,0:T(8,128)}, f32[32,4096]{1,0:T(8,128)}, u32[]{:S(2)}, u32[]{:S(2)}) collective-permute-start(f32[32,4096]{1,0:T(8,128)} %slice.161), channel_id=1, source_target_pairs={{0,2},{1,3},{2,0},{3,1},{4,6},{5,7},{6,4},{7,5},{8,10},{9,11},{10,... | collective-permute-start | bytes 1572872 | tf_op jit(solution)/shard_map/ppermute | solution.py:183
  41.6 22.9 %collective-permute-start.8 = (f32[32,1024]{1,0:T(8,128)}, f32[32,1024]{1,0:T(8,128)}, u32[]{:S(2)}, u32[]{:S(2)}) collective-permute-start(f32[32,1024]{1,0:T(8,128)} %slice.137), channel_id=1, source_target_pairs={{0,2},{1,3},{2,0},{3,1},{4,6},{5,7},{6,4},{7,5},{8,10},{9,11},{10,... | collective-permute-start | bytes 393224 | tf_op jit(solution)/shard_map/ppermute | solution.py:183
  43.2 33.9 %collective-permute-start.4 = (f32[32,3072]{1,0:T(8,128)S(1)}, f32[32,3072]{1,0:T(8,128)}, u32[]{:S(2)}, u32[]{:S(2)}) collective-permute-start(f32[32,3072]{1,0:T(8,128)S(1)} %slice.131), channel_id=1, source_target_pairs={{0,2},{1,3},{2,0},{3,1},{4,6},{5,7},{6,4},{7,5},{8,10},{9,11},{10,... | collective-permute-start | bytes 1179656 | tf_op jit(solution)/shard_map/ppermute | solution.py:183
  65.5 5.4 %collective-permute-start.9 = (f32[16,1024]{1,0:T(8,128)S(1)}, f32[16,1024]{1,0:T(8,128)S(1)}, u32[]{:S(2)}, u32[]{:S(2)}) collective-permute-start(f32[16,1024]{1,0:T(8,128)S(1)} %slice.171), channel_id=1, source_target_pairs={{0,4},{1,5},{2,6},{3,7},{4,0},{5,1},{6,2},{7,3},{8,12},{9,13},{10,... | collective-permute-start | bytes 196616 | tf_op jit(solution)/shard_map/ppermute | solution.py:183
  67.1 8.0 %collective-permute-start.19 = (f32[16,3072]{1,0:T(8,128)S(1)}, f32[16,3072]{1,0:T(8,128)S(1)}, u32[]{:S(2)}, u32[]{:S(2)}) collective-permute-start(f32[16,3072]{1,0:T(8,128)S(1)} %slice.180), channel_id=1, source_target_pairs={{0,4},{1,5},{2,6},{3,7},{4,0},{5,1},{6,2},{7,3},{8,12},{9,13},{10,... | collective-permute-start | bytes 589832 | tf_op jit(solution)/shard_map/ppermute | solution.py:183
  70.9 30.7 %collective-permute-start.10 = (f32[8,1024]{1,0:T(8,128)S(1)}, f32[8,1024]{1,0:T(8,128)S(1)}, u32[]{:S(2)}, u32[]{:S(2)}) collective-permute-start(f32[8,1024]{1,0:T(8,128)S(1)} %slice.172), channel_id=1, source_target_pairs={{0,8},{1,9},{2,10},{3,11},{4,12},{5,13},{6,14},{7,15},{8,0},{9,1},... | collective-permute-start | bytes 98312 | tf_op jit(solution)/shard_map/ppermute | solution.py:183
  75.1 14.8 %collective-permute-start.20 = (f32[8,3072]{1,0:T(8,128)S(1)}, f32[8,3072]{1,0:T(8,128)S(1)}, u32[]{:S(2)}, u32[]{:S(2)}) collective-permute-start(f32[8,3072]{1,0:T(8,128)S(1)} %slice.181), channel_id=1, source_target_pairs={{0,8},{1,9},{2,10},{3,11},{4,12},{5,13},{6,14},{7,15},{8,0},{9,1},... | collective-permute-start | bytes 294920 | tf_op jit(solution)/shard_map/ppermute | solution.py:183
  78.2 7.9 %collective-permute-start.5 = (f32[16,3072]{1,0:T(8,128)S(1)}, f32[16,3072]{1,0:T(8,128)S(1)}, u32[]{:S(2)}, u32[]{:S(2)}) collective-permute-start(f32[16,3072]{1,0:T(8,128)S(1)} %slice.168), channel_id=1, source_target_pairs={{0,4},{1,5},{2,6},{3,7},{4,0},{5,1},{6,2},{7,3},{8,12},{9,13},{10,... | collective-permute-start | bytes 589832 | tf_op jit(solution)/shard_map/ppermute | solution.py:183
  80.1 8.8 %collective-permute-start.22 = (f32[16,4096]{1,0:T(8,128)S(1)}, f32[16,4096]{1,0:T(8,128)S(1)}, u32[]{:S(2)}, u32[]{:S(2)}) collective-permute-start(f32[16,4096]{1,0:T(8,128)S(1)} %slice.183), channel_id=1, source_target_pairs={{0,4},{1,5},{2,6},{3,7},{4,0},{5,1},{6,2},{7,3},{8,12},{9,13},{10,... | collective-permute-start | bytes 786440 | tf_op jit(solution)/shard_map/ppermute | solution.py:183
  86.1 15.5 %collective-permute-start.6 = (f32[8,3072]{1,0:T(8,128)S(1)}, f32[8,3072]{1,0:T(8,128)S(1)}, u32[]{:S(2)}, u32[]{:S(2)}) collective-permute-start(f32[8,3072]{1,0:T(8,128)S(1)} %slice.169), channel_id=1, source_target_pairs={{0,8},{1,9},{2,10},{3,11},{4,12},{5,13},{6,14},{7,15},{8,0},{9,1},... | collective-permute-start | bytes 294920 | tf_op jit(solution)/shard_map/ppermute | solution.py:183
  89.0 6.8 %collective-permute-start.23 = (f32[8,4096]{1,0:T(8,128)S(1)}, f32[8,4096]{1,0:T(8,128)S(1)}, u32[]{:S(2)}, u32[]{:S(2)}) collective-permute-start(f32[8,4096]{1,0:T(8,128)S(1)} %slice.184), channel_id=1, source_target_pairs={{0,8},{1,9},{2,10},{3,11},{4,12},{5,13},{6,14},{7,15},{8,0},{9,1},... | collective-permute-start | bytes 393224 | tf_op jit(solution)/shard_map/ppermute | solution.py:183
  95.8 2.2 %copy-start = (f32[2,32,128,128]{3,2,1,0:T(8,128)S(1)}, f32[2,32,128,128]{3,2,1,0:T(8,128)}, u32[]{:S(2)}) copy-start(f32[2,32,128,128]{3,2,1,0:T(8,128)} %refs_8_.1) | copy-start | bytes 12582916

commit v4 on v3

--- a/solution.py
+++ b/solution.py
@@ -17,9 +17,11 @@
 LOCAL = 2
 ROWS = LOCAL * STEPS
 HEADS_WIDTH = H * DK
-KEY_WIDTHS = (1024, 3072)
 QUERY_WIDTHS = (4096,)
+KEY_WIDTHS = (4096,)
 VALUE_WIDTHS = (3072, 1024)
+FIRST_RANGES = (((0, 4096),),)
+SECOND_RANGES = (((0, 4096), (8192, 64)), ((4096, 3072),), ((7168, 1024),))
 
 norm_eps = 1e-06
 
@@ -164,7 +166,7 @@
         in_specs=[vmem] * (2 * len(KEY_WIDTHS + QUERY_WIDTHS) + 3),
         out_specs=[vmem] * 5,
         compiler_params=params,
-        cost_estimate=pl.CostEstimate(flops=40_000_000, bytes_accessed=9_000_000, transcendentals=0),
+        cost_estimate=pl.CostEstimate(flops=0, bytes_accessed=0, transcendentals=0),
         name="keys_part",
     )(*flat(keys), *flat(queries), early, taps, state)
     return pl.pallas_call(
@@ -177,6 +179,41 @@
         cost_estimate=pl.CostEstimate(flops=4_000_000, bytes_accessed=2_000_000, transcendentals=0),
         name="values_part",
     )(slots, halves, lengths, *flat(values), early, taps, *prepared)
+
+
+def product_kernel(ranges, mine_ref, theirs_ref, block_ref, other_ref, *out_refs):
+    half = mine_ref.shape[0] // 2
+    for at, parts in enumerate(ranges):
+        place = 0
+        for begin, width in parts:
+            columns, target = pl.ds(begin, width), pl.ds(place, width)
+            total = jnp.dot(
+                mine_ref[...], block_ref[:, columns], preferred_element_type=jnp.float32
+            )
+            total = total + jnp.dot(
+                theirs_ref[...], other_ref[:, columns], preferred_element_type=jnp.float32
+            )
+            out_refs[2 * at][:, target] = total[:half]
+            out_refs[2 * at + 1][:, target] = total[half:]
+            place += width
+
+
+def run_product(mine, theirs, block, other, ranges):
+    vmem = pl.BlockSpec(memory_space=pltpu.VMEM)
+    half = mine.shape[0] // 2
+    widths = [sum(width for _, width in parts) for parts in ranges]
+    outs = pl.pallas_call(
+        functools.partial(product_kernel, ranges),
+        out_shape=[
+            jax.ShapeDtypeStruct((half, width), jnp.float32) for width in widths for _ in range(2)
+        ],
+        in_specs=[vmem] * 4,
+        out_specs=[vmem] * (2 * len(widths)),
+        compiler_params=pltpu.CompilerParams(vmem_limit_bytes=32 * 1024 * 1024),
+        cost_estimate=pl.CostEstimate(flops=0, bytes_accessed=0, transcendentals=0),
+        name="partial_product",
+    )(mine, theirs, block, other)
+    return [(outs[2 * at], outs[2 * at + 1]) for at in range(len(widths))]
 
 
 def swap(value, bit, devices):
@@ -225,38 +262,44 @@
 
     mine, theirs = token_part(me), token_part(jnp.bitwise_xor(me, 1))
 
-    blocks, others = [], []
-    weight = qkv_weight
-    for part, widths in ((1, KEY_WIDTHS), (0, QUERY_WIDTHS), (2, VALUE_WIDTHS)):
-        begin = part * HEADS_WIDTH
-        for width in widths:
-            block = weight[:, begin : begin + width]
-            if not blocks:
-                block = jnp.concatenate([block, gate_weight], axis=1)
-            block, weight = lax.optimization_barrier((block, weight))
-            blocks.append(block)
-            others.append(swap(block, 1, devices))
-            begin += width
-
-    products = []
-    for block, other in zip(blocks, others):
-        total = jnp.dot(mine, block, preferred_element_type=jnp.float32)
-        total = total + jnp.dot(theirs, other, preferred_element_type=jnp.float32)
-        total, mine, theirs = lax.optimization_barrier((total, mine, theirs))
-        products.append(total)
-    first_tap, _ = lax.optimization_barrier((conv_weight, products[-1]))
+    def widen(gathered, beside, bit):
+        other, beside = lax.optimization_barrier((swap(gathered, bit, devices), beside))
+        return jnp.concatenate([gathered, other], axis=0), beside
+
+    tap_bits = [1 << b for b in range(devices.bit_length() - 1)]
+    gathered = conv_weight[None]
+    first = qkv_weight[:, :HEADS_WIDTH]
+    first, weight = lax.optimization_barrier((first, qkv_weight))
+    first_other = swap(first, 1, devices)
+    for bit in tap_bits[:-3]:
+        gathered, weight = widen(gathered, weight, bit)
+    gathered, weight = widen(gathered, weight, tap_bits[-3])
+    second = jnp.concatenate([weight[:, HEADS_WIDTH:], gate_weight], axis=1)
+    second_other = swap(second, 1, devices)
+    gathered, (mine, theirs) = widen(gathered, (mine, theirs), tap_bits[-2])
+
+    products = run_product(mine, theirs, first, first_other, FIRST_RANGES)
+    products, mine, theirs = lax.optimization_barrier((products, mine, theirs))
+    more = run_product(mine, theirs, second, second_other, SECOND_RANGES)
+    gathered, more = widen(gathered, more, tap_bits[-1])
+    (kept, sent), more = lax.optimization_barrier((products[0], more))
+    products = [(kept, products[0][1])] + more
     pieces = []
-    for total in products:
-        for bit in bits[:-1]:
-            half = total.shape[0] // 2
-            total = total[:half] + swap(total[half:], bit, devices)
-        pieces.append((total, swap(total[ROWS:], bits[-1], devices)))
-    keys, pieces = pieces[: len(KEY_WIDTHS)], pieces[len(KEY_WIDTHS) :]
-    queries, values = pieces[: len(QUERY_WIDTHS)], pieces[len(QUERY_WIDTHS) :]
-
-    gathered = first_tap[None]
-    for b in range(devices.bit_length() - 1):
-        gathered = jnp.concatenate([gathered, swap(gathered, 1 << b, devices)], axis=0)
+    done = [[] for _ in bits]
+    for kept, sent in products:
+        for level, bit in enumerate(bits):
+            window = 2 if level == 0 else 1
+            if len(done[level]) >= window:
+                sent, _ = lax.optimization_barrier((sent, done[level][-window]))
+            got = swap(sent, bit, devices)
+            done[level].append(got)
+            if bit != bits[-1]:
+                added = kept + got
+                half = added.shape[0] // 2
+                kept, sent = added[:half], added[half:]
+        pieces.append((kept, got))
+    queries, keys, values = pieces[:1], pieces[1:2], pieces[2:]
+
     places = jnp.arange(devices, dtype=jnp.int32)
     sorter = (jnp.bitwise_xor(places, me)[:, None] == places[None, :]).astype(jnp.bfloat16)
     taps = jnp.einsum("aj,jtc->tac", sorter, gathered, preferred_element_type=jnp.float32)

time: 115 us -> 98.8 us (0.86)
  matrix products: 9 us -> 0.8 us
  Pallas kernels: 4.69 us -> 10.1 us
  waiting for transfers between devices: 42.1 us -> 36.8 us
  starting transfers between devices: 23.7 us -> 19.4 us
  other arithmetic: 6.44 us -> 3.63 us
  local copies, waits for them, and re-layouts: 17.1 us -> 15.5 us
    dot_general x10 -> x0, matrix products: 8.2 us -> none  [the longest x5 5.8 us: on_device(): total = total + jnp.dot(theirs, other, preferred_element_type=jnp.float32)]
    pallas_call x0 -> x2, Pallas kernels: none -> 5.38 us  [run_product(): pl.pallas_call(functools.partial(product_kernel, ranges), out_shape=[jax....]
    slice x20 -> x10, local copies, waits for them, and re-layouts: 9.66 us -> 4.38 us  [the longest x1 2.4 us: on_device(): first = qkv_weight[:, :HEADS_WIDTH]]
    ppermute x24 -> x18, waiting for transfers between devices: 42.1 us -> 36.8 us  [swap(): return lax.ppermute(value, 'heads', [(i, i ^ bit) for i in range(devices)])]
    ppermute x24 -> x18, starting transfers between devices: 23.7 us -> 19.4 us  [swap(): return lax.ppermute(value, 'heads', [(i, i ^ bit) for i in range(devices)])]
    unnamed x18 -> x38, local copies, waits for them, and re-layouts: 3.15 us -> 6.81 us
    add x10 -> x8, other arithmetic: 4.3 us -> 1.36 us  [on_device(): added = kept + got]
  transfers between devices with their start and end apart: 24 -> 18, of which waited for: 8 -> 11; matrix products, arithmetic and copies ran while one was open for 23% -> 11% of each run, Pallas kernels for 3% -> 9%
where the time goes in v4:
time: 98.8 us; the launch traced here: 98.3 us
  waiting for transfers between devices  36.8 us (37%)
  starting transfers between devices  19.4 us (20%)
  local copies, waits for them, and re-layouts  15.5 us (16%)
  blocking collectives  11.7 us (12%)
  Pallas kernels  10.1 us (10%)
  other arithmetic  3.63 us (4%)
    ppermute x18, waiting for transfers between devices, swap(): return lax.ppermute(value, 'heads', [(i, i ^ bit) for i in range(devices)])  36.8 us
    ppermute x18, starting transfers between devices, swap(): return lax.ppermute(value, 'heads', [(i, i ^ bit) for i in range(devices)])  19.4 us
    all_to_all x1, blocking collectives, on_device(): lax.all_to_all(sending, 'heads', split_axis=0, concat_axis=0, tiled=True)  11.7 us
    unnamed x38, local copies, waits for them, and re-layouts  6.81 us
    pallas_call x2, Pallas kernels, run_product(): pl.pallas_call(functools.partial(product_kernel, ranges), out_shape=[jax....  5.38 us
    pallas_call x1, Pallas kernels, run_delta(): pl.pallas_call(keys_kernel, out_shape=[per_head] * 3 + lags, in_specs=[vm...  3.64 us
    slice x1, local copies, waits for them, and re-layouts, on_device(): first = qkv_weight[:, :HEADS_WIDTH]  2.4 us
  transfers between devices with their start and end apart: 18, of which 11 were waited for; matrix products, arithmetic and copies ran while one was open for 11% of the time, Pallas kernels for 9%

profile of v4, /device:TPU:0, one launch (start us, length us, event | category | flops | bytes accessed | tf_op | source)
XLA Modules:
  0.0 98.3 jit_solution(16890750709080823215)
XLA Ops:
  1.2 2.4 %slice.90.block_ref = bf16[144,4096]{1,0:T(8,128)(2,1)} slice(bf16[144,12288]{1,0:T(8,128)(2,1)} %param.12), slice={[0:144], [0:4096]} | slice | bytes 2359296 | tf_op jit(solution)/shard_map/slice | solution.py:271
  3.7 3.0 %collective-permute-start.1 = (bf16[2,4,768]{2,0,1:T(2,128)(2,1)S(1)}, bf16[2,4,768]{2,0,1:T(2,128)(2,1)S(1)}, u32[]{:S(2)}, u32[]{:S(2)}) collective-permute-start(bf16[2,4,768]{2,0,1:T(2,128)(2,1)S(1)} %pad_maximum_fusion.3), channel_id=1, source_target_pairs={{0,2},{1,3},{2,0},{3,1},{4,6},{5,7},{6,4},{7,5},{8,10},{9,11},{10,... | collective-permute-start | bytes 36872 | tf_op jit(solution)/shard_map/ppermute | solution.py:220
  6.9 1.6 %collective-permute-done.1 = bf16[2,4,768]{2,0,1:T(2,128)(2,1)S(1)} collective-permute-done((bf16[2,4,768]{2,0,1:T(2,128)(2,1)S(1)}, bf16[2,4,768]{2,0,1:T(2,128)(2,1)S(1)}, u32[]{:S(2)}, u32[]{:S(2)}) %collective-permute-start.1) | collective-permute-done | bytes 12320 | tf_op jit(solution)/shard_map/ppermute | solution.py:220
  8.5 1.9 %slice.91 = bf16[144,8192]{1,0:T(8,128)(2,1)S(1)} slice(bf16[144,12288]{1,0:T(8,128)(2,1)} %param.12), slice={[0:144], [4096:12288]} | slice | bytes 4718592 | tf_op jit(solution)/shard_map/slice | solution.py:277
  11.2 1.1 %constant_dynamic-slice_fusion.1 = (bf16[32,4,144]{2,1,0:T(4,128)(2,1)S(1)}, bf16[32,4,144]{2,1,0:T(4,128)(2,1)S(1)}) fusion(bf16[32,4,2304]{2,1,0:T(4,128)(2,1)} %param.11, s32[]{:T(128)S(6)} %select_n.36, s32[]{:T(128)S(6)} %select_n.35), kind=kLoop, calls=%fused_computation.51 | loop fusion | bytes 147464 | tf_op jit(solution)/shard_map/dynamic_slice | solution.py:259
  13.3 2.1 %collective-permute-start.2 = (bf16[4,4,768]{2,0,1:T(4,128)(2,1)S(1)}, bf16[4,4,768]{2,0,1:T(4,128)(2,1)S(1)}, u32[]{:S(2)}, u32[]{:S(2)}) collective-permute-start(bf16[4,4,768]{2,0,1:T(4,128)(2,1)S(1)} %pad_maximum_fusion.2), channel_id=1, source_target_pairs={{0,4},{1,5},{2,6},{3,7},{4,0},{5,1},{6,2},{7,3},{8,12},{9,13},{10,... | collective-permute-start | bytes 73736 | tf_op jit(solution)/shard_map/ppermute | solution.py:220
  15.6 1.7 %collective-permute-done.2 = bf16[4,4,768]{2,0,1:T(4,128)(2,1)S(1)} collective-permute-done((bf16[4,4,768]{2,0,1:T(4,128)(2,1)S(1)}, bf16[4,4,768]{2,0,1:T(4,128)(2,1)S(1)}, u32[]{:S(2)}, u32[]{:S(2)}) %collective-permute-start.2) | collective-permute-done | bytes 24608 | tf_op jit(solution)/shard_map/ppermute | solution.py:220
  17.4 3.1 %collective-permute-start.4 = (bf16[8,4,768]{2,0,1:T(8,128)(2,1)S(1)}, bf16[8,4,768]{2,0,1:T(8,128)(2,1)S(1)}, u32[]{:S(2)}, u32[]{:S(2)}) collective-permute-start(bf16[8,4,768]{2,0,1:T(8,128)(2,1)S(1)} %pad_maximum_fusion.1), channel_id=1, source_target_pairs={{0,8},{1,9},{2,10},{3,11},{4,12},{5,13},{6,14},{7,15},{8,0},{9,1},... | collective-permute-start | bytes 147464 | tf_op jit(solution)/shard_map/ppermute | solution.py:220
  20.5 2.9 %partial_product.2 = (f32[32,4096]{1,0:T(8,128)S(1)}, f32[32,4096]{1,0:T(8,128)}) custom-call(bf16[64,144]{1,0:T(8,128)(2,1)S(1)} %convolution_convert_fusion.3.mine_ref, bf16[64,144]{1,0:T(8,128)(2,1)S(1)} %convolution_convert_fusion.2.theirs_ref, bf16[144,4096]{1,0:T(8,128)(2,1)} %slice.90.block_ref, bf16[144,4096]{1,0:T(8,128)(2,1)} %collective-permute-done.3.other_ref), custom_call_target="tpu_custom_call" | custom-call | tf_op jit(solution)/shard_map/partial_product/pallas_call | solution.py:205
  23.5 1.5 %collective-permute-start.6 = (f32[32,4096]{1,0:T(8,128)}, f32[32,4096]{1,0:T(8,128)}, u32[]{:S(2)}, u32[]{:S(2)}) collective-permute-start(f32[32,4096]{1,0:T(8,128)} %get-tuple-element.63), channel_id=1, source_target_pairs={{0,2},{1,3},{2,0},{3,1},{4,6},{5,7},{6,4},{7,5},{8,10},{9,11},{10,... | collective-permute-start | bytes 1572872 | tf_op jit(solution)/shard_map/ppermute | solution.py:220
  25.0 2.5 %partial_product.3 = (f32[32,4160]{1,0:T(8,128)S(1)}, f32[32,4160]{1,0:T(8,128)S(1)}, f32[32,3072]{1,0:T(8,128)S(1)}, f32[32,3072]{1,0:T(8,128)S(1)}, f32[32,1024]{1,0:T(8,128)S(1)}, /*index=5*/f32[32,1024]{1,0:T(8,128)S(1)}) custom-call(bf16[64,144]{1,0:T(8,128)(2,1)S(1)} %convolution_convert_fusion.3.mine_ref, ...), custom_call_target="tpu_custom_call" | custom-call | tf_op jit(solution)/shard_map/partial_product/pallas_call | solution.py:205
  28.8 0.8 copy-done.5
  31.7 0.9 concatenate.30
  32.9 3.5 %collective-permute-done.6 = f32[32,4096]{1,0:T(8,128)} collective-permute-done((f32[32,4096]{1,0:T(8,128)}, f32[32,4096]{1,0:T(8,128)}, u32[]{:S(2)}, u32[]{:S(2)}) %collective-permute-start.6) | collective-permute-done | bytes 524320 | tf_op jit(solution)/shard_map/ppermute | solution.py:220
  36.5 1.1 %add.140 = f32[32,4096]{1,0:T(8,128)S(1)} add(f32[32,4096]{1,0:T(8,128)S(1)} %get-tuple-element.85, f32[32,4096]{1,0:T(8,128)} %collective-permute-done.6) | non-fusion elementwise | flops 131072 | bytes 1572864 | tf_op jit(solution)/shard_map/add | solution.py:297
  37.6 1.6 %collective-permute-start.9 = (f32[16,4096]{1,0:T(8,128)S(1)}, f32[16,4096]{1,0:T(8,128)S(1)}, u32[]{:S(2)}, u32[]{:S(2)}) collective-permute-start(f32[16,4096]{1,0:T(8,128)S(1)} %slice.122), channel_id=1, source_target_pairs={{0,4},{1,5},{2,6},{3,7},{4,0},{5,1},{6,2},{7,3},{8,12},{9,13},{10,... | collective-permute-start | bytes 786440 | tf_op jit(solution)/shard_map/ppermute | solution.py:220
  39.3 1.5 %collective-permute-start.8 = (f32[32,4160]{1,0:T(8,128)S(1)}, f32[32,4160]{1,0:T(8,128)S(1)}, u32[]{:S(2)}, u32[]{:S(2)}) collective-permute-start(f32[32,4160]{1,0:T(8,128)S(1)} %copy-done.6), channel_id=1, source_target_pairs={{0,2},{1,3},{2,0},{3,1},{4,6},{5,7},{6,4},{7,5},{8,10},{9,11},{10,... | collective-permute-start | bytes 1597448 | tf_op jit(solution)/shard_map/ppermute | solution.py:220
  41.3 1.1 %multiply_add_fusion.1 = (f32[2,1,12288]{2,0,1:T(2,128)S(1)}, f32[2,1,12288]{2,0,1:T(2,128)S(1)}, f32[2,1,12288]{2,0,1:T(2,128)S(1)}) fusion(f32[2,3,12288]{2,0,1:T(2,128)} %param.16, f32[12288]{0:T(1024)S(1)} %bitcast.24, f32[12288]{0:T(1024)S(1)} %bitcast.25, f32[12288]{0:T(1024)S(1)} %bitcast.26), kind=kLoop, calls=%fused_computation.11 | loop fusion | flops 221184 | bytes 737280 | tf_op jit(solution)/shard_map/add | solution.py:312
  42.5 1.6 %collective-permute-done.9 = f32[16,4096]{1,0:T(8,128)S(1)} collective-permute-done((f32[16,4096]{1,0:T(8,128)S(1)}, f32[16,4096]{1,0:T(8,128)S(1)}, u32[]{:S(2)}, u32[]{:S(2)}) %collective-permute-start.9) | collective-permute-done | bytes 262176 | tf_op jit(solution)/shard_map/ppermute | solution.py:220
  44.1 10.4 %collective-permute-done.8 = f32[32,4160]{1,0:T(8,128)S(1)} collective-permute-done((f32[32,4160]{1,0:T(8,128)S(1)}, f32[32,4160]{1,0:T(8,128)S(1)}, u32[]{:S(2)}, u32[]{:S(2)}) %collective-permute-start.8) | collective-permute-done | bytes 532512 | tf_op jit(solution)/shard_map/ppermute | solution.py:220
  55.1 1.5 %collective-permute-start.15 = (f32[32,1024]{1,0:T(8,128)S(1)}, f32[32,1024]{1,0:T(8,128)S(1)}, u32[]{:S(2)}, u32[]{:S(2)}) collective-permute-start(f32[32,1024]{1,0:T(8,128)S(1)} %copy-done.10), channel_id=1, source_target_pairs={{0,2},{1,3},{2,0},{3,1},{4,6},{5,7},{6,4},{7,5},{8,10},{9,11},{10,... | collective-permute-start | bytes 393224 | tf_op jit(solution)/shard_map/ppermute | solution.py:220
  57.0 3.9 %collective-permute-done.7 = f32[32,3072]{1,0:T(8,128)S(1)} collective-permute-done((f32[32,3072]{1,0:T(8,128)S(1)}, f32[32,3072]{1,0:T(8,128)S(1)}, u32[]{:S(2)}, u32[]{:S(2)}) %collective-permute-start.7) | collective-permute-done | bytes 393248 | tf_op jit(solution)/shard_map/ppermute | solution.py:220
  61.0 1.3 %collective-permute-done.15 = f32[32,1024]{1,0:T(8,128)S(1)} collective-permute-done((f32[32,1024]{1,0:T(8,128)S(1)}, f32[32,1024]{1,0:T(8,128)S(1)}, u32[]{:S(2)}, u32[]{:S(2)}) %collective-permute-start.15) | collective-permute-done | bytes 131104 | tf_op jit(solution)/shard_map/ppermute | solution.py:220
  63.1 1.4 %collective-permute-start.13 = (f32[8,4160]{1,0:T(8,128)S(1)}, f32[8,4160]{1,0:T(8,128)S(1)}, u32[]{:S(2)}, u32[]{:S(2)}) collective-permute-start(f32[8,4160]{1,0:T(8,128)S(1)} %get-tuple-element.88), channel_id=1, source_target_pairs={{0,8},{1,9},{2,10},{3,11},{4,12},{5,13},{6,14},{7,15},{8,0},{9,1},... | collective-permute-start | bytes 399368 | tf_op jit(solution)/shard_map/ppermute | solution.py:220
  64.5 6.3 %collective-permute-done.11 = f32[16,3072]{1,0:T(8,128)S(1)} collective-permute-done((f32[16,3072]{1,0:T(8,128)S(1)}, f32[16,3072]{1,0:T(8,128)S(1)}, u32[]{:S(2)}, u32[]{:S(2)}) %collective-permute-start.11) | collective-permute-done | bytes 196640 | tf_op jit(solution)/shard_map/ppermute | solution.py:220
  70.9 0.9 collective-permute-start.14
  71.8 3.3 %collective-permute-done.16 = f32[16,1024]{1,0:T(8,128)S(1)} collective-permute-done((f32[16,1024]{1,0:T(8,128)S(1)}, f32[16,1024]{1,0:T(8,128)S(1)}, u32[]{:S(2)}, u32[]{:S(2)}) %collective-permute-start.16) | collective-permute-done | bytes 65568 | tf_op jit(solution)/shard_map/ppermute | solution.py:220
  75.1 3.1 %collective-permute-done.14.refs_1_ = f32[8,3072]{1,0:T(8,128)S(1)} collective-permute-done((f32[8,3072]{1,0:T(8,128)S(1)}, f32[8,3072]{1,0:T(8,128)S(1)}, u32[]{:S(2)}, u32[]{:S(2)}) %collective-permute-start.14) | collective-permute-done | bytes 98336 | tf_op jit(solution)/shard_map/ppermute | solution.py:220
  78.8 2.2 %copy-done = f32[2,32,128,128]{3,2,1,0:T(8,128)S(1)} copy-done((f32[2,32,128,128]{3,2,1,0:T(8,128)S(1)}, f32[2,32,128,128]{3,2,1,0:T(8,128)}, u32[]{:S(2)}) %copy-start) | copy-done | bytes 4194328
  81.0 3.6 %keys_part.1 = (f32[32,8,128]{2,1,0:T(8,128)S(1)}, f32[32,8,128]{2,1,0:T(8,128)S(1)}, f32[32,8,128]{2,1,0:T(8,128)S(1)}, f32[3,32,8,128]{3,2,1,0:T(8,128)S(1)}, f32[4,32,8,128]{3,2,1,0:T(8,128)S(1)}) custom-call(f32[8,4160]{1,0:T(8,128)S(1)} %get-tuple-element.106.refs_0_, f32[8,4160]{1,0:T(8,128)S(1)} %collective-permute-done.13.refs_1_, ...), custom_call_target="tpu_custom_call" | custom-call | tf_op jit(solution)/shard_map/keys_part/pallas_call | solution.py:163
  84.6 1.1 %values_part.1 = bf16[16,16,128]{2,1,0:T(8,128)(2,1)S(1)} custom-call(s32[64]{0:T(128)S(1)} %select_reduce_fusion.slots_ref, s32[64]{0:T(128)S(1)} %get-tuple-element.119.halves_ref, s32[2]{0:T(128)S(1)} %fusion.14.lengths_ref, f32[8,3072]{1,0:T(8,128)S(1)} %get-tuple-element.111.refs_0_, f32[8,3072]{1,0:T(8,128)S(1)} %collective-permute-done.14.refs_1_, ...), custom_call_target="tpu_custom_call" | custom-call | flops 4000000 | bytes 2000000 | tf_op jit(solution)/shard_map/values_part/pallas_call | solution.py:172
  85.7 11.7 %all_to_all.5 = bf16[16,16,128]{2,1,0:T(8,128)(2,1)S(1)} all-to-all(bf16[16,16,128]{2,1,0:T(8,128)(2,1)S(1)} %values_part.1), channel_id=1, replica_groups=mesh['groups'=2,'heads'=16] {'heads'}, dimensions={0} | all-to-all | bytes 131072 | tf_op jit(solution)/shard_map/all_to_all | solution.py:330
  (100 shorter events, 11.2 us)
Async XLA Ops:
  0.0 6.8 %copy-start.17 = (s32[8]{0:T(128)S(1)}, s32[8]{0:T(128)}, u32[]{:S(2)}) copy-start(s32[8]{0:T(128)} %constant.44.clone) | copy-start | bytes 100
  0.0 6.8 %copy-start.12 = (bf16[144,64]{0,1:T(8,128)(2,1)S(1)}, bf16[144,64]{0,1:T(8,128)(2,1)}, u32[]{:S(2)}) copy-start(bf16[144,64]{0,1:T(8,128)(2,1)} %param.13) | copy-start | bytes 55300
  0.7 3.0 %collective-permute-start = (bf16[1,4,768]{2,0,1:T(2,128)(2,1)S(1)}, bf16[1,4,768]{2,0,1:T(2,128)(2,1)S(1)}, u32[]{:S(2)}, u32[]{:S(2)}) collective-permute-start(bf16[1,4,768]{2,0,1:T(2,128)(2,1)S(1)} %copy.23), channel_id=1, source_target_pairs={{0,1},{1,0},{2,3},{3,2},{4,5},{5,4},{6,7},{7,6},{8,9},{9,8},{10,11... | collective-permute-start | bytes 18440 | tf_op jit(solution)/shard_map/ppermute | solution.py:220
  3.6 16.9 %collective-permute-start.3 = (bf16[144,4096]{1,0:T(8,128)(2,1)}, bf16[144,4096]{1,0:T(8,128)(2,1)}, u32[]{:S(2)}, u32[]{:S(2)}) collective-permute-start(bf16[144,4096]{1,0:T(8,128)(2,1)} %slice.90.block_ref), channel_id=1, source_target_pairs={{0,1},{1,0},{2,3},{3,2},{4,5},{5,4},{6,7},{7,6},{8,9},{9,8},{10,11... | collective-permute-start | bytes 3538952 | tf_op jit(solution)/shard_map/ppermute | solution.py:220
  3.7 4.7 %collective-permute-start.1 = (bf16[2,4,768]{2,0,1:T(2,128)(2,1)S(1)}, bf16[2,4,768]{2,0,1:T(2,128)(2,1)S(1)}, u32[]{:S(2)}, u32[]{:S(2)}) collective-permute-start(bf16[2,4,768]{2,0,1:T(2,128)(2,1)S(1)} %pad_maximum_fusion.3), channel_id=1, source_target_pairs={{0,2},{1,3},{2,0},{3,1},{4,6},{5,7},{6,4},{7,5},{8,10},{9,11},{10,... | collective-permute-start | bytes 36872 | tf_op jit(solution)/shard_map/ppermute | solution.py:220
  10.3 0.7 copy-start.14
  10.3 2.1 %copy-start.15 = (s32[32]{0:T(128)S(1)}, s32[32]{0:T(128)}, u32[]{:S(2)}) copy-start(s32[32]{0:T(128)} %param.17) | copy-start | bytes 388
  10.4 2.5 %copy-start.16 = (s32[64]{0:T(128)S(1)}, s32[64]{0:T(128)}, u32[]{:S(2)}) copy-start(s32[64]{0:T(128)} %param.18) | copy-start | bytes 772
  10.5 14.4 %collective-permute-start.5 = (bf16[144,8256]{1,0:T(8,128)(2,1)S(1)}, bf16[144,8256]{1,0:T(8,128)(2,1)}, u32[]{:S(2)}, u32[]{:S(2)}) collective-permute-start(bf16[144,8256]{1,0:T(8,128)(2,1)S(1)} %pad_maximum_fusion.block_ref), channel_id=1, source_target_pairs={{0,1},{1,0},{2,3},{3,2},{4,5},{5,4},{6,7},{7,6},{8,9},{9,8},{10,11... | collective-permute-start | bytes 7133192 | tf_op jit(solution)/shard_map/ppermute | solution.py:220
  13.3 3.9 %collective-permute-start.2 = (bf16[4,4,768]{2,0,1:T(4,128)(2,1)S(1)}, bf16[4,4,768]{2,0,1:T(4,128)(2,1)S(1)}, u32[]{:S(2)}, u32[]{:S(2)}) collective-permute-start(bf16[4,4,768]{2,0,1:T(4,128)(2,1)S(1)} %pad_maximum_fusion.2), channel_id=1, source_target_pairs={{0,4},{1,5},{2,6},{3,7},{4,0},{5,1},{6,2},{7,3},{8,12},{9,13},{10,... | collective-permute-start | bytes 73736 | tf_op jit(solution)/shard_map/ppermute | solution.py:220
  17.4 13.7 %collective-permute-start.4 = (bf16[8,4,768]{2,0,1:T(8,128)(2,1)S(1)}, bf16[8,4,768]{2,0,1:T(8,128)(2,1)S(1)}, u32[]{:S(2)}, u32[]{:S(2)}) collective-permute-start(bf16[8,4,768]{2,0,1:T(8,128)(2,1)S(1)} %pad_maximum_fusion.1), channel_id=1, source_target_pairs={{0,8},{1,9},{2,10},{3,11},{4,12},{5,13},{6,14},{7,15},{8,0},{9,1},... | collective-permute-start | bytes 147464 | tf_op jit(solution)/shard_map/ppermute | solution.py:220
  23.5 13.0 %collective-permute-start.6 = (f32[32,4096]{1,0:T(8,128)}, f32[32,4096]{1,0:T(8,128)}, u32[]{:S(2)}, u32[]{:S(2)}) collective-permute-start(f32[32,4096]{1,0:T(8,128)} %get-tuple-element.63), channel_id=1, source_target_pairs={{0,2},{1,3},{2,0},{3,1},{4,6},{5,7},{6,4},{7,5},{8,10},{9,11},{10,... | collective-permute-start | bytes 1572872 | tf_op jit(solution)/shard_map/ppermute | solution.py:220
  27.4 0.7 copy-start.1
  28.8 0.8 copy-start.5
  29.6 0.7 copy-start.7
  31.0 8.2 %copy-start.6 = (f32[32,4160]{1,0:T(8,128)S(1)}, f32[32,4160]{1,0:T(8,128)}, u32[]{:S(2)}) copy-start(f32[32,4160]{1,0:T(8,128)} %copy-done.5) | copy-start | bytes 1597444
  31.1 9.7 %copy-start.8 = (f32[32,3072]{1,0:T(8,128)S(1)}, f32[32,3072]{1,0:T(8,128)}, u32[]{:S(2)}) copy-start(f32[32,3072]{1,0:T(8,128)} %copy-done.7) | copy-start | bytes 1179652
  37.6 17.5 %copy-start.10 = (f32[32,1024]{1,0:T(8,128)S(1)}, f32[32,1024]{1,0:T(8,128)}, u32[]{:S(2)}) copy-start(f32[32,1024]{1,0:T(8,128)} %copy-done.9) | copy-start | bytes 393220
  37.6 23.4 %copy-start.2 = (f32[32,3072]{1,0:T(8,128)S(1)}, f32[32,3072]{1,0:T(8,128)}, u32[]{:S(2)}) copy-start(f32[32,3072]{1,0:T(8,128)} %copy-done.1) | copy-start | bytes 1179652
  37.6 6.4 %collective-permute-start.9 = (f32[16,4096]{1,0:T(8,128)S(1)}, f32[16,4096]{1,0:T(8,128)S(1)}, u32[]{:S(2)}, u32[]{:S(2)}) collective-permute-start(f32[16,4096]{1,0:T(8,128)S(1)} %slice.122), channel_id=1, source_target_pairs={{0,4},{1,5},{2,6},{3,7},{4,0},{5,1},{6,2},{7,3},{8,12},{9,13},{10,... | collective-permute-start | bytes 786440 | tf_op jit(solution)/shard_map/ppermute | solution.py:220
  39.3 15.2 %collective-permute-start.8 = (f32[32,4160]{1,0:T(8,128)S(1)}, f32[32,4160]{1,0:T(8,128)S(1)}, u32[]{:S(2)}, u32[]{:S(2)}) collective-permute-start(f32[32,4160]{1,0:T(8,128)S(1)} %copy-done.6), channel_id=1, source_target_pairs={{0,2},{1,3},{2,0},{3,1},{4,6},{5,7},{6,4},{7,5},{8,10},{9,11},{10,... | collective-permute-start | bytes 1597448 | tf_op jit(solution)/shard_map/ppermute | solution.py:220
  40.8 20.2 %collective-permute-start.7 = (f32[32,3072]{1,0:T(8,128)S(1)}, f32[32,3072]{1,0:T(8,128)S(1)}, u32[]{:S(2)}, u32[]{:S(2)}) collective-permute-start(f32[32,3072]{1,0:T(8,128)S(1)} %copy-done.8), channel_id=1, source_target_pairs={{0,2},{1,3},{2,0},{3,1},{4,6},{5,7},{6,4},{7,5},{8,10},{9,11},{10,... | collective-permute-start | bytes 1179656 | tf_op jit(solution)/shard_map/ppermute | solution.py:220
  42.5 19.9 %copy-start.4 = (f32[32,1024]{1,0:T(8,128)S(1)}, f32[32,1024]{1,0:T(8,128)}, u32[]{:S(2)}) copy-start(f32[32,1024]{1,0:T(8,128)} %copy-done.3) | copy-start | bytes 393220
  54.6 7.8 %collective-permute-start.10 = (f32[16,4160]{1,0:T(8,128)S(1)}, f32[16,4160]{1,0:T(8,128)S(1)}, u32[]{:S(2)}, u32[]{:S(2)}) collective-permute-start(f32[16,4160]{1,0:T(8,128)S(1)} %slice.121), channel_id=1, source_target_pairs={{0,4},{1,5},{2,6},{3,7},{4,0},{5,1},{6,2},{7,3},{8,12},{9,13},{10,... | collective-permute-start | bytes 798728 | tf_op jit(solution)/shard_map/ppermute | solution.py:220
  55.1 7.3 %collective-permute-start.15 = (f32[32,1024]{1,0:T(8,128)S(1)}, f32[32,1024]{1,0:T(8,128)S(1)}, u32[]{:S(2)}, u32[]{:S(2)}) collective-permute-start(f32[32,1024]{1,0:T(8,128)S(1)} %copy-done.10), channel_id=1, source_target_pairs={{0,2},{1,3},{2,0},{3,1},{4,6},{5,7},{6,4},{7,5},{8,10},{9,11},{10,... | collective-permute-start | bytes 393224 | tf_op jit(solution)/shard_map/ppermute | solution.py:220
  56.7 6.4 %collective-permute-start.12 = (f32[8,4096]{1,0:T(8,128)S(1)}, f32[8,4096]{1,0:T(8,128)S(1)}, u32[]{:S(2)}, u32[]{:S(2)}) collective-permute-start(f32[8,4096]{1,0:T(8,128)S(1)} %get-tuple-element.109), channel_id=1, source_target_pairs={{0,8},{1,9},{2,10},{3,11},{4,12},{5,13},{6,14},{7,15},{8,0},{9,1},... | collective-permute-start | bytes 393224 | tf_op jit(solution)/shard_map/ppermute | solution.py:220
  62.4 8.4 %collective-permute-start.11 = (f32[16,3072]{1,0:T(8,128)S(1)}, f32[16,3072]{1,0:T(8,128)S(1)}, u32[]{:S(2)}, u32[]{:S(2)}) collective-permute-start(f32[16,3072]{1,0:T(8,128)S(1)} %slice.120), channel_id=1, source_target_pairs={{0,4},{1,5},{2,6},{3,7},{4,0},{5,1},{6,2},{7,3},{8,12},{9,13},{10,... | collective-permute-start | bytes 589832 | tf_op jit(solution)/shard_map/ppermute | solution.py:220
  63.1 7.8 %collective-permute-start.13 = (f32[8,4160]{1,0:T(8,128)S(1)}, f32[8,4160]{1,0:T(8,128)S(1)}, u32[]{:S(2)}, u32[]{:S(2)}) collective-permute-start(f32[8,4160]{1,0:T(8,128)S(1)} %get-tuple-element.88), channel_id=1, source_target_pairs={{0,8},{1,9},{2,10},{3,11},{4,12},{5,13},{6,14},{7,15},{8,0},{9,1},... | collective-permute-start | bytes 399368 | tf_op jit(solution)/shard_map/ppermute | solution.py:220
  70.8 4.3 %collective-permute-start.16 = (f32[16,1024]{1,0:T(8,128)S(1)}, f32[16,1024]{1,0:T(8,128)S(1)}, u32[]{:S(2)}, u32[]{:S(2)}) collective-permute-start(f32[16,1024]{1,0:T(8,128)S(1)} %slice.130), channel_id=1, source_target_pairs={{0,4},{1,5},{2,6},{3,7},{4,0},{5,1},{6,2},{7,3},{8,12},{9,13},{10,... | collective-permute-start | bytes 196616 | tf_op jit(solution)/shard_map/ppermute | solution.py:220
  70.9 7.3 %collective-permute-start.14 = (f32[8,3072]{1,0:T(8,128)S(1)}, f32[8,3072]{1,0:T(8,128)S(1)}, u32[]{:S(2)}, u32[]{:S(2)}) collective-permute-start(f32[8,3072]{1,0:T(8,128)S(1)} %get-tuple-element.89), channel_id=1, source_target_pairs={{0,8},{1,9},{2,10},{3,11},{4,12},{5,13},{6,14},{7,15},{8,0},{9,1},... | collective-permute-start | bytes 294920 | tf_op jit(solution)/shard_map/ppermute | solution.py:220
  78.2 6.4 %collective-permute-start.17 = (f32[8,1024]{1,0:T(8,128)S(1)}, f32[8,1024]{1,0:T(8,128)S(1)}, u32[]{:S(2)}, u32[]{:S(2)}) collective-permute-start(f32[8,1024]{1,0:T(8,128)S(1)} %get-tuple-element.94), channel_id=1, source_target_pairs={{0,8},{1,9},{2,10},{3,11},{4,12},{5,13},{6,14},{7,15},{8,0},{9,1},... | collective-permute-start | bytes 98312 | tf_op jit(solution)/shard_map/ppermute | solution.py:220
  78.8 2.2 %copy-start = (f32[2,32,128,128]{3,2,1,0:T(8,128)S(1)}, f32[2,32,128,128]{3,2,1,0:T(8,128)}, u32[]{:S(2)}) copy-start(f32[2,32,128,128]{3,2,1,0:T(8,128)} %refs_6_.1) | copy-start | bytes 12582916
  (4 other events, 2.6 us)

commit v5 on v2

--- a/solution.py
+++ b/solution.py
@@ -17,7 +17,12 @@
 LOCAL = 2
 ROWS = LOCAL * STEPS
 HEADS_WIDTH = H * DK
-PIECES = 2
+LEVELS = 32767.0
+SCALE_LANES = 128
+EXPONENT_AT = 64
+BLOCKS = HEADS_WIDTH // DK
+STATE_COPIES = 4
+
 
 norm_eps = 1e-06
 
@@ -50,11 +55,52 @@
     return value * lax.rsqrt(lane_sum(value * value) + norm_eps)
 
 
-def activate(pieces, part, head, early_ref, taps_ref, row_step):
-    per_piece = H // len(pieces)
-    kept_ref, sent_ref = pieces[head // per_piece]
-    inner = pl.ds(head % per_piece * DK, DK)
-    fresh = kept_ref[:ROWS, inner] + sent_ref[:, inner]
+def pack_rows(total, packed_ref):
+    rows, width = total.shape
+    blocks = width // DK
+    lane = lax.broadcasted_iota(jnp.int32, (rows, SCALE_LANES), 1)
+    scales = jnp.zeros((rows, SCALE_LANES), jnp.float32)
+    for block in range(blocks):
+        part = total[:, block * DK : (block + 1) * DK]
+        top = jnp.max(jnp.abs(part), axis=-1, keepdims=True) + 1e-30
+        exponent = jnp.ceil(jnp.log2(top))
+        mantissa = jnp.ceil(jnp.minimum(top * jnp.exp2(-exponent) * LEVELS, LEVELS))
+        factor = LEVELS * LEVELS * jnp.exp2(-exponent) / mantissa
+        coded = jnp.clip(jnp.floor(part * factor + 0.5), -LEVELS, LEVELS)
+        packed_ref[:, block * DK : (block + 1) * DK] = coded.astype(jnp.int32).astype(jnp.int16)
+        scales = jnp.where(lane == block, mantissa, scales)
+        scales = jnp.where(lane == EXPONENT_AT + block, exponent, scales)
+    packed_ref[:, width:] = scales.astype(jnp.int32).astype(jnp.int16)
+
+
+def to_float(coded):
+    return coded.astype(jnp.int32).astype(jnp.float32)
+
+
+def steps_of(packed_ref):
+    scales = to_float(packed_ref[:, packed_ref.shape[1] - SCALE_LANES :])
+    exponents = pltpu.roll(scales, EXPONENT_AT, 1)
+    return scales * jnp.exp2(exponents) * (1.0 / (LEVELS * LEVELS))
+
+
+def unpack_block(packed_ref, steps, block):
+    return to_float(packed_ref[:, block * DK : (block + 1) * DK]) * steps[:, block : block + 1]
+
+
+def fold_rows(value):
+    half = value.shape[1] // 2
+    return jnp.concatenate([value[:, :half], value[:, half:]], axis=0)
+
+
+def received(kept_ref, got_ref, steps, block):
+    half = kept_ref.shape[1] // DK // 2
+    rows = unpack_block(got_ref, steps, block % half)
+    rows = rows[:ROWS] if block < half else rows[ROWS:]
+    return kept_ref[:, block * DK : (block + 1) * DK] + rows
+
+
+def activate(kept_ref, got_ref, steps, part, head, early_ref, taps_ref, row_step):
+    fresh = received(kept_ref, got_ref, steps, head)
     columns = pl.ds(part * HEADS_WIDTH + head * DK, DK)
     total = early_ref[:, columns]
     for lag in range(TAPS):
@@ -63,20 +109,29 @@
     return total / (1.0 + jnp.exp(-total))
 
 
-def keys_kernel(*refs):
-    ins, outs = refs[: 4 * PIECES + 3], refs[4 * PIECES + 3 :]
-    key_refs = [(ins[2 * i], ins[2 * i + 1]) for i in range(PIECES)]
-    query_refs = [(ins[2 * i], ins[2 * i + 1]) for i in range(PIECES, 2 * PIECES)]
-    early_ref, taps_ref, state_ref = ins[4 * PIECES :]
-    beta_ref, key_seen_ref, query_seen_ref, pulls_ref, weights_ref = outs
+def keys_kernel(
+    query_ref, query_got_ref, key_ref, key_got_ref, early_ref, taps_ref, state_hbm,
+    beta_ref, key_seen_ref, query_seen_ref, pulls_ref, weights_ref, state_ref, sems,
+):
+    per_copy = H // STATE_COPIES
+    copies = []
+    for at in range(STATE_COPIES):
+        some = pl.ds(at * per_copy, per_copy)
+        copies.append(
+            pltpu.make_async_copy(state_hbm.at[:, some], state_ref.at[:, some], sems.at[at])
+        )
+        copies[-1].start()
     row = lax.broadcasted_iota(jnp.int32, (ROWS, DK), 0)
     row_step = row % STEPS
-    kept_ref, sent_ref = key_refs[0]
-    width = HEADS_WIDTH // PIECES
-    gates = kept_ref[:ROWS, width : width + 2 * H] + sent_ref[:, width : width + 2 * H]
+    query_steps, key_steps = steps_of(query_got_ref), steps_of(key_got_ref)
+    gates = received(key_ref, key_got_ref, key_steps, BLOCKS)
     for head in range(H):
-        key = unit_length(activate(key_refs, 1, head, early_ref, taps_ref, row_step))
-        query = unit_length(activate(query_refs, 0, head, early_ref, taps_ref, row_step))
+        key = unit_length(
+            activate(key_ref, key_got_ref, key_steps, 1, head, early_ref, taps_ref, row_step)
+        )
+        query = unit_length(
+            activate(query_ref, query_got_ref, query_steps, 0, head, early_ref, taps_ref, row_step)
+        )
         beta_logit = jnp.broadcast_to(gates[:, head : head + 1], (ROWS, DK))
         decay_logit = jnp.broadcast_to(gates[:, H + head : H + head + 1], (ROWS, DK))
         beta = 1.0 / (1.0 + jnp.exp(-beta_logit))
@@ -86,6 +141,8 @@
             earlier = pltpu.roll(decay, lag - 1, 0)
             fades.append(jnp.where(row_step >= lag - 1, fades[-1] * earlier, fades[-1]))
         both = jnp.concatenate([key, query], axis=0)
+        if head % per_copy == 0:
+            copies[head // per_copy].wait()
         seen = [
             jnp.dot(both, state_ref[r, head], precision=lax.Precision.HIGHEST,
                     preferred_element_type=jnp.float32)
@@ -105,19 +162,20 @@
             weights_ref[lag, head] = fades[lag] * lane_sum(query * moved_key)
 
 
-def values_kernel(slots_ref, halves_ref, lengths_ref, *refs):
-    value_refs = [(refs[2 * i], refs[2 * i + 1]) for i in range(PIECES)]
-    early_ref, taps_ref, beta_ref, key_seen_ref, query_seen_ref, pulls_ref, weights_ref = refs[
-        2 * PIECES : 2 * PIECES + 7
-    ]
-    out_ref, heads_ref = refs[2 * PIECES + 7 :]
+def values_kernel(
+    slots_ref, halves_ref, lengths_ref, value_ref, value_got_ref, early_ref, taps_ref,
+    beta_ref, key_seen_ref, query_seen_ref, pulls_ref, weights_ref, out_ref, heads_ref,
+):
     row = lax.broadcasted_iota(jnp.int32, (ROWS, DK), 0)
     row_step = row % STEPS
     lane = lax.broadcasted_iota(jnp.int32, (ROWS, DK), 1)
     row_length = jnp.where(row < STEPS, lengths_ref[0], lengths_ref[1])
     live = row_step < row_length
+    value_steps = steps_of(value_got_ref)
     for head in range(H):
-        value = activate(value_refs, 2, head, early_ref, taps_ref, row_step)
+        value = activate(
+            value_ref, value_got_ref, value_steps, 2, head, early_ref, taps_ref, row_step
+        )
         base = beta_ref[head] * value - key_seen_ref[head]
         solved = base
         for _ in range(STEPS - 1):
@@ -142,7 +200,7 @@
         out_ref[quad] = jnp.concatenate(joined, axis=0).astype(jnp.bfloat16)
 
 
-def run_delta(slots, halves, lengths, keys, queries, values, early, taps, state):
+def run_delta(slots, halves, lengths, queries, keys, values, early, taps, state):
     smem = pl.BlockSpec(memory_space=pltpu.SMEM)
     vmem = pl.BlockSpec(memory_space=pltpu.VMEM)
     params = pltpu.CompilerParams(vmem_limit_bytes=32 * 1024 * 1024)
@@ -150,26 +208,97 @@
     lags = [
         jax.ShapeDtypeStruct((count, H, ROWS, DK), jnp.float32) for count in (STEPS - 1, STEPS)
     ]
-    flat = lambda pieces: [ref for piece in pieces for ref in piece]
     prepared = pl.pallas_call(
         keys_kernel,
         out_shape=[per_head] * 3 + lags,
-        in_specs=[vmem] * (4 * PIECES + 3),
+        in_specs=[vmem] * 6 + [pl.BlockSpec(memory_space=pl.ANY)],
         out_specs=[vmem] * 5,
+        scratch_shapes=[
+            pltpu.VMEM(state.shape, jnp.float32),
+            pltpu.SemaphoreType.DMA((STATE_COPIES,)),
+        ],
         compiler_params=params,
         cost_estimate=pl.CostEstimate(flops=40_000_000, bytes_accessed=9_000_000, transcendentals=0),
         name="keys_part",
-    )(*flat(keys), *flat(queries), early, taps, state)
+    )(*queries, *keys, early, taps, state)
     return pl.pallas_call(
         values_kernel,
         out_shape=jax.ShapeDtypeStruct((UNITS // 4, 2 * ROWS, DK), jnp.bfloat16),
-        in_specs=[smem] * 3 + [vmem] * (2 * PIECES + 7),
+        in_specs=[smem] * 3 + [vmem] * 9,
         out_specs=vmem,
         scratch_shapes=[pltpu.VMEM((H, ROWS, DK), jnp.float32)],
         compiler_params=params,
         cost_estimate=pl.CostEstimate(flops=4_000_000, bytes_accessed=2_000_000, transcendentals=0),
         name="values_part",
-    )(slots, halves, lengths, *flat(values), early, taps, *prepared)
+    )(slots, halves, lengths, *values, early, taps, *prepared)
+
+
+def product_kernel(mine_ref, theirs_ref, block_ref, other_ref, *refs):
+    gate_refs, (kept_ref, packed_ref) = refs[:-2], refs[-2:]
+    half = mine_ref.shape[0] // 2
+
+    def product(own, other):
+        total = jnp.dot(mine_ref[...], own, preferred_element_type=jnp.float32)
+        return total + jnp.dot(theirs_ref[...], other, preferred_element_type=jnp.float32)
+
+    total = product(block_ref[...], other_ref[...])
+    if gate_refs:
+        gates = product(gate_refs[0][...], gate_refs[1][...])
+        zeros = jnp.zeros((gates.shape[0], 2 * DK - gates.shape[1]), jnp.float32)
+        total = jnp.concatenate([total, gates, zeros], axis=1)
+    kept_ref[...] = total[:half]
+    pack_rows(total[half:], packed_ref)
+
+
+def run_product(mine, theirs, weights, part, gates=()):
+    vmem = pl.BlockSpec(memory_space=pltpu.VMEM)
+    block = pl.BlockSpec((mine.shape[1], HEADS_WIDTH), lambda i: (0, part))
+    half = mine.shape[0] // 2
+    width = HEADS_WIDTH + len(gates) * DK
+    return pl.pallas_call(
+        product_kernel,
+        grid=(1,),
+        out_shape=[
+            jax.ShapeDtypeStruct((half, width), jnp.float32),
+            jax.ShapeDtypeStruct((half, width + SCALE_LANES), jnp.int16),
+        ],
+        in_specs=[vmem, vmem, block, block] + [vmem] * len(gates),
+        out_specs=[vmem] * 2,
+        compiler_params=pltpu.CompilerParams(vmem_limit_bytes=32 * 1024 * 1024),
+        cost_estimate=pl.CostEstimate(flops=0, bytes_accessed=0, transcendentals=0),
+        name="partial_product",
+    )(mine, theirs, *weights, *gates)
+
+
+def combine_kernel(kept_ref, got_ref, still_ref, packed_ref):
+    half = still_ref.shape[0]
+    steps = steps_of(got_ref)
+    sent = []
+    for block in range(kept_ref.shape[1] // DK):
+        columns = pl.ds(block * DK, DK)
+        total = kept_ref[:, columns] + unpack_block(got_ref, steps, block)
+        still_ref[:, columns] = total[:half]
+        sent.append(total[half:])
+    sent = jnp.concatenate(sent, axis=1)
+    pack_rows(fold_rows(sent) if half == ROWS else sent, packed_ref)
+
+
+def run_combine(kept, got):
+    vmem = pl.BlockSpec(memory_space=pltpu.VMEM)
+    half, width = kept.shape[0] // 2, kept.shape[1]
+    packed = (2 * ROWS, width // 2 + SCALE_LANES) if half == ROWS else (half, width + SCALE_LANES)
+    return pl.pallas_call(
+        combine_kernel,
+        out_shape=[
+            jax.ShapeDtypeStruct((half, width), jnp.float32),
+            jax.ShapeDtypeStruct(packed, jnp.int16),
+        ],
+        in_specs=[vmem] * 2,
+        out_specs=[vmem] * 2,
+        compiler_params=pltpu.CompilerParams(vmem_limit_bytes=32 * 1024 * 1024),
+        cost_estimate=pl.CostEstimate(flops=0, bytes_accessed=0, transcendentals=0),
+        name="combine",
+    )(kept, got)
 
 
 def swap(value, bit, devices):
@@ -206,45 +335,48 @@
         order.append(offset)
     holders = jnp.bitwise_xor(jnp.asarray(order, jnp.int32), me)
     old_rows = (holders[:, None] * LOCAL + jnp.arange(LOCAL, dtype=jnp.int32)[None, :]).reshape(-1)
-    flat_tokens = tokens.reshape(row_count * STEPS, D)
     steps = jnp.arange(STEPS, dtype=jnp.int32)
     wanted = (old_rows[:, None] * STEPS + steps[None, :]).reshape(-1)
     offered = (slot_of[:, None] * STEPS + steps[None, :]).reshape(-1)
     picker = (wanted[:, None] == offered[None, :]).astype(jnp.bfloat16)
 
     def token_part(owner):
-        columns = lax.dynamic_slice_in_dim(flat_tokens, owner * depth, depth, 1)
+        columns = lax.dynamic_slice_in_dim(tokens, owner * depth, depth, 2)
+        columns = columns.reshape(row_count * STEPS, depth)
         return jnp.dot(picker, columns, preferred_element_type=jnp.float32).astype(jnp.bfloat16)
 
     mine, theirs = token_part(me), token_part(jnp.bitwise_xor(me, 1))
-    half_rows = chips * ROWS // 2
-
-    width = HEADS_WIDTH // PIECES
-    chunks, others = [], []
-    weight = qkv_weight
-    for part in (1, 0, 2):
-        for piece in range(PIECES):
-            begin = part * HEADS_WIDTH + piece * width
-            block = weight[:, begin : begin + width]
-            if not chunks:
-                block = jnp.concatenate([block, gate_weight], axis=1)
-            block, weight = lax.optimization_barrier((block, weight))
-            chunks.append(block)
-            others.append(swap(block, 1, devices))
-
-    pieces = []
-    for block, other in zip(chunks, others):
-        total = jnp.dot(mine, block, preferred_element_type=jnp.float32)
-        total = total + jnp.dot(theirs, other, preferred_element_type=jnp.float32)
-        for bit in bits[:-1]:
-            half = total.shape[0] // 2
-            total = total[:half] + swap(total[half:], bit, devices)
-        pieces.append((total, swap(total[ROWS:], bits[-1], devices)))
-    keys, queries, values = (pieces[i * PIECES : (i + 1) * PIECES] for i in range(3))
-
-    gathered = conv_weight[None]
-    for b in range(devices.bit_length() - 1):
-        gathered = jnp.concatenate([gathered, swap(gathered, 1 << b, devices)], axis=0)
+
+    weights = (qkv_weight, swap(qkv_weight, 1, devices))
+    gates = (gate_weight, swap(gate_weight, 1, devices))
+
+    def in_order(value, *earlier):
+        return lax.optimization_barrier((value,) + earlier)[0]
+
+    def widen(gathered, unit, count):
+        others = [swap(gathered, unit * i, devices) for i in range(1, count)]
+        return jnp.concatenate([gathered] + others, axis=0)
+
+    near = widen(conv_weight[None], 1, 4)
+    gathered = widen(near, 4, devices // 4)
+    mine = in_order(mine, near)
+    query = run_product(mine, theirs, weights, 0)
+    query = (query[0], in_order(query[1], gathered))
+    mine = in_order(mine, *query)
+    key = run_product(mine, theirs, weights, 1, gates)
+    mine = in_order(mine, *key)
+    value = run_product(mine, theirs, weights, 2)
+
+    chunks = [query, key, value]
+    got = [swap(packed, bits[0], devices) for _, packed in chunks]
+    got[0] = in_order(got[0], *value)
+    for level, bit in enumerate(bits[1:]):
+        for at in range(len(chunks)):
+            arrived = in_order(got[at], *chunks[at - 1]) if at else got[at]
+            chunks[at] = run_combine(chunks[at][0], arrived)
+            got[at] = swap(chunks[at][1], bit, devices)
+    queries, keys, values = [(kept, came) for (kept, _), came in zip(chunks, got)]
+
     places = jnp.arange(devices, dtype=jnp.int32)
     sorter = (jnp.bitwise_xor(places, me)[:, None] == places[None, :]).astype(jnp.bfloat16)
     taps = jnp.einsum("aj,jtc->tac", sorter, gathered, preferred_element_type=jnp.float32)
@@ -263,7 +395,7 @@
         jnp.where(slot_of[None, :] == my_rows[:, None], lengths[None, :], 0), axis=1
     )
     local_out = run_delta(
-        old_slots, halves, my_lengths, keys, queries, values, early, taps, delta_state
+        old_slots, halves, my_lengths, queries, keys, values, early, taps, delta_state
     )
 
     placer = (offered[:, None] == jnp.arange(row_count * STEPS, dtype=jnp.int32)[None, :]).astype(

time: 122 us -> 90.1 us (0.74)
  starting transfers between devices: 36.5 us -> 14.8 us
  matrix products: 17.1 us -> 4.6 us
  waiting for transfers between devices: 33.4 us -> 21.2 us
  Pallas kernels: 4.7 us -> 12 us
  local copies, waits for them, and re-layouts: 12.7 us -> 19.1 us
    ppermute x28 -> x17, starting transfers between devices: 36.5 us -> 14.8 us  [swap(): return lax.ppermute(value, 'heads', [(i, i ^ bit) for i in range(devices)])]
    dot_general x12 -> x0, matrix products: 14.7 us -> none  [the longest x6 9.07 us: on_device(): total = jnp.dot(mine, block, preferred_element_type=jnp.float32)]
    ppermute x28 -> x17, waiting for transfers between devices: 33.4 us -> 21.2 us  [swap(): return lax.ppermute(value, 'heads', [(i, i ^ bit) for i in range(devices)])]
    pallas_call x0 -> x9, Pallas kernels: none -> 6.2 us  [the longest x3 3.4 us: run_product(): pl.pallas_call(product_kernel, grid=(1,), out_shape=[jax.ShapeDtypeStruct...]
    slice x25 -> x0, local copies, waits for them, and re-layouts: 5.68 us -> none  [the longest x7 5.46 us: on_device(): block = weight[:, begin:begin + width]]
    reshape x1 -> x2, local copies, waits for them, and re-layouts: 0.14 us -> 3.03 us  [token_part(): columns = columns.reshape(row_count * STEPS, depth)]
    unnamed x48 -> x20, local copies, waits for them, and re-layouts: 4.55 us -> 7.28 us
    concatenate x4 -> x1, other arithmetic: 3.14 us -> 0.83 us  [widen(): return jnp.concatenate([gathered] + others, axis=0)]
  transfers between devices with their start and end apart: 28 -> 17, of which waited for: 13 -> 8; matrix products, arithmetic and copies ran while one was open for 19% -> 26% of each run, Pallas kernels for 3% -> 12%
where the time goes in v5:
time: 90.1 us; the launch traced here: 89.1 us
  waiting for transfers between devices  21.2 us (24%)
  local copies, waits for them, and re-layouts  19.1 us (21%)
  starting transfers between devices  14.8 us (16%)
  Pallas kernels  12 us (13%)
  blocking collectives  10.8 us (12%)
  other arithmetic  6.27 us (7%)
  matrix products  4.6 us (5%)
    ppermute x17, waiting for transfers between devices, swap(): return lax.ppermute(value, 'heads', [(i, i ^ bit) for i in range(devices)])  21.2 us
    ppermute x17, starting transfers between devices, swap(): return lax.ppermute(value, 'heads', [(i, i ^ bit) for i in range(devices)])  14.8 us
    all_to_all x1, blocking collectives, on_device(): lax.all_to_all(sending, 'heads', split_axis=0, concat_axis=0, tiled=True)  10.8 us
    unnamed x20, local copies, waits for them, and re-layouts  7.28 us
    pallas_call x1, Pallas kernels, run_delta(): pl.pallas_call(keys_kernel, out_shape=[per_head] * 3 + lags, in_specs=[vm...  4.66 us
    pallas_call x3, Pallas kernels, run_product(): pl.pallas_call(product_kernel, grid=(1,), out_shape=[jax.ShapeDtypeStruct...  3.4 us
    dot_general x2, matrix products, token_part(): jnp.dot(picker, columns, preferred_element_type=jnp.float32)  3.28 us
    reshape x2, local copies, waits for them, and re-layouts, token_part(): columns = columns.reshape(row_count * STEPS, depth)  3.03 us
  transfers between devices with their start and end apart: 17, of which 8 were waited for; matrix products, arithmetic and copies ran while one was open for 26% of the time, Pallas kernels for 12%

profile of v5, /device:TPU:0, one launch (start us, length us, event | category | flops | bytes accessed | tf_op | source)
XLA Modules:
  0.0 89.1 jit_solution(17134770046886207490)
XLA Ops:
  0.5 1.3 %copy.26 = bf16[1,4,768]{2,0,1:T(2,128)(2,1)} copy(bf16[1,4,768]{2,1,0:T(4,128)(2,1)} %bitcast.27) | data formatting | bytes 12288 | tf_op jit(solution)/shard_map/broadcast_in_dim | solution.py:360
  1.8 2.6 %collective-permute-start.2 = (bf16[1,4,768]{2,0,1:T(2,128)(2,1)}, bf16[1,4,768]{2,0,1:T(2,128)(2,1)}, u32[]{:S(2)}, u32[]{:S(2)}) collective-permute-start(bf16[1,4,768]{2,0,1:T(2,128)(2,1)} %copy.26), channel_id=1, source_target_pairs={{0,3},{1,2},{2,1},{3,0},{4,7},{5,6},{6,5},{7,4},{8,11},{9,10},{10,... | collective-permute-start | bytes 18440 | tf_op jit(solution)/shard_map/ppermute | solution.py:305
  4.5 1.5 %copy.29.refs_0_ = bf16[144,64]{1,0:T(8,128)(2,1)} copy(bf16[144,64]{0,1:T(8,128)(2,1)} %param.13) | data formatting | bytes 36864 | tf_op args[2]
  6.4 1.8 %constant_dynamic-slice_fusion.1 = (bf16[32,4,144]{2,1,0:T(4,128)(2,1)}, bf16[32,4,144]{2,1,0:T(4,128)(2,1)}) fusion(bf16[32,4,2304]{2,1,0:T(4,128)(2,1)} %param.11, s32[]{:T(128)S(6)} %select_n.36, s32[]{:T(128)S(6)} %select_n.35), kind=kLoop, calls=%fused_computation.44 | loop fusion | bytes 147464 | tf_op jit(solution)/shard_map/dynamic_slice | solution.py:344
  8.1 1.5 %reshape.134 = bf16[128,144]{1,0:T(8,128)(2,1)} reshape(bf16[32,4,144]{2,1,0:T(4,128)(2,1)} %get-tuple-element.70) | data formatting | bytes 73728 | tf_op jit(solution)/shard_map/reshape | solution.py:345
  12.8 1.5 %reshape.135 = bf16[128,144]{1,0:T(8,128)(2,1)} reshape(bf16[32,4,144]{2,1,0:T(4,128)(2,1)} %get-tuple-element.69) | data formatting | bytes 73728 | tf_op jit(solution)/shard_map/reshape | solution.py:345
  15.1 0.9 fusion.14.lengths_ref
  16.6 1.6 %convolution_convert_fusion.3.mine_ref = bf16[64,144]{1,0:T(8,128)(2,1)} fusion(bf16[128,144]{1,0:T(8,128)(2,1)} %reshape.134, s32[128]{0:T(128)S(1)} %add.101, s32[64]{0:T(128)S(1)} %add.111), kind=kOutput, calls=%fused_computation.4 | convolution fusion | flops 2376704 | bytes 56064 | tf_op jit(solution)/shard_map/dot_general | solution.py:346
  18.3 1.6 %convolution_convert_fusion.2.theirs_ref = bf16[64,144]{1,0:T(8,128)(2,1)} fusion(bf16[128,144]{1,0:T(8,128)(2,1)} %reshape.135, s32[128]{0:T(128)S(1)} %add.101, s32[64]{0:T(128)S(1)} %add.111), kind=kOutput, calls=%fused_computation.3 | convolution fusion | flops 2376704 | bytes 56064 | tf_op jit(solution)/shard_map/dot_general | solution.py:346
  20.8 2.1 %collective-permute-start.4 = (bf16[4,4,768]{2,0,1:T(4,128)(2,1)S(1)}, bf16[4,4,768]{2,0,1:T(4,128)(2,1)}, u32[]{:S(2)}, u32[]{:S(2)}) collective-permute-start(bf16[4,4,768]{2,0,1:T(4,128)(2,1)S(1)} %pad_maximum_fusion), channel_id=1, source_target_pairs={{0,4},{1,5},{2,6},{3,7},{4,0},{5,1},{6,2},{7,3},{8,12},{9,13},{10,... | collective-permute-start | bytes 73736 | tf_op jit(solution)/shard_map/ppermute | solution.py:305
  23.0 2.6 %collective-permute-start.5 = (bf16[4,4,768]{2,0,1:T(4,128)(2,1)S(1)}, bf16[4,4,768]{2,0,1:T(4,128)(2,1)}, u32[]{:S(2)}, u32[]{:S(2)}) collective-permute-start(bf16[4,4,768]{2,0,1:T(4,128)(2,1)S(1)} %pad_maximum_fusion), channel_id=1, source_target_pairs={{0,8},{1,9},{2,10},{3,11},{4,12},{5,13},{6,14},{7,15},{8,0},{9,1},... | collective-permute-start | bytes 73736 | tf_op jit(solution)/shard_map/ppermute | solution.py:305
  26.8 1.3 %collective-permute-done.5 = bf16[4,4,768]{2,0,1:T(4,128)(2,1)} collective-permute-done((bf16[4,4,768]{2,0,1:T(4,128)(2,1)S(1)}, bf16[4,4,768]{2,0,1:T(4,128)(2,1)}, u32[]{:S(2)}, u32[]{:S(2)}) %collective-permute-start.5) | collective-permute-done | bytes 24608 | tf_op jit(solution)/shard_map/ppermute | solution.py:305
  28.1 3.2 %collective-permute-done.6 = bf16[4,4,768]{2,0,1:T(4,128)(2,1)} collective-permute-done((bf16[4,4,768]{2,0,1:T(4,128)(2,1)S(1)}, bf16[4,4,768]{2,0,1:T(4,128)(2,1)}, u32[]{:S(2)}, u32[]{:S(2)}) %collective-permute-start.6) | collective-permute-done | bytes 24608 | tf_op jit(solution)/shard_map/ppermute | solution.py:305
  31.3 2.9 %concatenate.16 = bf16[16,4,768]{2,0,1:T(8,128)(2,1)} concatenate(bf16[1,4,768]{2,0,1:T(2,128)(2,1)} %copy.26, bf16[1,4,768]{2,0,1:T(2,128)(2,1)} %collective-permute-done, bf16[1,4,768]{2,0,1:T(2,128)(2,1)} %collective-permute-done.1, bf16[1,4,768]{2,0,1:T(2,128)(2,1)} %collective-permute-done.2, bf16[4,4,768]{2,0,1:T(4,128)(2,1)} %collective-permute-done.4, ...), dimensions={0} | concatenate | bytes 196608 | tf_op jit(solution)/shard_map/concatenate | solution.py:358
  34.2 1.1 %fusion = bf16[1,4,16,768]{3,2,1,0:T(8,128)(2,1)S(1)} fusion(bf16[16,4,768]{2,0,1:T(8,128)(2,1)} %concatenate.16, s32[16]{0:T(128)} %iota_xor_fusion), kind=kOutput, calls=%fused_computation.1 | convolution fusion | flops 1622272 | bytes 196672 | tf_op jit(solution)/shard_map/aj,jtc->tac/dot_general | solution.py:382
  35.4 2.0 %copy-done = bf16[144,12288]{1,0:T(8,128)(2,1)S(1)} copy-done((bf16[144,12288]{1,0:T(8,128)(2,1)S(1)}, bf16[144,12288]{1,0:T(8,128)(2,1)}, u32[]{:S(2)}) %copy-start) | copy-done | bytes 3538968
  39.8 1.6 %collective-permute-start.10 = (s16[32,4224]{1,0:T(8,128)(2,1)S(1)}, s16[32,4224]{1,0:T(8,128)(2,1)S(1)}, u32[]{:S(2)}, u32[]{:S(2)}) collective-permute-start(s16[32,4224]{1,0:T(8,128)(2,1)S(1)} %get-tuple-element.40), channel_id=1, source_target_pairs={{0,2},{1,3},{2,0},{3,1},{4,6},{5,7},{6,4},{7,5},{8,10},{9,11},{10,... | collective-permute-start | bytes 811016 | tf_op jit(solution)/shard_map/ppermute | solution.py:305
  41.4 1.7 %partial_product.4 = (f32[32,4352]{1,0:T(8,128)S(1)}, s16[32,4480]{1,0:T(8,128)(2,1)S(1)}) custom-call(bf16[64,144]{1,0:T(8,128)(2,1)S(1)} %copy-done.4, bf16[64,144]{1,0:T(8,128)(2,1)S(1)} %copy-done.5, bf16[144,12288]{1,0:T(8,128)(2,1)S(1)} %copy-done, bf16[144,12288]{1,0:T(8,128)(2,1)S(1)} %collective-permute-done.3.other_ref, ...), custom_call_target="tpu_custom_call" | custom-call | tf_op jit(solution)/shard_map/partial_product/pallas_call | solution.py:258
  43.7 0.8 partial_product.5
  44.5 1.6 %collective-permute-start.8 = (s16[32,4224]{1,0:T(8,128)(2,1)S(1)}, s16[32,4224]{1,0:T(8,128)(2,1)S(1)}, u32[]{:S(2)}, u32[]{:S(2)}) collective-permute-start(s16[32,4224]{1,0:T(8,128)(2,1)S(1)} %get-tuple-element.46), channel_id=1, source_target_pairs={{0,2},{1,3},{2,0},{3,1},{4,6},{5,7},{6,4},{7,5},{8,10},{9,11},{10,... | collective-permute-start | bytes 811016 | tf_op jit(solution)/shard_map/ppermute | solution.py:305
  46.3 3.0 %collective-permute-done.10.got_ref = s16[32,4224]{1,0:T(8,128)(2,1)S(1)} collective-permute-done((s16[32,4224]{1,0:T(8,128)(2,1)S(1)}, s16[32,4224]{1,0:T(8,128)(2,1)S(1)}, u32[]{:S(2)}, u32[]{:S(2)}) %collective-permute-start.10) | collective-permute-done | bytes 270368 | tf_op jit(solution)/shard_map/ppermute | solution.py:305
  49.9 5.5 %collective-permute-done.9.got_ref = s16[32,4480]{1,0:T(8,128)(2,1)S(1)} collective-permute-done((s16[32,4480]{1,0:T(8,128)(2,1)S(1)}, s16[32,4480]{1,0:T(8,128)(2,1)S(1)}, u32[]{:S(2)}, u32[]{:S(2)}) %collective-permute-start.9) | collective-permute-done | bytes 286752 | tf_op jit(solution)/shard_map/ppermute | solution.py:305
  56.0 2.4 %collective-permute-done.8.got_ref = s16[32,4224]{1,0:T(8,128)(2,1)S(1)} collective-permute-done((s16[32,4224]{1,0:T(8,128)(2,1)S(1)}, s16[32,4224]{1,0:T(8,128)(2,1)S(1)}, u32[]{:S(2)}, u32[]{:S(2)}) %collective-permute-start.8) | collective-permute-done | bytes 270368 | tf_op jit(solution)/shard_map/ppermute | solution.py:305
  59.7 1.2 %collective-permute-start.15 = (s16[16,2176]{1,0:T(8,128)(2,1)S(1)}, s16[16,2176]{1,0:T(8,128)(2,1)S(1)}, u32[]{:S(2)}, u32[]{:S(2)}) collective-permute-start(s16[16,2176]{1,0:T(8,128)(2,1)S(1)} %get-tuple-element.57), channel_id=1, source_target_pairs={{0,8},{1,9},{2,10},{3,11},{4,12},{5,13},{6,14},{7,15},{8,0},{9,1},... | collective-permute-start | bytes 208904 | tf_op jit(solution)/shard_map/ppermute | solution.py:305
  60.8 2.7 %collective-permute-done.12.got_ref = s16[16,4480]{1,0:T(8,128)(2,1)S(1)} collective-permute-done((s16[16,4480]{1,0:T(8,128)(2,1)S(1)}, s16[16,4480]{1,0:T(8,128)(2,1)S(1)}, u32[]{:S(2)}, u32[]{:S(2)}) %collective-permute-start.12) | collective-permute-done | bytes 143392 | tf_op jit(solution)/shard_map/ppermute | solution.py:305
  64.1 1.7 %collective-permute-done.11.got_ref = s16[16,4224]{1,0:T(8,128)(2,1)S(1)} collective-permute-done((s16[16,4224]{1,0:T(8,128)(2,1)S(1)}, s16[16,4224]{1,0:T(8,128)(2,1)S(1)}, u32[]{:S(2)}, u32[]{:S(2)}) %collective-permute-start.11) | collective-permute-done | bytes 135200 | tf_op jit(solution)/shard_map/ppermute | solution.py:305
  66.2 1.3 %collective-permute-start.14 = (s16[16,2176]{1,0:T(8,128)(2,1)S(1)}, s16[16,2176]{1,0:T(8,128)(2,1)S(1)}, u32[]{:S(2)}, u32[]{:S(2)}) collective-permute-start(s16[16,2176]{1,0:T(8,128)(2,1)S(1)} %get-tuple-element.63), channel_id=1, source_target_pairs={{0,8},{1,9},{2,10},{3,11},{4,12},{5,13},{6,14},{7,15},{8,0},{9,1},... | collective-permute-start | bytes 208904 | tf_op jit(solution)/shard_map/ppermute | solution.py:305
  68.1 1.2 %collective-permute-done.16.key_got_ref = s16[16,2304]{1,0:T(8,128)(2,1)S(1)} collective-permute-done((s16[16,2304]{1,0:T(8,128)(2,1)S(1)}, s16[16,2304]{1,0:T(8,128)(2,1)S(1)}, u32[]{:S(2)}, u32[]{:S(2)}) %collective-permute-start.16) | collective-permute-done | bytes 73760 | tf_op jit(solution)/shard_map/ppermute | solution.py:305
  69.3 2.2 %copy-done.1 = f32[2,32,128,128]{3,2,1,0:T(8,128)S(1)} copy-done((f32[2,32,128,128]{3,2,1,0:T(8,128)S(1)}, f32[2,32,128,128]{3,2,1,0:T(8,128)}, u32[]{:S(2)}) %copy-start.1) | copy-done | bytes 4194328
  71.5 4.7 %keys_part.1 = (f32[32,8,128]{2,1,0:T(8,128)S(1)}, f32[32,8,128]{2,1,0:T(8,128)S(1)}, f32[32,8,128]{2,1,0:T(8,128)S(1)}, f32[3,32,8,128]{3,2,1,0:T(8,128)S(1)}, f32[4,32,8,128]{3,2,1,0:T(8,128)S(1)}) custom-call(f32[8,4096]{1,0:T(8,128)S(1)} %get-tuple-element.56.query_ref, s16[16,2176]{1,0:T(8,128)(2,1)S(1)} %collective-permute-done.15.query_got_ref, ...), custom_call_target="tpu_custom_call" | custom-call | flops 40000000 | bytes 9000000 | tf_op jit(solution)/shard_map/keys_part/pallas_call | solution.py:211
  76.2 1.2 %values_part.1 = bf16[16,16,128]{2,1,0:T(8,128)(2,1)S(1)} custom-call(s32[64]{0:T(128)S(1)} %select_reduce_fusion.slots_ref, s32[64]{0:T(128)S(1)} %get-tuple-element.79.halves_ref, s32[2]{0:T(128)S(1)} %fusion.14.lengths_ref, f32[8,4096]{1,0:T(8,128)S(1)} %get-tuple-element.62.value_ref, s16[16,2176]{1,0:T(8,128)(2,1)S(1)} %collective-permute-done.14.value_got_ref, ...), custom_call_target="tpu_custom_call" | custom-call | flops 4000000 | bytes 2000000 | tf_op jit(solution)/shard_map/values_part/pallas_call | solution.py:224
  77.4 10.8 %all_to_all.5 = bf16[16,16,128]{2,1,0:T(8,128)(2,1)S(1)} all-to-all(bf16[16,16,128]{2,1,0:T(8,128)(2,1)S(1)} %values_part.1), channel_id=1, replica_groups=mesh['groups'=2,'heads'=16] {'heads'}, dimensions={0} | all-to-all | bytes 131072 | tf_op jit(solution)/shard_map/all_to_all | solution.py:407
  (66 shorter events, 15.5 us)
Async XLA Ops:
  0.0 35.4 %collective-permute-start.3 = (bf16[144,12288]{1,0:T(8,128)(2,1)}, bf16[144,12288]{1,0:T(8,128)(2,1)S(1)}, u32[]{:S(2)}, u32[]{:S(2)}) collective-permute-start(bf16[144,12288]{1,0:T(8,128)(2,1)} %block_ref.5), channel_id=1, source_target_pairs={{0,1},{1,0},{2,3},{3,2},{4,5},{5,4},{6,7},{7,6},{8,9},{9,8},{10,11... | collective-permute-start | bytes 10616840 | tf_op jit(solution)/shard_map/ppermute | solution.py:305
  1.8 18.2 %collective-permute-start.2 = (bf16[1,4,768]{2,0,1:T(2,128)(2,1)}, bf16[1,4,768]{2,0,1:T(2,128)(2,1)}, u32[]{:S(2)}, u32[]{:S(2)}) collective-permute-start(bf16[1,4,768]{2,0,1:T(2,128)(2,1)} %copy.26), channel_id=1, source_target_pairs={{0,3},{1,2},{2,1},{3,0},{4,7},{5,6},{6,5},{7,4},{8,11},{9,10},{10,... | collective-permute-start | bytes 18440 | tf_op jit(solution)/shard_map/ppermute | solution.py:305
  4.4 15.6 %collective-permute-start.1 = (bf16[1,4,768]{2,0,1:T(2,128)(2,1)}, bf16[1,4,768]{2,0,1:T(2,128)(2,1)}, u32[]{:S(2)}, u32[]{:S(2)}) collective-permute-start(bf16[1,4,768]{2,0,1:T(2,128)(2,1)} %copy.26), channel_id=1, source_target_pairs={{0,2},{1,3},{2,0},{3,1},{4,6},{5,7},{6,4},{7,5},{8,10},{9,11},{10,... | collective-permute-start | bytes 18440 | tf_op jit(solution)/shard_map/ppermute | solution.py:305
  4.4 15.6 %collective-permute-start = (bf16[1,4,768]{2,0,1:T(2,128)(2,1)}, bf16[1,4,768]{2,0,1:T(2,128)(2,1)}, u32[]{:S(2)}, u32[]{:S(2)}) collective-permute-start(bf16[1,4,768]{2,0,1:T(2,128)(2,1)} %copy.26), channel_id=1, source_target_pairs={{0,1},{1,0},{2,3},{3,2},{4,5},{5,4},{6,7},{7,6},{8,9},{9,8},{10,11... | collective-permute-start | bytes 18440 | tf_op jit(solution)/shard_map/ppermute | solution.py:305
  6.0 35.4 %collective-permute-start.7 = (bf16[144,64]{1,0:T(8,128)(2,1)}, bf16[144,64]{1,0:T(8,128)(2,1)}, u32[]{:S(2)}, u32[]{:S(2)}) collective-permute-start(bf16[144,64]{1,0:T(8,128)(2,1)} %copy.29.refs_0_), channel_id=1, source_target_pairs={{0,1},{1,0},{2,3},{3,2},{4,5},{5,4},{6,7},{7,6},{8,9},{9,8},{10,11... | collective-permute-start | bytes 55304 | tf_op jit(solution)/shard_map/ppermute | solution.py:305
  20.8 6.0 %collective-permute-start.4 = (bf16[4,4,768]{2,0,1:T(4,128)(2,1)S(1)}, bf16[4,4,768]{2,0,1:T(4,128)(2,1)}, u32[]{:S(2)}, u32[]{:S(2)}) collective-permute-start(bf16[4,4,768]{2,0,1:T(4,128)(2,1)S(1)} %pad_maximum_fusion), channel_id=1, source_target_pairs={{0,4},{1,5},{2,6},{3,7},{4,0},{5,1},{6,2},{7,3},{8,12},{9,13},{10,... | collective-permute-start | bytes 73736 | tf_op jit(solution)/shard_map/ppermute | solution.py:305
  23.0 5.2 %collective-permute-start.5 = (bf16[4,4,768]{2,0,1:T(4,128)(2,1)S(1)}, bf16[4,4,768]{2,0,1:T(4,128)(2,1)}, u32[]{:S(2)}, u32[]{:S(2)}) collective-permute-start(bf16[4,4,768]{2,0,1:T(4,128)(2,1)S(1)} %pad_maximum_fusion), channel_id=1, source_target_pairs={{0,8},{1,9},{2,10},{3,11},{4,12},{5,13},{6,14},{7,15},{8,0},{9,1},... | collective-permute-start | bytes 73736 | tf_op jit(solution)/shard_map/ppermute | solution.py:305
  25.6 5.7 %collective-permute-start.6 = (bf16[4,4,768]{2,0,1:T(4,128)(2,1)S(1)}, bf16[4,4,768]{2,0,1:T(4,128)(2,1)}, u32[]{:S(2)}, u32[]{:S(2)}) collective-permute-start(bf16[4,4,768]{2,0,1:T(4,128)(2,1)S(1)} %pad_maximum_fusion), channel_id=1, source_target_pairs={{0,12},{1,13},{2,14},{3,15},{4,8},{5,9},{6,10},{7,11},{8,4},{9,5},... | collective-permute-start | bytes 73736 | tf_op jit(solution)/shard_map/ppermute | solution.py:305
  35.4 10.8 %copy-start.2 = (bf16[1,4,16,768]{3,1,2,0:T(4,128)(2,1)}, bf16[1,4,16,768]{3,1,2,0:T(4,128)(2,1)S(1)}, u32[]{:S(2)}) copy-start(bf16[1,4,16,768]{3,1,2,0:T(4,128)(2,1)S(1)} %copy.31) | copy-start | bytes 294916
  35.4 2.0 %copy-start = (bf16[144,12288]{1,0:T(8,128)(2,1)S(1)}, bf16[144,12288]{1,0:T(8,128)(2,1)}, u32[]{:S(2)}) copy-start(bf16[144,12288]{1,0:T(8,128)(2,1)} %block_ref.5) | copy-start | bytes 10616836
  37.4 0.8 copy-start.4
  38.2 0.8 copy-start.5
  39.0 2.4 %copy-start.6 = (bf16[144,64]{1,0:T(8,128)(2,1)S(1)}, bf16[144,64]{1,0:T(8,128)(2,1)}, u32[]{:S(2)}) copy-start(bf16[144,64]{1,0:T(8,128)(2,1)} %copy.29.refs_0_) | copy-start | bytes 55300
  39.8 9.5 %collective-permute-start.10 = (s16[32,4224]{1,0:T(8,128)(2,1)S(1)}, s16[32,4224]{1,0:T(8,128)(2,1)S(1)}, u32[]{:S(2)}, u32[]{:S(2)}) collective-permute-start(s16[32,4224]{1,0:T(8,128)(2,1)S(1)} %get-tuple-element.40), channel_id=1, source_target_pairs={{0,2},{1,3},{2,0},{3,1},{4,6},{5,7},{6,4},{7,5},{8,10},{9,11},{10,... | collective-permute-start | bytes 811016 | tf_op jit(solution)/shard_map/ppermute | solution.py:305
  43.1 12.3 %collective-permute-start.9 = (s16[32,4480]{1,0:T(8,128)(2,1)S(1)}, s16[32,4480]{1,0:T(8,128)(2,1)S(1)}, u32[]{:S(2)}, u32[]{:S(2)}) collective-permute-start(s16[32,4480]{1,0:T(8,128)(2,1)S(1)} %get-tuple-element.43), channel_id=1, source_target_pairs={{0,2},{1,3},{2,0},{3,1},{4,6},{5,7},{6,4},{7,5},{8,10},{9,11},{10,... | collective-permute-start | bytes 860168 | tf_op jit(solution)/shard_map/ppermute | solution.py:305
  43.7 15.4 %copy-start.7 = (f32[2,3,12288]{2,0,1:T(2,128)S(1)}, f32[2,3,12288]{2,0,1:T(2,128)}, u32[]{:S(2)}) copy-start(f32[2,3,12288]{2,0,1:T(2,128)} %param.16) | copy-start | bytes 884740
  44.5 22.9 %copy-start.8 = (f32[4]{0:T(128)S(1)}, f32[4]{0:T(128)}, u32[]{:S(2)}) copy-start(f32[4]{0:T(128)} %pad.5.clone) | copy-start | bytes 52
  44.5 13.9 %collective-permute-start.8 = (s16[32,4224]{1,0:T(8,128)(2,1)S(1)}, s16[32,4224]{1,0:T(8,128)(2,1)S(1)}, u32[]{:S(2)}, u32[]{:S(2)}) collective-permute-start(s16[32,4224]{1,0:T(8,128)(2,1)S(1)} %get-tuple-element.46), channel_id=1, source_target_pairs={{0,2},{1,3},{2,0},{3,1},{4,6},{5,7},{6,4},{7,5},{8,10},{9,11},{10,... | collective-permute-start | bytes 811016 | tf_op jit(solution)/shard_map/ppermute | solution.py:305
  46.2 23.1 %copy-start.3 = (bf16[1,4,16,768]{3,1,2,0:T(4,128)(2,1)S(1)}, bf16[1,4,16,768]{3,1,2,0:T(4,128)(2,1)}, u32[]{:S(2)}) copy-start(bf16[1,4,16,768]{3,1,2,0:T(4,128)(2,1)} %copy-done.2) | copy-start | bytes 294916
  49.8 9.4 %collective-permute-start.13 = (s16[16,4224]{1,0:T(8,128)(2,1)S(1)}, s16[16,4224]{1,0:T(8,128)(2,1)S(1)}, u32[]{:S(2)}, u32[]{:S(2)}) collective-permute-start(s16[16,4224]{1,0:T(8,128)(2,1)S(1)} %get-tuple-element.49), channel_id=1, source_target_pairs={{0,4},{1,5},{2,6},{3,7},{4,0},{5,1},{6,2},{7,3},{8,12},{9,13},{10,... | collective-permute-start | bytes 405512 | tf_op jit(solution)/shard_map/ppermute | solution.py:305
  56.0 7.6 %collective-permute-start.12 = (s16[16,4480]{1,0:T(8,128)(2,1)S(1)}, s16[16,4480]{1,0:T(8,128)(2,1)S(1)}, u32[]{:S(2)}, u32[]{:S(2)}) collective-permute-start(s16[16,4480]{1,0:T(8,128)(2,1)S(1)} %get-tuple-element.52), channel_id=1, source_target_pairs={{0,4},{1,5},{2,6},{3,7},{4,0},{5,1},{6,2},{7,3},{8,12},{9,13},{10,... | collective-permute-start | bytes 430088 | tf_op jit(solution)/shard_map/ppermute | solution.py:305
  59.0 6.8 %collective-permute-start.11 = (s16[16,4224]{1,0:T(8,128)(2,1)S(1)}, s16[16,4224]{1,0:T(8,128)(2,1)S(1)}, u32[]{:S(2)}, u32[]{:S(2)}) collective-permute-start(s16[16,4224]{1,0:T(8,128)(2,1)S(1)} %get-tuple-element.55), channel_id=1, source_target_pairs={{0,4},{1,5},{2,6},{3,7},{4,0},{5,1},{6,2},{7,3},{8,12},{9,13},{10,... | collective-permute-start | bytes 405512 | tf_op jit(solution)/shard_map/ppermute | solution.py:305
  59.7 8.4 %collective-permute-start.15 = (s16[16,2176]{1,0:T(8,128)(2,1)S(1)}, s16[16,2176]{1,0:T(8,128)(2,1)S(1)}, u32[]{:S(2)}, u32[]{:S(2)}) collective-permute-start(s16[16,2176]{1,0:T(8,128)(2,1)S(1)} %get-tuple-element.57), channel_id=1, source_target_pairs={{0,8},{1,9},{2,10},{3,11},{4,12},{5,13},{6,14},{7,15},{8,0},{9,1},... | collective-permute-start | bytes 208904 | tf_op jit(solution)/shard_map/ppermute | solution.py:305
  64.0 5.3 %collective-permute-start.16 = (s16[16,2304]{1,0:T(8,128)(2,1)S(1)}, s16[16,2304]{1,0:T(8,128)(2,1)S(1)}, u32[]{:S(2)}, u32[]{:S(2)}) collective-permute-start(s16[16,2304]{1,0:T(8,128)(2,1)S(1)} %get-tuple-element.60), channel_id=1, source_target_pairs={{0,8},{1,9},{2,10},{3,11},{4,12},{5,13},{6,14},{7,15},{8,0},{9,1},... | collective-permute-start | bytes 221192 | tf_op jit(solution)/shard_map/ppermute | solution.py:305
  66.2 10.0 %collective-permute-start.14 = (s16[16,2176]{1,0:T(8,128)(2,1)S(1)}, s16[16,2176]{1,0:T(8,128)(2,1)S(1)}, u32[]{:S(2)}, u32[]{:S(2)}) collective-permute-start(s16[16,2176]{1,0:T(8,128)(2,1)S(1)} %get-tuple-element.63), channel_id=1, source_target_pairs={{0,8},{1,9},{2,10},{3,11},{4,12},{5,13},{6,14},{7,15},{8,0},{9,1},... | collective-permute-start | bytes 208904 | tf_op jit(solution)/shard_map/ppermute | solution.py:305
  69.3 2.2 %copy-start.1 = (f32[2,32,128,128]{3,2,1,0:T(8,128)S(1)}, f32[2,32,128,128]{3,2,1,0:T(8,128)}, u32[]{:S(2)}) copy-start(f32[2,32,128,128]{3,2,1,0:T(8,128)} %state_hbm.1) | copy-start | bytes 12582916

commit v6 on v5

--- a/solution.py
+++ b/solution.py
@@ -21,7 +21,7 @@
 SCALE_LANES = 128
 EXPONENT_AT = 64
 BLOCKS = HEADS_WIDTH // DK
-STATE_COPIES = 4
+WEIGHT_COPIES = 2
 
 
 norm_eps = 1e-06
@@ -109,18 +109,36 @@
     return total / (1.0 + jnp.exp(-total))
 
 
+def state_kernel(state_ref, high_ref, low_ref):
+    for r in range(LOCAL):
+        for at in range(state_ref.shape[1]):
+            value = state_ref[r, at]
+            high = value.astype(jnp.bfloat16)
+            high_ref[at, :, r * DK : (r + 1) * DK] = high
+            low = (value - high.astype(jnp.float32)).astype(jnp.bfloat16)
+            low_ref[at, :, r * DK : (r + 1) * DK] = low
+
+
+def run_state(state):
+    heads = H // 4
+    out = jax.ShapeDtypeStruct((H, DK, LOCAL * DK), jnp.bfloat16)
+    spec = pl.BlockSpec((heads, DK, LOCAL * DK), lambda i: (i, 0, 0))
+    return pl.pallas_call(
+        state_kernel,
+        grid=(4,),
+        out_shape=[out, out],
+        in_specs=[pl.BlockSpec((LOCAL, heads, DK, DK), lambda i: (0, i, 0, 0))],
+        out_specs=[spec, spec],
+        compiler_params=pltpu.CompilerParams(vmem_limit_bytes=32 * 1024 * 1024),
+        cost_estimate=pl.CostEstimate(flops=0, bytes_accessed=0, transcendentals=0),
+        name="state_parts",
+    )(state)
+
+
 def keys_kernel(
-    query_ref, query_got_ref, key_ref, key_got_ref, early_ref, taps_ref, state_hbm,
-    beta_ref, key_seen_ref, query_seen_ref, pulls_ref, weights_ref, state_ref, sems,
+    query_ref, query_got_ref, key_ref, key_got_ref, early_ref, taps_ref, high_ref, low_ref,
+    beta_ref, key_seen_ref, query_seen_ref, pulls_ref, weights_ref,
 ):
-    per_copy = H // STATE_COPIES
-    copies = []
-    for at in range(STATE_COPIES):
-        some = pl.ds(at * per_copy, per_copy)
-        copies.append(
-            pltpu.make_async_copy(state_hbm.at[:, some], state_ref.at[:, some], sems.at[at])
-        )
-        copies[-1].start()
     row = lax.broadcasted_iota(jnp.int32, (ROWS, DK), 0)
     row_step = row % STEPS
     query_steps, key_steps = steps_of(query_got_ref), steps_of(key_got_ref)
@@ -141,13 +159,13 @@
             earlier = pltpu.roll(decay, lag - 1, 0)
             fades.append(jnp.where(row_step >= lag - 1, fades[-1] * earlier, fades[-1]))
         both = jnp.concatenate([key, query], axis=0)
-        if head % per_copy == 0:
-            copies[head // per_copy].wait()
-        seen = [
-            jnp.dot(both, state_ref[r, head], precision=lax.Precision.HIGHEST,
-                    preferred_element_type=jnp.float32)
-            for r in range(LOCAL)
-        ]
+        both_high = both.astype(jnp.bfloat16)
+        both_low = (both - both_high.astype(jnp.float32)).astype(jnp.bfloat16)
+        stacked = jnp.concatenate([both_high, both_low], axis=0)
+        main = jnp.dot(stacked, high_ref[head], preferred_element_type=jnp.float32)
+        rest = jnp.dot(both_high, low_ref[head], preferred_element_type=jnp.float32)
+        seen = main[: 2 * ROWS] + main[2 * ROWS :] + rest
+        seen = [seen[:, r * DK : (r + 1) * DK] for r in range(LOCAL)]
         beta_ref[head] = beta
         key_seen_ref[head] = beta * fades[STEPS] * jnp.where(
             row < STEPS, seen[0][:ROWS], seen[1][:ROWS]
@@ -211,16 +229,12 @@
     prepared = pl.pallas_call(
         keys_kernel,
         out_shape=[per_head] * 3 + lags,
-        in_specs=[vmem] * 6 + [pl.BlockSpec(memory_space=pl.ANY)],
+        in_specs=[vmem] * 8,
         out_specs=[vmem] * 5,
-        scratch_shapes=[
-            pltpu.VMEM(state.shape, jnp.float32),
-            pltpu.SemaphoreType.DMA((STATE_COPIES,)),
-        ],
         compiler_params=params,
         cost_estimate=pl.CostEstimate(flops=40_000_000, bytes_accessed=9_000_000, transcendentals=0),
         name="keys_part",
-    )(*queries, *keys, early, taps, state)
+    )(*queries, *keys, early, taps, *state)
     return pl.pallas_call(
         values_kernel,
         out_shape=jax.ShapeDtypeStruct((UNITS // 4, 2 * ROWS, DK), jnp.bfloat16),
@@ -233,37 +247,107 @@
     )(slots, halves, lengths, *values, early, taps, *prepared)
 
 
-def product_kernel(mine_ref, theirs_ref, block_ref, other_ref, *refs):
-    gate_refs, (kept_ref, packed_ref) = refs[:-2], refs[-2:]
+def rows_kernel(
+    depth, me_ref, slot_of_ref, tokens_hbm, mine_ref, theirs_ref, window_ref, sem
+):
+    me = me_ref[0]
+    width = window_ref.shape[2]
+    offset = me // 2 * (2 * depth)
+    start = jnp.minimum(offset // DK * DK, D - width)
+    columns = pl.ds(pl.multiple_of(start, DK), width)
+    copy = pltpu.make_async_copy(tokens_hbm.at[:, :, columns], window_ref, sem)
+    copy.start()
+    shape = (mine_ref.shape[0], slot_of_ref.shape[1])
+    row = lax.broadcasted_iota(jnp.int32, shape, 0)
+    place = row // ROWS
+    count = (shape[0] // ROWS).bit_length() - 1
+    holder = jnp.zeros(shape, jnp.int32)
+    for at in range(count):
+        holder = holder + ((place >> (count - 1 - at)) & 1) * (2 << at)
+    holder = jnp.bitwise_xor(holder, me)
+    match = holder * LOCAL + row % ROWS // STEPS == slot_of_ref[...]
+    copy.wait()
+    window = window_ref[...].astype(jnp.float32)
+    total = jnp.zeros((shape[0], width), jnp.float32)
+    for step in range(STEPS):
+        picker = jnp.where(match & (row % STEPS == step), 1.0, 0.0).astype(jnp.bfloat16)
+        here = window[:, step, :].astype(jnp.bfloat16)
+        total = total + jnp.dot(picker, here, preferred_element_type=jnp.float32)
+    total = pltpu.roll(total, lax.rem(width - (offset - start), width), 1)
+    low, high = total[:, :depth], total[:, depth : 2 * depth]
+    first_core = me % 2 == 0
+    mine_ref[...] = jnp.where(first_core, low, high).astype(jnp.bfloat16)
+    theirs_ref[...] = jnp.where(first_core, high, low).astype(jnp.bfloat16)
+
+
+def run_rows(me, slot_of, tokens, depth, chips):
+    width = -(-(2 * depth + DK - 1) // DK) * DK
+    out = jax.ShapeDtypeStruct((chips * ROWS, depth), jnp.bfloat16)
+    vmem = pl.BlockSpec(memory_space=pltpu.VMEM)
+    return pl.pallas_call(
+        functools.partial(rows_kernel, depth),
+        out_shape=[out, out],
+        in_specs=[
+            pl.BlockSpec(memory_space=pltpu.SMEM), vmem, pl.BlockSpec(memory_space=pltpu.HBM)
+        ],
+        out_specs=[vmem, vmem],
+        scratch_shapes=[
+            pltpu.VMEM((tokens.shape[0], STEPS, width), jnp.bfloat16),
+            pltpu.SemaphoreType.DMA,
+        ],
+        compiler_params=pltpu.CompilerParams(vmem_limit_bytes=32 * 1024 * 1024),
+        cost_estimate=pl.CostEstimate(flops=0, bytes_accessed=0, transcendentals=0),
+        name="token_rows",
+    )(me.reshape(1), slot_of.reshape(1, -1), tokens)
+
+
+def product_kernel(part, mine_ref, theirs_ref, own_hbm, other_hbm, *refs):
+    gate_refs, (kept_ref, packed_ref, own_ref, other_ref, sems) = refs[:-5], refs[-5:]
     half = mine_ref.shape[0] // 2
+    step = HEADS_WIDTH // WEIGHT_COPIES
+    copies = []
+    for at in range(WEIGHT_COPIES):
+        source, target = pl.ds(part * HEADS_WIDTH + at * step, step), pl.ds(at * step, step)
+        pair = [
+            pltpu.make_async_copy(hbm.at[:, source], ref.at[:, target], sems.at[side, at])
+            for side, (hbm, ref) in enumerate(((own_hbm, own_ref), (other_hbm, other_ref)))
+        ]
+        for copy in pair:
+            copy.start()
+        copies.append(pair)
 
     def product(own, other):
         total = jnp.dot(mine_ref[...], own, preferred_element_type=jnp.float32)
         return total + jnp.dot(theirs_ref[...], other, preferred_element_type=jnp.float32)
 
-    total = product(block_ref[...], other_ref[...])
+    totals = []
+    for at in range(WEIGHT_COPIES):
+        for copy in copies[at]:
+            copy.wait()
+        columns = pl.ds(at * step, step)
+        totals.append(product(own_ref[:, columns], other_ref[:, columns]))
     if gate_refs:
         gates = product(gate_refs[0][...], gate_refs[1][...])
-        zeros = jnp.zeros((gates.shape[0], 2 * DK - gates.shape[1]), jnp.float32)
-        total = jnp.concatenate([total, gates, zeros], axis=1)
+        totals += [gates, jnp.zeros((gates.shape[0], 2 * DK - gates.shape[1]), jnp.float32)]
+    total = jnp.concatenate(totals, axis=1)
     kept_ref[...] = total[:half]
     pack_rows(total[half:], packed_ref)
 
 
 def run_product(mine, theirs, weights, part, gates=()):
-    vmem = pl.BlockSpec(memory_space=pltpu.VMEM)
-    block = pl.BlockSpec((mine.shape[1], HEADS_WIDTH), lambda i: (0, part))
+    vmem, hbm = pl.BlockSpec(memory_space=pltpu.VMEM), pl.BlockSpec(memory_space=pltpu.HBM)
     half = mine.shape[0] // 2
     width = HEADS_WIDTH + len(gates) * DK
     return pl.pallas_call(
-        product_kernel,
-        grid=(1,),
+        functools.partial(product_kernel, part),
         out_shape=[
             jax.ShapeDtypeStruct((half, width), jnp.float32),
             jax.ShapeDtypeStruct((half, width + SCALE_LANES), jnp.int16),
         ],
-        in_specs=[vmem, vmem, block, block] + [vmem] * len(gates),
+        in_specs=[vmem, vmem, hbm, hbm] + [vmem] * len(gates),
         out_specs=[vmem] * 2,
+        scratch_shapes=[pltpu.VMEM((mine.shape[1], HEADS_WIDTH), jnp.bfloat16)] * 2
+        + [pltpu.SemaphoreType.DMA((2, WEIGHT_COPIES))],
         compiler_params=pltpu.CompilerParams(vmem_limit_bytes=32 * 1024 * 1024),
         cost_estimate=pl.CostEstimate(flops=0, bytes_accessed=0, transcendentals=0),
         name="partial_product",
@@ -326,26 +410,10 @@
 
     old_slots, halves = unit_tables(old_heads, new_units)
     bits = [1 << b for b in range(1, devices.bit_length() - 1)]
-    order = []
-    for place in range(chips):
-        offset = 0
-        for at, bit in enumerate(bits):
-            if place & (chips >> (at + 1)):
-                offset |= bit
-        order.append(offset)
-    holders = jnp.bitwise_xor(jnp.asarray(order, jnp.int32), me)
-    old_rows = (holders[:, None] * LOCAL + jnp.arange(LOCAL, dtype=jnp.int32)[None, :]).reshape(-1)
     steps = jnp.arange(STEPS, dtype=jnp.int32)
-    wanted = (old_rows[:, None] * STEPS + steps[None, :]).reshape(-1)
     offered = (slot_of[:, None] * STEPS + steps[None, :]).reshape(-1)
-    picker = (wanted[:, None] == offered[None, :]).astype(jnp.bfloat16)
-
-    def token_part(owner):
-        columns = lax.dynamic_slice_in_dim(tokens, owner * depth, depth, 2)
-        columns = columns.reshape(row_count * STEPS, depth)
-        return jnp.dot(picker, columns, preferred_element_type=jnp.float32).astype(jnp.bfloat16)
-
-    mine, theirs = token_part(me), token_part(jnp.bitwise_xor(me, 1))
+
+    mine, theirs = run_rows(me, slot_of, tokens, depth, chips)
 
     weights = (qkv_weight, swap(qkv_weight, 1, devices))
     gates = (gate_weight, swap(gate_weight, 1, devices))
@@ -353,34 +421,15 @@
     def in_order(value, *earlier):
         return lax.optimization_barrier((value,) + earlier)[0]
 
-    def widen(gathered, unit, count):
-        others = [swap(gathered, unit * i, devices) for i in range(1, count)]
-        return jnp.concatenate([gathered] + others, axis=0)
-
-    near = widen(conv_weight[None], 1, 4)
-    gathered = widen(near, 4, devices // 4)
-    mine = in_order(mine, near)
     query = run_product(mine, theirs, weights, 0)
-    query = (query[0], in_order(query[1], gathered))
     mine = in_order(mine, *query)
     key = run_product(mine, theirs, weights, 1, gates)
     mine = in_order(mine, *key)
     value = run_product(mine, theirs, weights, 2)
 
-    chunks = [query, key, value]
-    got = [swap(packed, bits[0], devices) for _, packed in chunks]
-    got[0] = in_order(got[0], *value)
-    for level, bit in enumerate(bits[1:]):
-        for at in range(len(chunks)):
-            arrived = in_order(got[at], *chunks[at - 1]) if at else got[at]
-            chunks[at] = run_combine(chunks[at][0], arrived)
-            got[at] = swap(chunks[at][1], bit, devices)
-    queries, keys, values = [(kept, came) for (kept, _), came in zip(chunks, got)]
-
-    places = jnp.arange(devices, dtype=jnp.int32)
-    sorter = (jnp.bitwise_xor(places, me)[:, None] == places[None, :]).astype(jnp.bfloat16)
-    taps = jnp.einsum("aj,jtc->tac", sorter, gathered, preferred_element_type=jnp.float32)
-    taps = taps.astype(jnp.bfloat16).reshape(TAPS, 3 * HEADS_WIDTH)
+    state = run_state(in_order(delta_state, *value))
+    taps = in_order(lax.all_gather(conv_weight, "heads", axis=0), *state)
+    taps = taps.transpose(1, 0, 2).reshape(TAPS, 3 * HEADS_WIDTH)
     taps_f = taps.astype(jnp.float32)
     early = []
     for step in range(STEPS):
@@ -390,12 +439,23 @@
         early.append(term)
     early = jnp.stack(early, axis=1).reshape(ROWS, 3 * HEADS_WIDTH)
 
+    chunks = [query, key, value]
+    got = [swap(packed, bits[0], devices) for _, packed in chunks]
+    got[0] = in_order(got[0], *value, *state)
+    got[1] = in_order(got[1], early)
+    for level, bit in enumerate(bits[1:]):
+        for at in range(len(chunks)):
+            arrived = in_order(got[at], *chunks[at - 1]) if at else got[at]
+            chunks[at] = run_combine(chunks[at][0], arrived)
+            got[at] = swap(chunks[at][1], bit, devices)
+    queries, keys, values = [(kept, came) for (kept, _), came in zip(chunks, got)]
+
     my_rows = me * LOCAL + jnp.arange(LOCAL, dtype=jnp.int32)
     my_lengths = jnp.sum(
         jnp.where(slot_of[None, :] == my_rows[:, None], lengths[None, :], 0), axis=1
     )
     local_out = run_delta(
-        old_slots, halves, my_lengths, queries, keys, values, early, taps, delta_state
+        old_slots, halves, my_lengths, queries, keys, values, early, taps, state
     )
 
     placer = (offered[:, None] == jnp.arange(row_count * STEPS, dtype=jnp.int32)[None, :]).astype(

time: 90.1 us -> 88 us (0.977)
  blocking collectives: 10.8 us -> 25 us
  Pallas kernels: 12 us -> 18.6 us
  local copies, waits for them, and re-layouts: 19.1 us -> 13 us
  waiting for transfers between devices: 21.2 us -> 16.7 us
  matrix products: 4.6 us -> 0.21 us
  starting transfers between devices: 14.8 us -> 10.7 us
  other arithmetic: 6.27 us -> 2.79 us
    all_gather x0 -> x1, blocking collectives: none -> 25 us  [on_device(): taps = in_order(lax.all_gather(conv_weight, 'heads', axis=0), *state)]
    ppermute x17 -> x11, waiting for transfers between devices: 21.2 us -> 10.1 us  [swap(): return lax.ppermute(value, 'heads', [(i, i ^ bit) for i in range(devices)])]
    all_to_all x1 -> x0, blocking collectives: 10.8 us -> none  [on_device(): lax.all_to_all(sending, 'heads', split_axis=0, concat_axis=0, tiled=True)]
    ppermute x17 -> x11, starting transfers between devices: 14.8 us -> 7.17 us  [swap(): return lax.ppermute(value, 'heads', [(i, i ^ bit) for i in range(devices)])]
    all_to_all x0 -> x1, waiting for transfers between devices: none -> 6.68 us  [on_device(): lax.all_to_all(sending, 'heads', split_axis=0, concat_axis=0, tiled=True)]
    pallas_call x3 -> x5, Pallas kernels: 3.4 us -> 8.05 us  [the longest x3 6.21 us: run_product(): pl.pallas_call(functools.partial(product_kernel, part), out_shape=[jax.Sh...]
    dot_general x3 -> x0, matrix products: 4.39 us -> none  [the longest x2 3.28 us: token_part(): jnp.dot(picker, columns, preferred_element_type=jnp.float32)]
    all_to_all x0 -> x1, starting transfers between devices: none -> 3.5 us  [on_device(): lax.all_to_all(sending, 'heads', split_axis=0, concat_axis=0, tiled=True)]
  transfers between devices with their start and end apart: 17 -> 12, of which waited for: 8 -> 7; matrix products, arithmetic and copies ran while one was open for 26% -> 8% of each run, Pallas kernels for 12% -> 19%
where the time goes in v6:
time: 88 us; the launch traced here: 87.3 us
  blocking collectives  25 us (28%)
  Pallas kernels  18.6 us (21%)
  waiting for transfers between devices  16.7 us (19%)
  local copies, waits for them, and re-layouts  13 us (15%)
  starting transfers between devices  10.7 us (12%)
  other arithmetic  2.79 us (3%)
    all_gather x1, blocking collectives, on_device(): taps = in_order(lax.all_gather(conv_weight, 'heads', axis=0), *state)  25 us
    ppermute x11, waiting for transfers between devices, swap(): return lax.ppermute(value, 'heads', [(i, i ^ bit) for i in range(devices)])  10.1 us
    unnamed x35, local copies, waits for them, and re-layouts  9.94 us
    ppermute x11, starting transfers between devices, swap(): return lax.ppermute(value, 'heads', [(i, i ^ bit) for i in range(devices)])  7.17 us
    all_to_all x1, waiting for transfers between devices, on_device(): lax.all_to_all(sending, 'heads', split_axis=0, concat_axis=0, tiled=True)  6.68 us
    pallas_call x3, Pallas kernels, run_product(): pl.pallas_call(functools.partial(product_kernel, part), out_shape=[jax.Sh...  6.21 us
    pallas_call x6, Pallas kernels, run_combine(): pl.pallas_call(combine_kernel, out_shape=[jax.ShapeDtypeStruct((half, wid...  4.71 us
    pallas_call x1, Pallas kernels, run_delta(): pl.pallas_call(keys_kernel, out_shape=[per_head] * 3 + lags, in_specs=[vm...  3.99 us
  transfers between devices with their start and end apart: 12, of which 7 were waited for; matrix products, arithmetic and copies ran while one was open for 8% of the time, Pallas kernels for 19%

profile of v6, /device:TPU:0, one launch (start us, length us, event | category | flops | bytes accessed | tf_op | source)
XLA Modules:
  0.0 87.3 jit_solution(1046086993854316624)
XLA Ops:
  0.5 1.5 %copy.21.refs_0_ = bf16[144,64]{1,0:T(8,128)(2,1)} copy(bf16[144,64]{0,1:T(8,128)(2,1)} %param.12) | data formatting | bytes 36864 | tf_op args[2]
  2.0 0.8 select_reduce_fusion.1
  2.8 0.7 broadcast_multiply_fusion
  3.4 0.7 and_select_fusion
  4.1 25.0 %all-gather.1 = bf16[16,4,768]{2,1,0:T(4,128)(2,1)} all-gather(bf16[1,4,768]{2,1,0:T(4,128)(2,1)} %bitcast.23), channel_id=2, replica_groups=mesh['groups'=2,'heads'=16] {'heads'}, dimensions={0}, use_global_device_ids=true | all-gather | bytes 104448 | tf_op jit(solution)/shard_map/all_gather | solution.py:431
  29.1 1.1 %copy-done.5 = bf16[32,4,2304]{2,1,0:T(4,128)(2,1)S(1)} copy-done((bf16[32,4,2304]{2,1,0:T(4,128)(2,1)S(1)}, bf16[32,4,2304]{2,1,0:T(4,128)(2,1)}, u32[]{:S(2)}) %copy-start.5) | copy-done | bytes 589848
  30.9 0.8 token_rows.1
  31.7 2.0 %copy-done = bf16[144,12288]{1,0:T(8,128)(2,1)S(1)} copy-done((bf16[144,12288]{1,0:T(8,128)(2,1)S(1)}, bf16[144,12288]{1,0:T(8,128)(2,1)}, u32[]{:S(2)}) %copy-start) | copy-done | bytes 3538968
  33.7 1.8 %partial_product.3 = (f32[32,4096]{1,0:T(8,128)S(1)}, s16[32,4224]{1,0:T(8,128)(2,1)}) custom-call(bf16[64,144]{1,0:T(8,128)(2,1)S(1)} %get-tuple-element.49.mine_ref, bf16[64,144]{1,0:T(8,128)(2,1)S(1)} %get-tuple-element.43.theirs_ref, bf16[144,12288]{1,0:T(8,128)(2,1)S(1)} %copy-done, bf16[144,12288]{1,0:T(8,128)(2,1)S(1)} %collective-permute-done.other_hbm), custom_call_target="tpu_custom_call" | custom-call | tf_op jit(solution)/shard_map/partial_product/pallas_call | solution.py:341
  35.6 2.6 %partial_product.4 = (f32[32,4352]{1,0:T(8,128)S(1)}, s16[32,4480]{1,0:T(8,128)(2,1)}) custom-call(bf16[64,144]{1,0:T(8,128)(2,1)S(1)} %get-tuple-element.49.mine_ref, bf16[64,144]{1,0:T(8,128)(2,1)S(1)} %get-tuple-element.43.theirs_ref, bf16[144,12288]{1,0:T(8,128)(2,1)S(1)} %copy-done, bf16[144,12288]{1,0:T(8,128)(2,1)S(1)} %collective-permute-done.other_hbm, ...), custom_call_target="tpu_custom_call" | custom-call | tf_op jit(solution)/shard_map/partial_product/pallas_call | solution.py:341
  38.3 0.8 copy-done.6
  39.1 2.0 %collective-permute-start.3 = (s16[32,4480]{1,0:T(8,128)(2,1)}, s16[32,4480]{1,0:T(8,128)(2,1)}, u32[]{:S(2)}, u32[]{:S(2)}) collective-permute-start(s16[32,4480]{1,0:T(8,128)(2,1)} %get-tuple-element.48), channel_id=1, source_target_pairs={{0,2},{1,3},{2,0},{3,1},{4,6},{5,7},{6,4},{7,5},{8,10},{9,11},{10,... | collective-permute-start | bytes 860168 | tf_op jit(solution)/shard_map/ppermute | solution.py:389
  41.0 1.8 %partial_product.5 = (f32[32,4096]{1,0:T(8,128)S(1)}, s16[32,4224]{1,0:T(8,128)(2,1)}) custom-call(bf16[64,144]{1,0:T(8,128)(2,1)S(1)} %get-tuple-element.49.mine_ref, bf16[64,144]{1,0:T(8,128)(2,1)S(1)} %get-tuple-element.43.theirs_ref, bf16[144,12288]{1,0:T(8,128)(2,1)S(1)} %copy-done, bf16[144,12288]{1,0:T(8,128)(2,1)S(1)} %collective-permute-done.other_hbm), custom_call_target="tpu_custom_call" | custom-call | tf_op jit(solution)/shard_map/partial_product/pallas_call | solution.py:341
  43.3 1.0 %state_parts.1 = (bf16[32,128,256]{2,1,0:T(8,128)(2,1)S(1)}, bf16[32,128,256]{2,1,0:T(8,128)(2,1)S(1)}) custom-call(f32[2,32,128,128]{3,2,1,0:T(8,128)S(1)} %copy-done.1), custom_call_target="tpu_custom_call" | custom-call | tf_op jit(solution)/shard_map/state_parts/pallas_call | solution.py:126
  44.4 1.3 %copy-done.2 = bf16[32,128,256]{2,1,0:T(8,128)(2,1)} copy-done((bf16[32,128,256]{2,1,0:T(8,128)(2,1)}, bf16[32,128,256]{2,1,0:T(8,128)(2,1)S(1)}, u32[]{:S(2)}) %copy-start.2) | copy-done | bytes 2097176
  46.2 1.0 %copy.22 = f32[2,4,12288]{2,1,0:T(4,128)} copy(f32[2,4,12288]{2,0,1:T(2,128)S(1)} %maximum_maximum_fusion) | data formatting | bytes 786432 | tf_op jit(solution)/shard_map/stack | solution.py:440
  47.2 1.1 %reshape.84.early_ref = f32[8,12288]{1,0:T(8,128)S(1)} reshape(f32[2,4,12288]{2,1,0:T(4,128)} %copy.22) | data formatting | bytes 786432 | tf_op jit(solution)/shard_map/reshape | solution.py:440
  48.4 1.2 %copy-done.11 = f32[32,4096]{1,0:T(8,128)S(1)} copy-done((f32[32,4096]{1,0:T(8,128)S(1)}, f32[32,4096]{1,0:T(8,128)}, u32[]{:S(2)}) %copy-start.11) | copy-done | bytes 524312
  49.6 1.5 %combine.6 = (f32[16,4096]{1,0:T(8,128)S(1)}, s16[16,4224]{1,0:T(8,128)(2,1)S(1)}) custom-call(f32[32,4096]{1,0:T(8,128)S(1)} %copy-done.11, s16[32,4224]{1,0:T(8,128)(2,1)} %collective-permute-done.4.got_ref), custom_call_target="tpu_custom_call" | custom-call | tf_op jit(solution)/shard_map/combine/pallas_call | solution.py:374
  51.3 1.5 %combine.7 = (f32[16,4352]{1,0:T(8,128)S(1)}, s16[16,4480]{1,0:T(8,128)(2,1)S(1)}) custom-call(f32[32,4352]{1,0:T(8,128)S(1)} %copy-done.7, s16[32,4480]{1,0:T(8,128)(2,1)} %collective-permute-done.3.got_ref), custom_call_target="tpu_custom_call" | custom-call | tf_op jit(solution)/shard_map/combine/pallas_call | solution.py:374
  52.8 1.9 %collective-permute-start.6 = (s16[16,4480]{1,0:T(8,128)(2,1)S(1)}, s16[16,4480]{1,0:T(8,128)(2,1)S(1)}, u32[]{:S(2)}, u32[]{:S(2)}) collective-permute-start(s16[16,4480]{1,0:T(8,128)(2,1)S(1)} %get-tuple-element.62), channel_id=1, source_target_pairs={{0,4},{1,5},{2,6},{3,7},{4,0},{5,1},{6,2},{7,3},{8,12},{9,13},{10,... | collective-permute-start | bytes 430088 | tf_op jit(solution)/shard_map/ppermute | solution.py:389
  54.7 1.7 %collective-permute-done.2.got_ref = s16[32,4224]{1,0:T(8,128)(2,1)S(1)} collective-permute-done((s16[32,4224]{1,0:T(8,128)(2,1)}, s16[32,4224]{1,0:T(8,128)(2,1)S(1)}, u32[]{:S(2)}, u32[]{:S(2)}) %collective-permute-start.2) | collective-permute-done | bytes 270368 | tf_op jit(solution)/shard_map/ppermute | solution.py:389
  56.4 1.0 %copy-done.9 = f32[32,4096]{1,0:T(8,128)S(1)} copy-done((f32[32,4096]{1,0:T(8,128)S(1)}, f32[32,4096]{1,0:T(8,128)}, u32[]{:S(2)}) %copy-start.9) | copy-done | bytes 524312
  59.9 2.3 %collective-permute-start.10 = (s16[16,2304]{1,0:T(8,128)(2,1)S(1)}, s16[16,2304]{1,0:T(8,128)(2,1)S(1)}, u32[]{:S(2)}, u32[]{:S(2)}) collective-permute-start(s16[16,2304]{1,0:T(8,128)(2,1)S(1)} %get-tuple-element.70), channel_id=1, source_target_pairs={{0,8},{1,9},{2,10},{3,11},{4,12},{5,13},{6,14},{7,15},{8,0},{9,1},... | collective-permute-start | bytes 221192 | tf_op jit(solution)/shard_map/ppermute | solution.py:389
  62.2 2.1 %collective-permute-done.5.got_ref = s16[16,4224]{1,0:T(8,128)(2,1)S(1)} collective-permute-done((s16[16,4224]{1,0:T(8,128)(2,1)S(1)}, s16[16,4224]{1,0:T(8,128)(2,1)S(1)}, u32[]{:S(2)}, u32[]{:S(2)}) %collective-permute-start.5) | collective-permute-done | bytes 135200 | tf_op jit(solution)/shard_map/ppermute | solution.py:389
  64.9 3.5 %collective-permute-done.9.query_got_ref = s16[16,2176]{1,0:T(8,128)(2,1)S(1)} collective-permute-done((s16[16,2176]{1,0:T(8,128)(2,1)S(1)}, s16[16,2176]{1,0:T(8,128)(2,1)S(1)}, u32[]{:S(2)}, u32[]{:S(2)}) %collective-permute-start.9) | collective-permute-done | bytes 69664 | tf_op jit(solution)/shard_map/ppermute | solution.py:389
  68.4 1.8 %collective-permute-done.10.key_got_ref = s16[16,2304]{1,0:T(8,128)(2,1)S(1)} collective-permute-done((s16[16,2304]{1,0:T(8,128)(2,1)S(1)}, s16[16,2304]{1,0:T(8,128)(2,1)S(1)}, u32[]{:S(2)}, u32[]{:S(2)}) %collective-permute-start.10) | collective-permute-done | bytes 73760 | tf_op jit(solution)/shard_map/ppermute | solution.py:389
  70.2 4.0 %keys_part.1 = (f32[32,8,128]{2,1,0:T(8,128)S(1)}, f32[32,8,128]{2,1,0:T(8,128)S(1)}, f32[32,8,128]{2,1,0:T(8,128)S(1)}, f32[3,32,8,128]{3,2,1,0:T(8,128)S(1)}, f32[4,32,8,128]{3,2,1,0:T(8,128)S(1)}) custom-call(f32[8,4096]{1,0:T(8,128)S(1)} %get-tuple-element.66.query_ref, s16[16,2176]{1,0:T(8,128)(2,1)S(1)} %collective-permute-done.9.query_got_ref, ...), custom_call_target="tpu_custom_call" | custom-call | flops 40000000 | bytes 9000000 | tf_op jit(solution)/shard_map/keys_part/pallas_call | solution.py:229
  74.3 1.8 %values_part.1 = bf16[16,16,128]{2,1,0:T(8,128)(2,1)} custom-call(s32[64]{0:T(128)S(1)} %select_reduce_fusion.slots_ref, s32[64]{0:T(128)S(1)} %get-tuple-element.87.halves_ref, s32[2]{0:T(128)S(1)} %fusion.4.lengths_ref, f32[8,4096]{1,0:T(8,128)S(1)} %get-tuple-element.72.value_ref, s16[16,2176]{1,0:T(8,128)(2,1)S(1)} %collective-permute-done.8.value_got_ref, ...), custom_call_target="tpu_custom_call" | custom-call | flops 4000000 | bytes 2000000 | tf_op jit(solution)/shard_map/values_part/pallas_call | solution.py:238
  76.1 3.5 %all-to-all-start = ((bf16[16,16,128]{2,1,0:T(8,128)(2,1)}), bf16[16,16,128]{2,1,0:T(8,128)(2,1)S(1)}, u32[]{:S(2)}, u32[]{:S(2)}) async-start(bf16[16,16,128]{2,1,0:T(8,128)(2,1)} %values_part.1), calls=%async_computation | async-start | bytes 131072 | tf_op jit(solution)/shard_map/all_to_all | solution.py:467
  79.8 6.7 %all-to-all-done = bf16[16,16,128]{2,1,0:T(8,128)(2,1)S(1)} async-done(((bf16[16,16,128]{2,1,0:T(8,128)(2,1)}), bf16[16,16,128]{2,1,0:T(8,128)(2,1)S(1)}, u32[]{:S(2)}, u32[]{:S(2)}) %all-to-all-start) | async-done | bytes 65568 | tf_op jit(solution)/shard_map/all_to_all | solution.py:467
  86.6 0.7 reshape.86
  (58 shorter events, 5.8 us)
Async XLA Ops:
  0.0 31.7 %collective-permute-start = (bf16[144,12288]{1,0:T(8,128)(2,1)}, bf16[144,12288]{1,0:T(8,128)(2,1)S(1)}, u32[]{:S(2)}, u32[]{:S(2)}) collective-permute-start(bf16[144,12288]{1,0:T(8,128)(2,1)} %own_hbm.5), channel_id=1, source_target_pairs={{0,1},{1,0},{2,3},{3,2},{4,5},{5,4},{6,7},{7,6},{8,9},{9,8},{10,11... | collective-permute-start | bytes 10616840 | tf_op jit(solution)/shard_map/ppermute | solution.py:389
  1.9 33.6 %collective-permute-start.1 = (bf16[144,64]{1,0:T(8,128)(2,1)}, bf16[144,64]{1,0:T(8,128)(2,1)}, u32[]{:S(2)}, u32[]{:S(2)}) collective-permute-start(bf16[144,64]{1,0:T(8,128)(2,1)} %copy.21.refs_0_), channel_id=1, source_target_pairs={{0,1},{1,0},{2,3},{3,2},{4,5},{5,4},{6,7},{7,6},{8,9},{9,8},{10,11... | collective-permute-start | bytes 55304 | tf_op jit(solution)/shard_map/ppermute | solution.py:389
  29.1 1.1 %copy-start.5 = (bf16[32,4,2304]{2,1,0:T(4,128)(2,1)S(1)}, bf16[32,4,2304]{2,1,0:T(4,128)(2,1)}, u32[]{:S(2)}) copy-start(bf16[32,4,2304]{2,1,0:T(4,128)(2,1)} %tokens_hbm.1) | copy-start | bytes 1769476
  30.2 0.7 copy-start.13
  31.7 2.0 %copy-start = (bf16[144,12288]{1,0:T(8,128)(2,1)S(1)}, bf16[144,12288]{1,0:T(8,128)(2,1)}, u32[]{:S(2)}) copy-start(bf16[144,12288]{1,0:T(8,128)(2,1)} %own_hbm.5) | copy-start | bytes 10616836
  33.7 1.9 %copy-start.12 = (bf16[144,64]{1,0:T(8,128)(2,1)S(1)}, bf16[144,64]{1,0:T(8,128)(2,1)}, u32[]{:S(2)}) copy-start(bf16[144,64]{1,0:T(8,128)(2,1)} %copy.21.refs_0_) | copy-start | bytes 55300
  35.5 2.8 %copy-start.10 = (f32[32,4096]{1,0:T(8,128)}, f32[32,4096]{1,0:T(8,128)S(1)}, u32[]{:S(2)}) copy-start(f32[32,4096]{1,0:T(8,128)S(1)} %get-tuple-element.44.kept_ref) | copy-start | bytes 1572868
  35.5 12.9 %collective-permute-start.4 = (s16[32,4224]{1,0:T(8,128)(2,1)}, s16[32,4224]{1,0:T(8,128)(2,1)}, u32[]{:S(2)}, u32[]{:S(2)}) collective-permute-start(s16[32,4224]{1,0:T(8,128)(2,1)} %get-tuple-element.45), channel_id=1, source_target_pairs={{0,2},{1,3},{2,0},{3,1},{4,6},{5,7},{6,4},{7,5},{8,10},{9,11},{10,... | collective-permute-start | bytes 811016 | tf_op jit(solution)/shard_map/ppermute | solution.py:389
  38.2 0.8 copy-start.6
  39.1 12.3 %collective-permute-start.3 = (s16[32,4480]{1,0:T(8,128)(2,1)}, s16[32,4480]{1,0:T(8,128)(2,1)}, u32[]{:S(2)}, u32[]{:S(2)}) collective-permute-start(s16[32,4480]{1,0:T(8,128)(2,1)} %get-tuple-element.48), channel_id=1, source_target_pairs={{0,2},{1,3},{2,0},{3,1},{4,6},{5,7},{6,4},{7,5},{8,10},{9,11},{10,... | collective-permute-start | bytes 860168 | tf_op jit(solution)/shard_map/ppermute | solution.py:389
  41.0 2.3 %copy-start.1 = (f32[2,32,128,128]{3,2,1,0:T(8,128)S(1)}, f32[2,32,128,128]{3,2,1,0:T(8,128)}, u32[]{:S(2)}) copy-start(f32[2,32,128,128]{3,2,1,0:T(8,128)} %state_ref) | copy-start | bytes 12582916
  42.8 3.4 %copy-start.8 = (f32[32,4096]{1,0:T(8,128)}, f32[32,4096]{1,0:T(8,128)S(1)}, u32[]{:S(2)}) copy-start(f32[32,4096]{1,0:T(8,128)S(1)} %get-tuple-element.50.kept_ref) | copy-start | bytes 1572868
  42.8 2.9 %copy-start.4 = (bf16[16,4,768]{2,1,0:T(4,128)(2,1)S(1)}, bf16[16,4,768]{2,1,0:T(4,128)(2,1)}, u32[]{:S(2)}) copy-start(bf16[16,4,768]{2,1,0:T(4,128)(2,1)} %all-gather.1) | copy-start | bytes 294916
  42.9 3.0 %copy-start.15 = (f32[2,3,12288]{2,0,1:T(2,128)S(1)}, f32[2,3,12288]{2,0,1:T(2,128)}, u32[]{:S(2)}) copy-start(f32[2,3,12288]{2,0,1:T(2,128)} %param.15) | copy-start | bytes 884740
  42.9 13.6 %collective-permute-start.2 = (s16[32,4224]{1,0:T(8,128)(2,1)}, s16[32,4224]{1,0:T(8,128)(2,1)S(1)}, u32[]{:S(2)}, u32[]{:S(2)}) collective-permute-start(s16[32,4224]{1,0:T(8,128)(2,1)} %get-tuple-element.51), channel_id=1, source_target_pairs={{0,2},{1,3},{2,0},{3,1},{4,6},{5,7},{6,4},{7,5},{8,10},{9,11},{10,... | collective-permute-start | bytes 811016 | tf_op jit(solution)/shard_map/ppermute | solution.py:389
  43.3 8.0 %copy-start.7 = (f32[32,4352]{1,0:T(8,128)S(1)}, f32[32,4352]{1,0:T(8,128)}, u32[]{:S(2)}) copy-start(f32[32,4352]{1,0:T(8,128)} %copy-done.6) | copy-start | bytes 1671172
  44.4 1.4 %copy-start.2 = (bf16[32,128,256]{2,1,0:T(8,128)(2,1)}, bf16[32,128,256]{2,1,0:T(8,128)(2,1)S(1)}, u32[]{:S(2)}) copy-start(bf16[32,128,256]{2,1,0:T(8,128)(2,1)S(1)} %get-tuple-element.54.low_ref) | copy-start | bytes 6291460
  45.7 12.4 %copy-start.14 = (s32[32]{0:T(128)S(1)}, s32[32]{0:T(128)}, u32[]{:S(2)}) copy-start(s32[32]{0:T(128)} %param.18) | copy-start | bytes 388
  45.7 12.4 %copy-start.16 = (s32[32]{0:T(128)S(1)}, s32[32]{0:T(128)}, u32[]{:S(2)}) copy-start(s32[32]{0:T(128)} %param.19) | copy-start | bytes 388
  48.3 21.9 %copy-start.3 = (bf16[32,128,256]{2,1,0:T(8,128)(2,1)S(1)}, bf16[32,128,256]{2,1,0:T(8,128)(2,1)}, u32[]{:S(2)}) copy-start(bf16[32,128,256]{2,1,0:T(8,128)(2,1)} %copy-done.2) | copy-start | bytes 6291460
  48.4 1.2 %copy-start.11 = (f32[32,4096]{1,0:T(8,128)S(1)}, f32[32,4096]{1,0:T(8,128)}, u32[]{:S(2)}) copy-start(f32[32,4096]{1,0:T(8,128)} %copy-done.10) | copy-start | bytes 1572868
  51.0 7.3 %collective-permute-start.7 = (s16[16,4224]{1,0:T(8,128)(2,1)S(1)}, s16[16,4224]{1,0:T(8,128)(2,1)S(1)}, u32[]{:S(2)}, u32[]{:S(2)}) collective-permute-start(s16[16,4224]{1,0:T(8,128)(2,1)S(1)} %get-tuple-element.59), channel_id=1, source_target_pairs={{0,4},{1,5},{2,6},{3,7},{4,0},{5,1},{6,2},{7,3},{8,12},{9,13},{10,... | collective-permute-start | bytes 405512 | tf_op jit(solution)/shard_map/ppermute | solution.py:389
  52.8 6.6 %collective-permute-start.6 = (s16[16,4480]{1,0:T(8,128)(2,1)S(1)}, s16[16,4480]{1,0:T(8,128)(2,1)S(1)}, u32[]{:S(2)}, u32[]{:S(2)}) collective-permute-start(s16[16,4480]{1,0:T(8,128)(2,1)S(1)} %get-tuple-element.62), channel_id=1, source_target_pairs={{0,4},{1,5},{2,6},{3,7},{4,0},{5,1},{6,2},{7,3},{8,12},{9,13},{10,... | collective-permute-start | bytes 430088 | tf_op jit(solution)/shard_map/ppermute | solution.py:389
  56.4 1.0 %copy-start.9 = (f32[32,4096]{1,0:T(8,128)S(1)}, f32[32,4096]{1,0:T(8,128)}, u32[]{:S(2)}) copy-start(f32[32,4096]{1,0:T(8,128)} %copy-done.8) | copy-start | bytes 1572868
  58.0 6.3 %collective-permute-start.5 = (s16[16,4224]{1,0:T(8,128)(2,1)S(1)}, s16[16,4224]{1,0:T(8,128)(2,1)S(1)}, u32[]{:S(2)}, u32[]{:S(2)}) collective-permute-start(s16[16,4224]{1,0:T(8,128)(2,1)S(1)} %get-tuple-element.65), channel_id=1, source_target_pairs={{0,4},{1,5},{2,6},{3,7},{4,0},{5,1},{6,2},{7,3},{8,12},{9,13},{10,... | collective-permute-start | bytes 405512 | tf_op jit(solution)/shard_map/ppermute | solution.py:389
  58.7 9.7 %collective-permute-start.9 = (s16[16,2176]{1,0:T(8,128)(2,1)S(1)}, s16[16,2176]{1,0:T(8,128)(2,1)S(1)}, u32[]{:S(2)}, u32[]{:S(2)}) collective-permute-start(s16[16,2176]{1,0:T(8,128)(2,1)S(1)} %get-tuple-element.67), channel_id=1, source_target_pairs={{0,8},{1,9},{2,10},{3,11},{4,12},{5,13},{6,14},{7,15},{8,0},{9,1},... | collective-permute-start | bytes 208904 | tf_op jit(solution)/shard_map/ppermute | solution.py:389
  59.9 10.4 %collective-permute-start.10 = (s16[16,2304]{1,0:T(8,128)(2,1)S(1)}, s16[16,2304]{1,0:T(8,128)(2,1)S(1)}, u32[]{:S(2)}, u32[]{:S(2)}) collective-permute-start(s16[16,2304]{1,0:T(8,128)(2,1)S(1)} %get-tuple-element.70), channel_id=1, source_target_pairs={{0,8},{1,9},{2,10},{3,11},{4,12},{5,13},{6,14},{7,15},{8,0},{9,1},... | collective-permute-start | bytes 221192 | tf_op jit(solution)/shard_map/ppermute | solution.py:389
  64.7 9.5 %collective-permute-start.8 = (s16[16,2176]{1,0:T(8,128)(2,1)S(1)}, s16[16,2176]{1,0:T(8,128)(2,1)S(1)}, u32[]{:S(2)}, u32[]{:S(2)}) collective-permute-start(s16[16,2176]{1,0:T(8,128)(2,1)S(1)} %get-tuple-element.73), channel_id=1, source_target_pairs={{0,8},{1,9},{2,10},{3,11},{4,12},{5,13},{6,14},{7,15},{8,0},{9,1},... | collective-permute-start | bytes 208904 | tf_op jit(solution)/shard_map/ppermute | solution.py:389
  76.1 10.4 %all-to-all-start = ((bf16[16,16,128]{2,1,0:T(8,128)(2,1)}), bf16[16,16,128]{2,1,0:T(8,128)(2,1)S(1)}, u32[]{:S(2)}, u32[]{:S(2)}) async-start(bf16[16,16,128]{2,1,0:T(8,128)(2,1)} %values_part.1), calls=%async_computation | async-start | bytes 131072 | tf_op jit(solution)/shard_map/all_to_all | solution.py:467
